TPU v7x, 512 devices: a whole 4x4x16 slice. The times are simulated.
512 devices in a mesh: inner: 16 (over x_hi, y, core), outer: 32 (over x_lo, z).
Axes of the slice: x: 4 (x_hi: 2, x_lo: 2; x = x_hi * 2 + x_lo), y: 4, z: 16, core: 2. Of those that a mesh axis runs over, the one named last changes fastest.
Arguments:
- queries: bfloat16 [65536, 4096], P(('inner', 'outer')), may hold values from -41 to 41
- key_states: bfloat16 [65536, 512], P(('inner', 'outer')), may hold values from -4 to 4
- value_states: bfloat16 [65536, 512], P(('inner', 'outer')), may hold values from -6 to 6
- out_grad: bfloat16 [65536, 4096], P(('inner', 'outer')), may hold values from -6 to 6
- segment_ids: int32 [65536], P(('inner', 'outer')), may hold values from 0 to 511, never falling along the last dimension, each value on 1 to 256 neighbouring positions
Outputs:
- query_grad: bfloat16 [65536, 4096], P(('inner', 'outer'))
- key_grad: bfloat16 [65536, 512], P(('inner', 'outer'))
- value_grad: bfloat16 [65536, 512], P(('inner', 'outer'))
Inputs may be any that keep to these rules, and one draw needn't show every extreme that they name: `segment_ids`: ids never fall along the tokens; every document has 1 to 256 tokens, and one has exactly that many.
All inputs are finite; a program needn't handle non-finite values.
Results may differ from a plain program's by a relative error of at most 0.025.
Values may be sent and summed in bfloat16 or wider, within the bound.
No kernel may reach another device: no remote copies, remote signals or barrier semaphores. Data moves between devices by JAX's collectives and lax.ppermute only.
A program may use at most 64 MiB of HBM per device.

v0:
```python
import jax
import jax.numpy as jnp
from jax import lax
from jax.sharding import PartitionSpec as P

HK = 4
HD = 128
REACH = 2


NEG = -1e30


def from_behind(value, axis, steps):
    count = lax.axis_size(axis)
    initial, last = (max(0, -steps), min(count, count - steps))
    return lax.ppermute(value, axis, [(source, source + steps) for source in range(initial, last)])


def block_mask(seg_query, seg_key, diagonal):
    allowed = seg_query[:, None] == seg_key[None, :]
    if diagonal:
        rows = lax.broadcasted_iota(jnp.int32, allowed.shape, 0)
        cols = lax.broadcasted_iota(jnp.int32, allowed.shape, 1)
        allowed = allowed & (cols <= rows)
    return allowed


def forward_block(state, q_heads, piece, seg_query, scale, diagonal):
    run_max, run_sum, run_acc = state
    pair, seg_key = piece
    scores = (
        jnp.einsum("tkgd,wkd->kgtw", q_heads, pair[0], preferred_element_type=jnp.float32) * scale
    )
    allowed = block_mask(seg_query, seg_key, diagonal)
    scores = jnp.where(allowed, scores, NEG)
    new_max = jnp.maximum(run_max, jnp.max(scores, -1))
    shrink = jnp.exp(run_max - new_max)
    probs = jnp.exp(jnp.where(allowed, scores - new_max[..., None], NEG))
    run_sum = run_sum * shrink + jnp.sum(probs, -1)
    update = jnp.einsum(
        "kgtw,wkd->tkgd", probs.astype(jnp.bfloat16), pair[1], preferred_element_type=jnp.float32
    )
    run_acc = run_acc * jnp.transpose(shrink, (2, 0, 1))[..., None] + update
    return (new_max, run_sum, run_acc)


def backward_block(q_heads, grad_heads, piece, seg_query, lse, delta, scale, diagonal):
    pair, seg_key = piece
    scores = (
        jnp.einsum("tkgd,wkd->kgtw", q_heads, pair[0], preferred_element_type=jnp.float32) * scale
    )
    allowed = block_mask(seg_query, seg_key, diagonal)
    probs = jnp.exp(jnp.where(allowed, scores - lse[..., None], NEG))
    probs_low = probs.astype(jnp.bfloat16)
    dprobs = jnp.einsum("tkgd,wkd->kgtw", grad_heads, pair[1], preferred_element_type=jnp.float32)
    dscores = (probs * (dprobs - delta[..., None])).astype(jnp.bfloat16)
    dq = jnp.einsum("kgtw,wkd->tkgd", dscores, pair[0], preferred_element_type=jnp.float32) * scale
    dk = jnp.einsum("kgtw,tkgd->wkd", dscores, q_heads, preferred_element_type=jnp.float32) * scale
    dv = jnp.einsum("kgtw,tkgd->wkd", probs_low, grad_heads, preferred_element_type=jnp.float32)
    return (dq, jnp.stack([dk, dv]))


def shards(queries, key_states, value_states, out_grad, segment_ids):
    tokens = queries.shape[0]
    group = queries.shape[1] // (HK * HD)
    scale = HD ** (-0.5)
    q_heads = queries.reshape(tokens, HK, group, HD)
    grad_heads = out_grad.reshape(tokens, HK, group, HD)
    pair = jnp.stack([key_states.reshape(tokens, HK, HD), value_states.reshape(tokens, HK, HD)])
    seg_wire = segment_ids + 1
    own = (pair, seg_wire)
    window = []
    moving = own
    for step in range(1, REACH + 1):
        moving = from_behind((moving[0], moving[1]), ("inner", "outer"), 1)
        window.append(moving)
    state = (
        jnp.full((HK, group, tokens), NEG, jnp.float32),
        jnp.zeros((HK, group, tokens), jnp.float32),
        jnp.zeros((tokens, HK, group, HD), jnp.float32),
    )
    state = forward_block(state, q_heads, own, seg_wire, scale, True)
    for piece in window:
        state = forward_block(state, q_heads, piece, seg_wire, scale, False)
    run_max, run_sum, run_acc = state
    lse = run_max + jnp.log(run_sum)
    attended = (run_acc / jnp.transpose(run_sum, (2, 0, 1))[..., None]).astype(jnp.bfloat16)
    delta = jnp.transpose(
        jnp.sum(grad_heads.astype(jnp.float32) * attended.astype(jnp.float32), -1), (1, 2, 0)
    )
    back_window = []
    for step in range(1, REACH + 1):
        back_window.append(from_behind((own[0], own[1]), ("inner", "outer"), step))
    query_total, own_part = backward_block(
        q_heads, grad_heads, own, seg_wire, lse, delta, scale, True
    )
    partials = [own_part]
    for piece in back_window:
        dq, part = backward_block(q_heads, grad_heads, piece, seg_wire, lse, delta, scale, False)
        query_total = query_total + dq
        partials.append(part)
    carried = partials[REACH]
    for step in range(REACH - 1, -1, -1):
        carried = (
            from_behind(carried.astype(jnp.bfloat16), ("inner", "outer"), -1).astype(carried.dtype)
            + partials[step]
        )
    query_grad = query_total.reshape(tokens, HK * group * HD).astype(jnp.bfloat16)
    key_grad = carried[0].reshape(tokens, HK * HD).astype(jnp.bfloat16)
    value_grad = carried[1].reshape(tokens, HK * HD).astype(jnp.bfloat16)
    return (query_grad, key_grad, value_grad)


def solution(mesh):
    placed = (
        P(("inner", "outer"), None),
        P(("inner", "outer"), None),
        P(("inner", "outer"), None),
        P(("inner", "outer"), None),
        P(("inner", "outer")),
    )
    return jax.shard_map(
        shards,
        mesh=mesh,
        in_specs=placed,
        out_specs=(
            P(("inner", "outer"), None),
            P(("inner", "outer"), None),
            P(("inner", "outer"), None),
        ),
        check_vma=False,
    )
```

profile of v0, /device:TPU:4, one launch (start us, length us, event | category | flops | bytes accessed | tf_op | source)
XLA Modules:
  0.0 83.3 jit_solution(4442760278356748609)
XLA Ops:
  0.6 0.7 broadcast_add_fusion
  1.4 3.8 %collective-permute-start = (s32[128]{0:T(128)S(1)}, s32[128]{0:T(128)S(1)}, u32[]{:S(2)}, u32[]{:S(2)}) collective-permute-start(s32[128]{0:T(128)S(1)} %broadcast_add_fusion), channel_id=1, source_target_pairs={{0,1},{1,2},{2,3},{3,4},{4,5},{5,6},{6,7},{7,8},{8,9},{9,10},{10,1... | collective-permute-start | bytes 1544 | tf_op jit(solution)/shard_map/ppermute | solution.py:17
  5.2 5.2 %collective-permute-start.5 = (s32[128]{0:T(128)S(1)}, s32[128]{0:T(128)S(1)}, u32[]{:S(2)}, u32[]{:S(2)}) collective-permute-start(s32[128]{0:T(128)S(1)} %broadcast_add_fusion), channel_id=1, source_target_pairs={{0,2},{1,3},{2,4},{3,5},{4,6},{5,7},{6,8},{7,9},{8,10},{9,11},{10,... | collective-permute-start | bytes 1544 | tf_op jit(solution)/shard_map/ppermute | solution.py:17
  10.4 1.0 %copy.42 = bf16[128,512]{0,1:T(8,128)(2,1)S(1)} copy(bf16[128,512]{1,0:T(8,128)(2,1)} %param.6) | data formatting | bytes 262144 | tf_op args[1]
  11.4 0.1 copy.44
  11.6 1.0 %copy.43 = bf16[128,512]{0,1:T(8,128)(2,1)S(1)} copy(bf16[128,512]{1,0:T(8,128)(2,1)} %param.7) | data formatting | bytes 262144 | tf_op args[2]
  12.6 0.1 copy.45
  12.7 0.7 pad_maximum_fusion
  13.5 5.0 %collective-permute-start.1 = (bf16[2,128,4,128]{3,1,2,0:T(8,128)(2,1)}, bf16[2,128,4,128]{3,1,2,0:T(8,128)(2,1)}, u32[]{:S(2)}, u32[]{:S(2)}) collective-permute-start(bf16[2,128,4,128]{3,1,2,0:T(8,128)(2,1)} %pad_maximum_fusion), channel_id=1, source_target_pairs={{0,1},{1,2},{2,3},{3,4},{4,5},{5,6},{6,7},{7,8},{8,9},{9,10},{10,1... | collective-permute-start | bytes 786440 | tf_op jit(solution)/shard_map/ppermute | solution.py:17
  18.5 5.2 %collective-permute-start.4 = (bf16[2,128,4,128]{3,1,2,0:T(8,128)(2,1)}, bf16[2,128,4,128]{3,1,2,0:T(8,128)(2,1)}, u32[]{:S(2)}, u32[]{:S(2)}) collective-permute-start(bf16[2,128,4,128]{3,1,2,0:T(8,128)(2,1)} %pad_maximum_fusion), channel_id=1, source_target_pairs={{0,2},{1,3},{2,4},{3,5},{4,6},{5,7},{6,8},{7,9},{8,10},{9,11},{10,... | collective-permute-start | bytes 786440 | tf_op jit(solution)/shard_map/ppermute | solution.py:17
  23.7 0.9 %squeeze_stack_reshape.4 = bf16[128,4,128]{2,1,0:T(4,128)(2,1)S(1)} reshape(bf16[128,512]{1,0:T(8,128)(2,1)} %param.6) | data formatting | bytes 262144 | tf_op jit(solution)/shard_map/squeeze;stack;reshape | solution.py:58
  24.6 3.8 %collective-permute-start.2 = (s32[128]{0:T(128)S(1)}, s32[128]{0:T(128)S(1)}, u32[]{:S(2)}, u32[]{:S(2)}) collective-permute-start(s32[128]{0:T(128)S(1)} %collective-permute-done), channel_id=1, source_target_pairs={{0,1},{1,2},{2,3},{3,4},{4,5},{5,6},{6,7},{7,8},{8,9},{9,10},{10,1... | collective-permute-start | bytes 1544 | tf_op jit(solution)/shard_map/ppermute | solution.py:17
  28.5 0.9 %squeeze_stack_reshape.10 = bf16[128,4,128]{2,1,0:T(4,128)(2,1)S(1)} reshape(bf16[128,512]{1,0:T(8,128)(2,1)} %param.7) | data formatting | bytes 262144 | tf_op jit(solution)/shard_map/squeeze;stack;reshape | solution.py:56
  29.4 0.7 copy.130
  30.1 0.1 copy.92
  30.2 0.1 copy.86
  30.4 1.6 %copy.48 = bf16[128,4096]{0,1:T(8,128)(2,1)S(1)} copy(bf16[128,4096]{1,0:T(8,128)(2,1)} %param.8) | data formatting | bytes 2097152 | tf_op args[3]
  32.0 7.8 %collective-permute-done.2 = s32[128]{0:T(128)S(1)} collective-permute-done((s32[128]{0:T(128)S(1)}, s32[128]{0:T(128)S(1)}, u32[]{:S(2)}, u32[]{:S(2)}) %collective-permute-start.2) | collective-permute-done | bytes 544 | tf_op jit(solution)/shard_map/ppermute | solution.py:17
  40.0 0.5 fusion.17
  40.5 1.9 %collective-permute-start.3 = (bf16[2,128,4,128]{3,1,2,0:T(8,128)(2,1)}, bf16[2,128,4,128]{3,1,2,0:T(8,128)(2,1)S(1)}, u32[]{:S(2)}, u32[]{:S(2)}) collective-permute-start(bf16[2,128,4,128]{3,1,2,0:T(8,128)(2,1)} %collective-permute-done.1), channel_id=1, source_target_pairs={{0,1},{1,2},{2,3},{3,4},{4,5},{5,6},{6,7},{7,8},{8,9},{9,10},{10,1... | collective-permute-start | bytes 786440 | tf_op jit(solution)/shard_map/ppermute | solution.py:17
  42.4 1.4 %fusion.18 = (f32[4,8,128]{2,1,0:T(8,128)S(1)}, f32[4,128,128,8]{2,1,3,0:T(8,128)S(1)}) fusion(pred[128,128]{0,1:T(8,128)(4,1)S(1)} %get-tuple-element.20, bf16[128,4,8,128]{0,3,2,1:T(8,128)(2,1)S(1)} %bitcast.313, bf16[2,128,4,128]{3,1,2,0:T(8,128)(2,1)} %collective-permute-done.1), kind=kOutput, calls=%fused_computation.36 | convolution fusion | flops 135786496 | bytes 3309568 | tf_op jit(solution)/shard_map/tkgd,wkd->kgtw/dot_general | solution.py:33
  43.8 1.3 %fusion.77 = f32[4,128,128,8]{2,1,3,0:T(8,128)S(1)} fusion(bf16[128,4,8,128]{0,3,2,1:T(8,128)(2,1)S(1)} %bitcast.314, bf16[2,128,4,128]{3,1,2,0:T(8,128)(2,1)} %collective-permute-done.4), kind=kOutput, calls=%fused_computation.103 | convolution fusion | flops 134217728 | bytes 3276800 | tf_op jit(solution)/shard_map/tkgd,wkd->kgtw/dot_general | solution.py:51
  45.1 7.8 %collective-permute-done.3 = bf16[2,128,4,128]{3,1,2,0:T(8,128)(2,1)S(1)} collective-permute-done((bf16[2,128,4,128]{3,1,2,0:T(8,128)(2,1)}, bf16[2,128,4,128]{3,1,2,0:T(8,128)(2,1)S(1)}, u32[]{:S(2)}, u32[]{:S(2)}) %collective-permute-start.3) | collective-permute-done | bytes 262176 | tf_op jit(solution)/shard_map/ppermute | solution.py:17
  52.9 0.4 fusion.19
  53.4 0.6 fusion.28
  54.0 1.3 %fusion.24 = (f32[4,8,128]{2,1,0:T(8,128)S(1)}, f32[4,8,128]{2,1,0:T(8,128)S(1)}) fusion(f32[4,128,128,8]{2,1,3,0:T(8,128)S(1)} %get-tuple-element.27, f32[4,8,128]{2,1,0:T(8,128)S(1)} %get-tuple-element.17, pred[128,128]{0,1:T(8,128)(4,1)S(1)} %get-tuple-element.21, f32[4,8,128]{2,1,0:T(8,128)S(1)} %get-tuple-element.12, ...), kind=kLoop, calls=%fused_computation.42 | loop fusion | flops 5234688 | bytes 4292608 | tf_op jit(solution)/shard_map/reduce_sum | solution.py:40
  55.3 0.8 fusion.41
  56.1 1.7 %fusion.39 = f32[4,128,8,128]{3,1,2,0:T(8,128)S(1)} fusion(f32[4,128,128,8]{2,1,3,0:T(8,128)S(1)} %get-tuple-element.25, f32[4,8,128]{2,1,0:T(8,128)S(1)} %get-tuple-element.12, pred[128,128]{0,1:T(8,128)(4,1)S(1)} %get-tuple-element.20, bf16[2,128,4,128]{3,1,2,0:T(8,128)(2,1)} %collective-permute-done.1), kind=kOutput, calls=%fused_computation.62 | convolution fusion | flops 136839168 | bytes 4358144 | tf_op jit(solution)/shard_map/kgtw,wkd->tkgd/dot_general | solution.py:41
  57.8 1.3 %multiply_reduce_fusion = f32[128,4,8]{0,2,1:T(8,128)S(1)} fusion(bf16[128,4,8,128]{0,3,2,1:T(8,128)(2,1)S(1)} %bitcast.320, f32[128,4,8]{0,2,1:T(8,128)S(1)} %get-tuple-element.9, f32[4,128,128,8]{2,1,3,0:T(8,128)S(1)} %get-tuple-element.23, f32[4,8,128]{2,1,0:T(8,128)S(1)} %get-tuple-element.11, pred[128,128]{0,1:T(8,128)(4,1)S(1)} %get-tuple-element.19, ...), kind=kOutput, calls=%fused_computation.31 | convolution fusion | flops 142602240 | bytes 7585792 | tf_op jit(solution)/shard_map/kgtw,wkd->tkgd/dot_general | solution.py:41
  59.2 0.8 fusion.12
  59.9 0.6 fusion.37
  60.5 1.6 %fusion.2 = bf16[4,8,128,128]{2,3,1,0:T(8,128)(2,1)S(1)} fusion(bf16[128,4,8,128]{0,3,2,1:T(8,128)(2,1)S(1)} %bitcast.323, f32[4,128,128,8]{2,1,3,0:T(8,128)S(1)} %fusion.77, f32[4,8,128]{2,1,0:T(8,128)S(1)} %bitcast.334, f32[4,8,128]{2,1,0:T(8,128)S(1)} %log_add_fusion, pred[128,128]{0,1:T(8,128)(4,1)S(1)} %get-tuple-element.18, ...), kind=kOutput, calls=%fused_computation.4 | convolution fusion | flops 137363456 | bytes 4374528 | tf_op jit(solution)/shard_map/tkgd,wkd->kgtw/dot_general | solution.py:56
  62.2 0.4 fusion.36
  62.6 2.1 %collective-permute-start.6 = (bf16[2,128,4,128]{3,1,2,0:T(8,128)(2,1)S(1)}, bf16[2,128,4,128]{3,1,2,0:T(8,128)(2,1)S(1)}, u32[]{:S(2)}, u32[]{:S(2)}) collective-permute-start(bf16[2,128,4,128]{3,1,2,0:T(8,128)(2,1)S(1)} %pad_maximum_fusion.1), channel_id=1, source_target_pairs={{1,0},{2,1},{3,2},{4,3},{5,4},{6,5},{7,6},{8,7},{9,8},{10,9},{11,1... | collective-permute-start | bytes 786440 | tf_op jit(solution)/shard_map/ppermute | solution.py:17
  64.8 0.4 fusion.102
  65.2 1.6 %fusion.6 = bf16[4,8,128,128]{2,3,1,0:T(8,128)(2,1)S(1)} fusion(bf16[128,4,8,128]{0,3,2,1:T(8,128)(2,1)S(1)} %bitcast.324, f32[4,128,128,8]{2,1,3,0:T(8,128)S(1)} %get-tuple-element.25, f32[4,8,128]{2,1,0:T(8,128)S(1)} %bitcast.335, f32[4,8,128]{2,1,0:T(8,128)S(1)} %log_add_fusion, pred[128,128]{0,1:T(8,128)(4,1)S(1)} %get-tuple-element.20, ...), kind=kOutput, calls=%fused_computation.11 | convolution fusion | flops 137363456 | bytes 4374528 | tf_op jit(solution)/shard_map/tkgd,wkd->kgtw/dot_general | solution.py:56
  66.8 1.4 %fusion.75 = f32[4,128,8,128]{3,1,2,0:T(8,128)S(1)} fusion(bf16[4,8,128,128]{2,3,1,0:T(8,128)(2,1)S(1)} %fusion.6, bf16[2,128,4,128]{3,1,2,0:T(8,128)(2,1)} %collective-permute-done.1), kind=kOutput, calls=%fused_computation.101 | convolution fusion | flops 134217728 | bytes 3276800 | tf_op jit(solution)/shard_map/kgtw,wkd->tkgd/dot_general | solution.py:58
  68.2 1.8 %fusion = bf16[128,4,8,128]{0,3,2,1:T(8,128)(2,1)S(1)} fusion(f32[4,128,8,128]{3,1,2,0:T(8,128)S(1)} %fusion.75, f32[4,8,128,128]{2,3,1,0:T(8,128)S(1)} %fusion.102, bf16[4,8,128,128]{2,3,1,0:T(8,128)(2,1)S(1)} %fusion.2, bf16[2,128,4,128]{3,1,2,0:T(8,128)(2,1)} %collective-permute-done.4), kind=kOutput, calls=%fused_computation.1 | convolution fusion | flops 137363456 | bytes 6422528 | tf_op jit(solution)/shard_map/kgtw,wkd->tkgd/dot_general | solution.py:58
  70.0 0.6 convolution_bitcast_fusion.2
  70.6 0.4 fusion.32
  71.1 5.4 %collective-permute-start.7 = (bf16[2,128,4,128]{3,1,2,0:T(8,128)(2,1)S(1)}, bf16[2,128,4,128]{3,1,2,0:T(8,128)(2,1)}, u32[]{:S(2)}, u32[]{:S(2)}) collective-permute-start(bf16[2,128,4,128]{3,1,2,0:T(8,128)(2,1)S(1)} %fusion.72), channel_id=1, source_target_pairs={{1,0},{2,1},{3,2},{4,3},{5,4},{6,5},{7,6},{8,7},{9,8},{10,9},{11,1... | collective-permute-start | bytes 786440 | tf_op jit(solution)/shard_map/ppermute | solution.py:17
  76.6 1.3 %convolution_bitcast_fusion = f32[1,128,4,128]{3,1,2,0:T(8,128)} fusion(bf16[128,4,8,128]{0,3,2,1:T(8,128)(2,1)S(1)} %bitcast.326, f32[4,128,128,8]{2,1,3,0:T(8,128)S(1)} %get-tuple-element.27, f32[4,8,128]{2,1,0:T(8,128)S(1)} %log_add_fusion, pred[128,128]{0,1:T(8,128)(4,1)S(1)} %get-tuple-element.21), kind=kOutput, calls=%fused_computation.47 | convolution fusion | flops 136314880 | bytes 3440640 | tf_op jit(solution)/shard_map/kgtw,tkgd->wkd/dot_general | solution.py:60
  77.8 1.3 %copy.77 = bf16[128,4096]{1,0:T(8,128)(2,1)} copy(bf16[128,4096]{0,1:T(8,128)(2,1)S(1)} %bitcast.319) | data formatting | bytes 2097152
  79.1 0.4 fusion.30
  79.6 0.9 %collective-permute-done.7 = bf16[2,128,4,128]{3,1,2,0:T(8,128)(2,1)} collective-permute-done((bf16[2,128,4,128]{3,1,2,0:T(8,128)(2,1)S(1)}, bf16[2,128,4,128]{3,1,2,0:T(8,128)(2,1)}, u32[]{:S(2)}, u32[]{:S(2)}) %collective-permute-start.7) | collective-permute-done | bytes 262176 | tf_op jit(solution)/shard_map/ppermute | solution.py:17
  80.4 1.0 %fusion.73 = bf16[2,128,4,128]{3,1,2,0:T(8,128)(2,1)S(1)} fusion(f32[1,128,4,128]{3,1,2,0:T(8,128)S(1)} %copy-done.3, f32[1,128,4,128]{3,1,2,0:T(8,128)S(1)} %fusion.30, bf16[2,128,4,128]{3,1,2,0:T(8,128)(2,1)} %collective-permute-done.7), kind=kLoop, calls=%fused_computation.91 | loop fusion | flops 524288 | bytes 1048576 | tf_op jit(solution)/shard_map/convert.1
  81.6 0.8 copy.78
  82.5 0.8 copy.79
  (22 shorter events, 0.6 us)
Async XLA Ops:
  0.6 28.8 %copy-start.2 = (bf16[128,4096]{1,0:T(8,128)(2,1)S(1)}, bf16[128,4096]{1,0:T(8,128)(2,1)}, u32[]{:S(2)}) copy-start(bf16[128,4096]{1,0:T(8,128)(2,1)} %param.5) | copy-start | bytes 3145732
  1.4 23.2 %collective-permute-start = (s32[128]{0:T(128)S(1)}, s32[128]{0:T(128)S(1)}, u32[]{:S(2)}, u32[]{:S(2)}) collective-permute-start(s32[128]{0:T(128)S(1)} %broadcast_add_fusion), channel_id=1, source_target_pairs={{0,1},{1,2},{2,3},{3,4},{4,5},{5,6},{6,7},{7,8},{8,9},{9,10},{10,1... | collective-permute-start | bytes 1544 | tf_op jit(solution)/shard_map/ppermute | solution.py:17
  5.2 26.8 %collective-permute-start.5 = (s32[128]{0:T(128)S(1)}, s32[128]{0:T(128)S(1)}, u32[]{:S(2)}, u32[]{:S(2)}) collective-permute-start(s32[128]{0:T(128)S(1)} %broadcast_add_fusion), channel_id=1, source_target_pairs={{0,2},{1,3},{2,4},{3,5},{4,6},{5,7},{6,8},{7,9},{8,10},{9,11},{10,... | collective-permute-start | bytes 1544 | tf_op jit(solution)/shard_map/ppermute | solution.py:17
  13.5 27.0 %collective-permute-start.1 = (bf16[2,128,4,128]{3,1,2,0:T(8,128)(2,1)}, bf16[2,128,4,128]{3,1,2,0:T(8,128)(2,1)}, u32[]{:S(2)}, u32[]{:S(2)}) collective-permute-start(bf16[2,128,4,128]{3,1,2,0:T(8,128)(2,1)} %pad_maximum_fusion), channel_id=1, source_target_pairs={{0,1},{1,2},{2,3},{3,4},{4,5},{5,6},{6,7},{7,8},{8,9},{9,10},{10,1... | collective-permute-start | bytes 786440 | tf_op jit(solution)/shard_map/ppermute | solution.py:17
  18.5 25.3 %collective-permute-start.4 = (bf16[2,128,4,128]{3,1,2,0:T(8,128)(2,1)}, bf16[2,128,4,128]{3,1,2,0:T(8,128)(2,1)}, u32[]{:S(2)}, u32[]{:S(2)}) collective-permute-start(bf16[2,128,4,128]{3,1,2,0:T(8,128)(2,1)} %pad_maximum_fusion), channel_id=1, source_target_pairs={{0,2},{1,3},{2,4},{3,5},{4,6},{5,7},{6,8},{7,9},{8,10},{9,11},{10,... | collective-permute-start | bytes 786440 | tf_op jit(solution)/shard_map/ppermute | solution.py:17
  24.6 15.2 %collective-permute-start.2 = (s32[128]{0:T(128)S(1)}, s32[128]{0:T(128)S(1)}, u32[]{:S(2)}, u32[]{:S(2)}) collective-permute-start(s32[128]{0:T(128)S(1)} %collective-permute-done), channel_id=1, source_target_pairs={{0,1},{1,2},{2,3},{3,4},{4,5},{5,6},{6,7},{7,8},{8,9},{9,10},{10,1... | collective-permute-start | bytes 1544 | tf_op jit(solution)/shard_map/ppermute | solution.py:17
  32.0 33.2 %copy-start = (bf16[128,4096]{0,1:T(8,128)(2,1)}, bf16[128,4096]{0,1:T(8,128)(2,1)S(1)}, u32[]{:S(2)}) copy-start(bf16[128,4096]{0,1:T(8,128)(2,1)S(1)} %copy.48) | copy-start | bytes 3145732
  40.5 12.4 %collective-permute-start.3 = (bf16[2,128,4,128]{3,1,2,0:T(8,128)(2,1)}, bf16[2,128,4,128]{3,1,2,0:T(8,128)(2,1)S(1)}, u32[]{:S(2)}, u32[]{:S(2)}) collective-permute-start(bf16[2,128,4,128]{3,1,2,0:T(8,128)(2,1)} %collective-permute-done.1), channel_id=1, source_target_pairs={{0,1},{1,2},{2,3},{3,4},{4,5},{5,6},{6,7},{7,8},{8,9},{9,10},{10,1... | collective-permute-start | bytes 786440 | tf_op jit(solution)/shard_map/ppermute | solution.py:17
  62.6 8.4 %collective-permute-start.6 = (bf16[2,128,4,128]{3,1,2,0:T(8,128)(2,1)S(1)}, bf16[2,128,4,128]{3,1,2,0:T(8,128)(2,1)S(1)}, u32[]{:S(2)}, u32[]{:S(2)}) collective-permute-start(bf16[2,128,4,128]{3,1,2,0:T(8,128)(2,1)S(1)} %pad_maximum_fusion.1), channel_id=1, source_target_pairs={{1,0},{2,1},{3,2},{4,3},{5,4},{6,5},{7,6},{8,7},{9,8},{10,9},{11,1... | collective-permute-start | bytes 786440 | tf_op jit(solution)/shard_map/ppermute | solution.py:17
  68.2 1.8 %copy-start.1 = (bf16[128,4096]{0,1:T(8,128)(2,1)S(1)}, bf16[128,4096]{0,1:T(8,128)(2,1)}, u32[]{:S(2)}) copy-start(bf16[128,4096]{0,1:T(8,128)(2,1)} %copy-done) | copy-start | bytes 3145732
  71.1 9.3 %collective-permute-start.7 = (bf16[2,128,4,128]{3,1,2,0:T(8,128)(2,1)S(1)}, bf16[2,128,4,128]{3,1,2,0:T(8,128)(2,1)}, u32[]{:S(2)}, u32[]{:S(2)}) collective-permute-start(bf16[2,128,4,128]{3,1,2,0:T(8,128)(2,1)S(1)} %fusion.72), channel_id=1, source_target_pairs={{1,0},{2,1},{3,2},{4,3},{5,4},{6,5},{7,6},{8,7},{9,8},{10,9},{11,1... | collective-permute-start | bytes 786440 | tf_op jit(solution)/shard_map/ppermute | solution.py:17
  79.1 1.3 %copy-start.3 = (f32[1,128,4,128]{3,1,2,0:T(8,128)S(1)}, f32[1,128,4,128]{3,1,2,0:T(8,128)}, u32[]{:S(2)}) copy-start(f32[1,128,4,128]{3,1,2,0:T(8,128)} %convolution_bitcast_fusion) | copy-start | bytes 786436
where the time goes:
time: 83.9 us; the launch traced here: 83.3 us
  starting transfers between devices  32.5 us (39%)
  matrix products  18.7 us (22%)
  waiting for transfers between devices  16.5 us (20%)
  local copies, waits for them, and re-layouts  9.91 us (12%)
  other arithmetic  4.66 us (6%)
  between operations  1.04 us (1%)
    ppermute x8, starting transfers between devices, from_behind(): lax.ppermute(value, axis, [(source, source + steps) for source in range(i...  32.5 us
    ppermute x8, waiting for transfers between devices, from_behind(): lax.ppermute(value, axis, [(source, source + steps) for source in range(i...  16.5 us
    unnamed x14, local copies, waits for them, and re-layouts  6.54 us
    dot_general x3, matrix products, backward_block(): jnp.einsum('tkgd,wkd->kgtw', grad_heads, pair[1], preferred_element_type=...  4.03 us
    dot_general x3, matrix products, forward_block(): jnp.einsum('kgtw,wkd->tkgd', probs.astype(jnp.bfloat16), pair[1], preferr...  3.8 us
    dot_general x3, matrix products, backward_block(): jnp.einsum('kgtw,wkd->tkgd', dscores, pair[0], preferred_element_type=jnp...  3.58 us
    dot_general x3, matrix products, backward_block(): jnp.einsum('kgtw,tkgd->wkd', probs_low, grad_heads, preferred_element_typ...  2.39 us
    reduce_sum x2, other arithmetic, forward_block(): run_sum = run_sum * shrink + jnp.sum(probs, -1)  1.9 us
  transfers between devices with their start and end apart: 8, of which 3 were waited for; matrix products, arithmetic and copies ran while one was open for 24% of the time, Pallas kernels for 0%

commit v1 on v0

v1 whole, which is shorter than its diff:
```python
import functools

import jax
import jax.numpy as jnp
from jax import lax
from jax.experimental import pallas as pl
from jax.experimental.pallas import tpu as pltpu
from jax.sharding import PartitionSpec as P

HK = 4
HD = 128
SEG_ROWS = 16
NEG = -1e30
LOG2E = 1.4426950408889634
AXES = ("inner", "outer")
CHUNKS = 2
VMEM_LIMIT = 24 * 1024 * 1024


def shift(value, steps):
    count = lax.axis_size(AXES)
    first, last = max(0, -steps), min(count, count - steps)
    return lax.ppermute(value, AXES, [(i, i + steps) for i in range(first, last)])


def dot(a, b):
    return jnp.dot(a, b, preferred_element_type=jnp.float32)


def stacked(ref, first, count):
    return jnp.concatenate(
        [ref[:, (first + h) * HD : (first + h + 1) * HD] for h in range(count)], axis=0
    )


def sees_own(tokens, copies):
    key = lax.broadcasted_iota(jnp.int32, (tokens, tokens), 0)
    query = lax.broadcasted_iota(jnp.int32, (tokens, tokens), 1)
    return jnp.concatenate([key <= query] * copies, axis=1)


def segments(ref, tokens):
    coded = ref[2 * tokens : 2 * tokens + SEG_ROWS, :].astype(jnp.float32)
    row = coded[0:1] * 2.0 + coded[1:2]
    return jnp.broadcast_to(row, (tokens, tokens))


def pack_kernel(tokens, k_ref, v_ref, seg_ref, *refs):
    out_refs, seg_own, sems = refs[:-2], refs[-2], refs[-1]
    width = k_ref.shape[1] // len(out_refs)
    ids = pltpu.make_async_copy(seg_ref, seg_own, sems.at[0])
    ids.start()
    copies = []
    for index, out_ref in enumerate(out_refs):
        cols = pl.ds(index * width, width)
        for half, source in enumerate((k_ref, v_ref)):
            copies.append(
                pltpu.make_async_copy(
                    source.at[:, cols], out_ref.at[pl.ds(half * tokens, tokens), :],
                    sems.at[1 + 2 * index + half],
                )
            )
    for copy in copies:
        copy.start()
    ids.wait()
    seg = jnp.broadcast_to((seg_own[...] + 1)[None, :], (SEG_ROWS, tokens))
    row = lax.broadcasted_iota(jnp.int32, (SEG_ROWS, tokens), 0)
    coded = jnp.where(row == 0, seg >> 1, jnp.where(row == 1, seg & 1, 0))
    coded = coded.astype(jnp.float32).astype(jnp.bfloat16)
    for out_ref in out_refs:
        out_ref[2 * tokens : 2 * tokens + SEG_ROWS, :] = jnp.concatenate([coded] * (width // tokens), axis=1)
    for copy in copies:
        copy.wait()


def turn_kernel(q_ref, g_ref, qt_ref, gt_ref):
    for h in range(q_ref.shape[1] // HD):
        cols = slice(h * HD, (h + 1) * HD)
        qt_ref[:, cols] = jnp.transpose(q_ref[:, cols])
        gt_ref[:, cols] = jnp.transpose(g_ref[:, cols])


def score_kernel(group, tokens, scale, q_ref, g_ref, qt_ref, gt_ref, own_ref, one_ref, two_ref,
                 p_ref, ds_ref, far_ref, near_ref, bias_ref):
    @pl.when(pl.program_id(0) == 0)
    def _():
        seg_query = segments(own_ref, tokens)
        seg_own = jnp.transpose(seg_query)
        seg_one = jnp.transpose(segments(one_ref, tokens))
        seg_two = jnp.transpose(segments(two_ref, tokens))
        mixed = jnp.where(sees_own(tokens, 1), seg_own, seg_two)
        bias_ref[0:tokens, :] = jnp.where(mixed == seg_query, 0.0, NEG)
        bias_ref[tokens : 2 * tokens, :] = jnp.where(seg_one == seg_query, 0.0, NEG)

    tri = sees_own(tokens, 2)
    own_mask = jnp.where(tri, 1.0, 0.0).astype(jnp.bfloat16)
    far_mask = jnp.where(tri, 0.0, 1.0).astype(jnp.bfloat16)
    bias_mix = jnp.concatenate([bias_ref[0:tokens, :]] * 2, axis=1)
    bias_one = jnp.concatenate([bias_ref[tokens : 2 * tokens, :]] * 2, axis=1)
    keys = jnp.concatenate([own_ref[0:tokens, :], one_ref[0:tokens, :], two_ref[0:tokens, :]], axis=0)
    vals = jnp.concatenate(
        [own_ref[tokens : 2 * tokens, :], one_ref[tokens : 2 * tokens, :], two_ref[tokens : 2 * tokens, :]],
        axis=0,
    )
    factor = scale * LOG2E
    sum_k = jnp.zeros((2 * tokens, HD), jnp.float32)
    sum_v = jnp.zeros((2 * tokens, HD), jnp.float32)
    pairs = group // 2
    spans = [slice(pair * 2 * HD, (pair + 1) * 2 * HD) for pair in range(pairs)]
    products = [(dot(keys, qt_ref[:, spans[0]]), dot(vals, gt_ref[:, spans[0]]))]
    for pair, cols in enumerate(spans):
        if pair + 1 < pairs:
            products.append((dot(keys, qt_ref[:, spans[pair + 1]]), dot(vals, gt_ref[:, spans[pair + 1]])))
        raw, dp = products[pair]
        s_mix = jnp.where(tri, raw[0:tokens], raw[2 * tokens :]) + bias_mix
        s_one = raw[tokens : 2 * tokens] + bias_one
        top = jnp.max(jnp.maximum(s_mix, s_one), axis=0, keepdims=True)
        e_mix = jnp.exp2((s_mix - top) * factor)
        e_one = jnp.exp2((s_one - top) * factor)
        inverse = 1.0 / jnp.sum(e_mix + e_one, axis=0, keepdims=True)
        p_mix = e_mix * inverse
        p_one = e_one * inverse
        d_mix = jnp.where(tri, dp[0:tokens], dp[2 * tokens :])
        d_one = dp[tokens : 2 * tokens]
        delta = jnp.sum(p_mix * d_mix + p_one * d_one, axis=0, keepdims=True)
        ds_mix = (p_mix * (d_mix - delta)).astype(jnp.bfloat16)
        ds_one = (p_one * (d_one - delta)).astype(jnp.bfloat16)
        p_mix = p_mix.astype(jnp.bfloat16)
        p_one = p_one.astype(jnp.bfloat16)
        p_ref[:, cols] = p_mix * own_mask
        ds_ref[0:tokens, cols] = ds_mix
        ds_ref[tokens : 2 * tokens, cols] = ds_one
        sum_k = sum_k + dot(jnp.concatenate([ds_one, ds_mix * far_mask], axis=0), stacked(q_ref, 2 * pair, 2))
        sum_v = sum_v + dot(jnp.concatenate([p_one, p_mix * far_mask], axis=0), stacked(g_ref, 2 * pair, 2))
    near_ref[0:tokens, :] = sum_k[0:tokens] * scale
    near_ref[tokens : 2 * tokens, :] = sum_v[0:tokens]
    far_ref[0:tokens, :] = (sum_k[tokens:] * scale).astype(far_ref.dtype)
    far_ref[tokens : 2 * tokens, :] = sum_v[tokens:].astype(far_ref.dtype)


def rest_kernel(group, tokens, scale, p_ref, ds_ref, q_ref, g_ref, own_ref, one_ref, two_ref, *refs):
    dq_ref, own_out = refs[-2:]
    far_ref = refs[0] if len(refs) > 2 else None
    tri = sees_own(tokens, 2)
    own_mask = jnp.where(tri, 1.0, 0.0).astype(jnp.bfloat16)
    far_mask = jnp.where(tri, 0.0, 1.0).astype(jnp.bfloat16)

    def flipped(ref):
        return jnp.transpose(ref[0:tokens, :].astype(jnp.float32)).astype(jnp.bfloat16)

    keys_t = jnp.concatenate([flipped(own_ref), flipped(one_ref), flipped(two_ref)], axis=1)
    sum_k = jnp.zeros((tokens, HD), jnp.float32)
    sum_v = jnp.zeros((tokens, HD), jnp.float32)
    for pair in range(group // 2):
        cols = slice(pair * 2 * HD, (pair + 1) * 2 * HD)
        ds_mix = ds_ref[0:tokens, cols]
        ds_own = ds_mix * own_mask
        sum_k = sum_k + dot(ds_own, stacked(q_ref, 2 * pair, 2))
        sum_v = sum_v + dot(p_ref[:, cols], stacked(g_ref, 2 * pair, 2))
        rows = jnp.concatenate([ds_own, ds_ref[tokens : 2 * tokens, cols], ds_mix * far_mask], axis=0)
        dq_t = dot(keys_t, rows) * scale
        for h in range(2):
            head = dq_t[:, h * HD : (h + 1) * HD]
            dq_ref[:, (2 * pair + h) * HD : (2 * pair + h + 1) * HD] = jnp.transpose(head).astype(dq_ref.dtype)
    sum_k = sum_k * scale
    if far_ref is not None:
        sum_k = sum_k + far_ref[0:tokens, :].astype(jnp.float32)
        sum_v = sum_v + far_ref[tokens : 2 * tokens, :].astype(jnp.float32)
    own_out[0:tokens, :] = sum_k
    own_out[tokens : 2 * tokens, :] = sum_v


def join_kernel(first_ref, handed_ref, second_ref, out_ref):
    width = first_ref.shape[1]
    out_ref[:, 0:width] = (first_ref[...] + handed_ref[...].astype(jnp.float32)).astype(out_ref.dtype)
    out_ref[:, width:] = second_ref[...].astype(out_ref.dtype)


def final_kernel(tokens, near_ref, *refs):
    k_out, v_out = refs[-2:]
    for index, own_ref in enumerate(refs[:-2]):
        width = own_ref.shape[1]
        cols = slice(index * width, (index + 1) * width)
        total = own_ref[...] + near_ref[:, cols].astype(jnp.float32)
        k_out[:, cols] = total[0:tokens].astype(k_out.dtype)
        v_out[:, cols] = total[tokens:].astype(v_out.dtype)


def column(rows, width, offset=0):
    return pl.BlockSpec((rows, width), lambda i: (0, i + offset))


def bf16(*shape):
    return jax.ShapeDtypeStruct(shape, jnp.bfloat16)


def f32(*shape):
    return jax.ShapeDtypeStruct(shape, jnp.float32)


def cost(flops, bytes_accessed, transcendentals=0):
    return pl.CostEstimate(flops=flops, bytes_accessed=bytes_accessed, transcendentals=transcendentals)


PARAMS = pltpu.CompilerParams(vmem_limit_bytes=VMEM_LIMIT)


def pack_call(key_states, value_states, segment_ids):
    tokens, width = key_states.shape
    operands = [pltpu.with_memory_space_constraint(x, pltpu.HBM) for x in (key_states, value_states, segment_ids)]
    return pl.pallas_call(
        functools.partial(pack_kernel, tokens),
        in_specs=[pl.BlockSpec(memory_space=pltpu.HBM)] * 3,
        out_shape=[bf16(2 * tokens + SEG_ROWS, width // CHUNKS) for _ in range(CHUNKS)],
        scratch_shapes=[
            pltpu.VMEM((tokens,), jnp.int32),
            pltpu.SemaphoreType.DMA((1 + 2 * CHUNKS,)),
        ],
        cost_estimate=cost(0, 8 * tokens * width),
        compiler_params=PARAMS,
        name="pack",
    )(*operands)


def turn_call(q, g):
    tokens, span = q.shape
    wide = span // HK
    return pl.pallas_call(
        turn_kernel,
        grid=(HK,),
        in_specs=[column(tokens, wide)] * 2,
        out_specs=[column(HD, wide)] * 2,
        out_shape=[bf16(HD, span)] * 2,
        cost_estimate=cost(0, 16 * tokens * span),
        compiler_params=PARAMS,
        name="turn",
    )(q, g)


def score_call(q, g, qt, gt, own, one, two, offset, group, tokens, scale):
    count = own.shape[1] // HD
    wide = group * HD
    span = count * wide
    payload = column(2 * tokens + SEG_ROWS, HD)
    return pl.pallas_call(
        functools.partial(score_kernel, group, tokens, scale),
        grid=(count,),
        in_specs=[column(tokens, wide, offset)] * 2 + [column(HD, wide, offset)] * 2 + [payload] * 3,
        out_specs=[column(tokens, wide), column(2 * tokens, wide), column(2 * tokens, HD), column(2 * tokens, HD)],
        out_shape=[
            bf16(tokens, span),
            bf16(2 * tokens, span),
            bf16(2 * tokens, count * HD),
            f32(2 * tokens, count * HD),
        ],
        scratch_shapes=[pltpu.VMEM((2 * tokens, tokens), jnp.float32)],
        cost_estimate=cost(2 * tokens * 3 * span * tokens * 4, 12 * tokens * span, 2 * tokens * span),
        compiler_params=PARAMS,
        name="scores",
    )(q, g, qt, gt, own, one, two)


def rest_call(p, ds, q, g, own, one, two, far, before, offset, group, tokens, scale):
    count = own.shape[1] // HD
    wide = group * HD
    payload = column(2 * tokens + SEG_ROWS, HD)
    operands = [p, ds, q, g, own, one, two]
    specs = [column(tokens, wide), column(2 * tokens, wide)] + [column(tokens, wide, offset)] * 2 + [payload] * 3
    aliases = {}
    if far is not None:
        operands.append(far)
        specs.append(column(2 * tokens, HD))
    if before is not None:
        aliases = {len(operands): 0}
        operands.append(before)
        specs.append(pl.BlockSpec(memory_space=pl.ANY))
    return pl.pallas_call(
        functools.partial(rest_kernel, group, tokens, scale),
        grid=(count,),
        in_specs=specs,
        out_specs=[column(tokens, wide, offset), column(2 * tokens, HD)],
        out_shape=[bf16(tokens, q.shape[1]), f32(2 * tokens, count * HD)],
        input_output_aliases=aliases,
        cost_estimate=cost(2 * tokens * 3 * count * wide * tokens * 2, 12 * tokens * count * wide),
        compiler_params=PARAMS,
        name="rest",
    )(*operands)


def join_call(first, handed, second):
    rows, width = first.shape
    return pl.pallas_call(
        join_kernel,
        out_shape=bf16(rows, 2 * width),
        cost_estimate=cost(0, 12 * rows * width),
        compiler_params=PARAMS,
        name="join",
    )(first, handed, second)


def final_call(near, owns):
    tokens, width = near.shape[0] // 2, near.shape[1]
    return pl.pallas_call(
        functools.partial(final_kernel, tokens),
        out_shape=[bf16(tokens, width)] * 2,
        cost_estimate=cost(0, 16 * tokens * width),
        compiler_params=PARAMS,
        name="final",
    )(near, *owns)


def shards(queries, key_states, value_states, out_grad, segment_ids):
    tokens = queries.shape[0]
    group = queries.shape[1] // (HK * HD)
    scale = HD ** (-0.5)
    chunks = range(CHUNKS)
    step = HK // CHUNKS
    own = pack_call(key_states, value_states, segment_ids)
    one = [shift(x, 1) for x in own]
    two = [shift(own[0], 2), shift(one[1], 1)]
    qt, gt = turn_call(queries, out_grad)
    first = [
        score_call(queries, out_grad, qt, gt, own[c], one[c], two[c], c * step, group, tokens, scale)
        for c in chunks
    ]
    handed = shift(first[0][2], -1)
    near = join_call(first[0][3], handed, first[1][3])
    near = shift(near, -1)
    far = [None, shift(first[1][2], -2)]
    query_grad, parts = None, []
    for c in chunks:
        query_grad, part = rest_call(
            first[c][0], first[c][1], queries, out_grad, own[c], one[c], two[c], far[c], query_grad,
            c * step, group, tokens, scale,
        )
        parts.append(part)
    key_grad, value_grad = final_call(near, parts)
    return query_grad, key_grad, value_grad


def solution(mesh):
    rows = P(AXES, None)
    return jax.shard_map(
        shards,
        mesh=mesh,
        in_specs=(rows, rows, rows, rows, P(AXES)),
        out_specs=(rows, rows, rows),
        check_vma=False,
    )
```

time: 83.9 us -> 57.9 us (0.69)
  matrix products: 18.7 us -> 0 us
  Pallas kernels: 0 us -> 13.8 us
  local copies, waits for them, and re-layouts: 9.91 us -> 2.45 us
  waiting for transfers between devices: 16.5 us -> 10.8 us
  other arithmetic: 4.66 us -> 0 us
  starting transfers between devices: 32.5 us -> 29.7 us
    dot_general x19 -> x0, matrix products: 18.7 us -> none  [the longest x3 4.03 us: backward_block(): jnp.einsum('tkgd,wkd->kgtw', grad_heads, pair[1], preferred_element_type=...]
    pallas_call x0 -> x8, Pallas kernels: none -> 13.8 us  [the longest x2 6.64 us: score_call(): pl.pallas_call(functools.partial(score_kernel, group, tokens, scale), gri...]
    ppermute x8 -> x7, waiting for transfers between devices: 16.5 us -> 10.8 us  [shift(): lax.ppermute(value, AXES, [(i, i + steps) for i in range(first, last)])]
    unnamed x14 -> x6, local copies, waits for them, and re-layouts: 6.54 us -> 2.45 us
    ppermute x8 -> x7, starting transfers between devices: 32.5 us -> 29.7 us  [shift(): lax.ppermute(value, AXES, [(i, i + steps) for i in range(first, last)])]
    another operation x6 -> x0, local copies, waits for them, and re-layouts: 2.44 us -> none  [the longest x2 1.08 us: backward_block(): pair[1]]
    reduce_sum x2 -> x0, other arithmetic: 1.9 us -> none  [forward_block(): run_sum = run_sum * shrink + jnp.sum(probs, -1)]
    another operation x3 -> x0, other arithmetic: 1.75 us -> none
  transfers between devices with their start and end apart: 8 -> 7, of which waited for: 3 -> 3; matrix products, arithmetic and copies ran while one was open for 24% -> 0% of each run, Pallas kernels for 0% -> 21%
where the time goes in v1:
time: 57.9 us; the launch traced here: 57.5 us
  starting transfers between devices  29.7 us (51%)
  Pallas kernels  13.8 us (24%)
  waiting for transfers between devices  10.8 us (19%)
  local copies, waits for them, and re-layouts  2.45 us (4%)
  between operations  0.78 us (1%)
    ppermute x7, starting transfers between devices, shift(): lax.ppermute(value, AXES, [(i, i + steps) for i in range(first, last)])  29.7 us
    ppermute x7, waiting for transfers between devices, shift(): lax.ppermute(value, AXES, [(i, i + steps) for i in range(first, last)])  10.8 us
    pallas_call x2, Pallas kernels, score_call(): pl.pallas_call(functools.partial(score_kernel, group, tokens, scale), gri...  6.64 us
    pallas_call x2, Pallas kernels, rest_call(): pl.pallas_call(functools.partial(rest_kernel, group, tokens, scale), grid...  4.24 us
    unnamed x6, local copies, waits for them, and re-layouts  2.45 us
  transfers between devices with their start and end apart: 7, of which 3 were waited for; matrix products, arithmetic and copies ran while one was open for 0% of the time, Pallas kernels for 21%

profile of v1, /device:TPU:4, one launch (start us, length us, event | category | flops | bytes accessed | tf_op | source)
XLA Modules:
  0.0 57.5 jit_solution(11596032994603195670)
XLA Ops:
  0.6 1.0 %pack.1 = (bf16[272,256]{1,0:T(8,128)(2,1)S(1)}, bf16[272,256]{1,0:T(8,128)(2,1)S(1)}) custom-call(bf16[128,512]{1,0:T(8,128)(2,1)} %k_ref.1, bf16[128,512]{1,0:T(8,128)(2,1)} %v_ref.1, s32[128]{0:T(128)} %seg_ref.1), custom_call_target="tpu_custom_call" | custom-call | bytes 524288 | tf_op jit(solution)/shard_map/pack/pallas_call | solution.py:211
  1.6 3.8 %collective-permute-start = (bf16[272,256]{1,0:T(8,128)(2,1)S(1)}, bf16[272,256]{1,0:T(8,128)(2,1)S(1)}, u32[]{:S(2)}, u32[]{:S(2)}) collective-permute-start(bf16[272,256]{1,0:T(8,128)(2,1)S(1)} %get-tuple-element.23.own_ref), channel_id=1, source_target_pairs={{0,1},{1,2},{2,3},{3,4},{4,5},{5,6},{6,7},{7,8},{8,9},{9,10},{10,1... | collective-permute-start | bytes 417800 | tf_op jit(solution)/shard_map/ppermute | solution.py:23
  5.5 5.2 %collective-permute-start.4 = (bf16[272,256]{1,0:T(8,128)(2,1)S(1)}, bf16[272,256]{1,0:T(8,128)(2,1)S(1)}, u32[]{:S(2)}, u32[]{:S(2)}) collective-permute-start(bf16[272,256]{1,0:T(8,128)(2,1)S(1)} %get-tuple-element.27.own_ref), channel_id=1, source_target_pairs={{0,2},{1,3},{2,4},{3,5},{4,6},{5,7},{6,8},{7,9},{8,10},{9,11},{10,... | collective-permute-start | bytes 417800 | tf_op jit(solution)/shard_map/ppermute | solution.py:23
  10.7 5.0 %collective-permute-start.3 = (bf16[272,256]{1,0:T(8,128)(2,1)S(1)}, bf16[272,256]{1,0:T(8,128)(2,1)S(1)}, u32[]{:S(2)}, u32[]{:S(2)}) collective-permute-start(bf16[272,256]{1,0:T(8,128)(2,1)S(1)} %get-tuple-element.27.own_ref), channel_id=1, source_target_pairs={{0,1},{1,2},{2,3},{3,4},{4,5},{5,6},{6,7},{7,8},{8,9},{9,10},{10,1... | collective-permute-start | bytes 417800 | tf_op jit(solution)/shard_map/ppermute | solution.py:23
  15.7 2.6 %collective-permute-done.one_ref = bf16[272,256]{1,0:T(8,128)(2,1)S(1)} collective-permute-done((bf16[272,256]{1,0:T(8,128)(2,1)S(1)}, bf16[272,256]{1,0:T(8,128)(2,1)S(1)}, u32[]{:S(2)}, u32[]{:S(2)}) %collective-permute-start) | collective-permute-done | bytes 139296 | tf_op jit(solution)/shard_map/ppermute | solution.py:23
  18.3 1.9 %collective-permute-start.1 = (bf16[272,256]{1,0:T(8,128)(2,1)S(1)}, bf16[272,256]{1,0:T(8,128)(2,1)S(1)}, u32[]{:S(2)}, u32[]{:S(2)}) collective-permute-start(bf16[272,256]{1,0:T(8,128)(2,1)S(1)} %collective-permute-done.one_ref), channel_id=1, source_target_pairs={{0,1},{1,2},{2,3},{3,4},{4,5},{5,6},{6,7},{7,8},{8,9},{9,10},{10,1... | collective-permute-start | bytes 417800 | tf_op jit(solution)/shard_map/ppermute | solution.py:23
  20.2 0.0 copy-start
  20.2 1.2 %copy-done = bf16[128,4096]{1,0:T(8,128)(2,1)S(1)} copy-done((bf16[128,4096]{1,0:T(8,128)(2,1)S(1)}, bf16[128,4096]{1,0:T(8,128)(2,1)}, u32[]{:S(2)}) %copy-start) | copy-done | bytes 1048600
  21.4 0.0 copy-start.2
  21.4 1.2 %copy-done.2 = bf16[128,4096]{1,0:T(8,128)(2,1)S(1)} copy-done((bf16[128,4096]{1,0:T(8,128)(2,1)S(1)}, bf16[128,4096]{1,0:T(8,128)(2,1)}, u32[]{:S(2)}) %copy-start.2) | copy-done | bytes 1048600
  22.7 1.1 %turn.1 = (bf16[128,4096]{1,0:T(8,128)(2,1)S(1)}, bf16[128,4096]{1,0:T(8,128)(2,1)S(1)}) custom-call(bf16[128,4096]{1,0:T(8,128)(2,1)S(1)} %copy-done, bf16[128,4096]{1,0:T(8,128)(2,1)S(1)} %copy-done.2), custom_call_target="tpu_custom_call" | custom-call | bytes 8388608 | tf_op jit(solution)/shard_map/turn/pallas_call | solution.py:228
  23.8 0.0 collective-permute-done.4.two_ref
  23.8 3.3 %collective-permute-done.3.one_ref = bf16[272,256]{1,0:T(8,128)(2,1)S(1)} collective-permute-done((bf16[272,256]{1,0:T(8,128)(2,1)S(1)}, bf16[272,256]{1,0:T(8,128)(2,1)S(1)}, u32[]{:S(2)}, u32[]{:S(2)}) %collective-permute-start.3) | collective-permute-done | bytes 139296 | tf_op jit(solution)/shard_map/ppermute | solution.py:23
  27.1 3.3 %scores.3 = (bf16[128,2048]{1,0:T(8,128)(2,1)S(1)}, bf16[256,2048]{1,0:T(8,128)(2,1)S(1)}, bf16[256,256]{1,0:T(8,128)(2,1)S(1)}, f32[256,256]{1,0:T(8,128)S(1)}) custom-call(bf16[128,4096]{1,0:T(8,128)(2,1)S(1)} %copy-done, bf16[128,4096]{1,0:T(8,128)(2,1)S(1)} %copy-done.2, bf16[128,4096]{1,0:T(8,128)(2,1)S(1)} %get-tuple-element.21.qt_ref, ...), custom_call_target="tpu_custom_call" | custom-call | flops 805306368 | bytes 3145728 | tf_op jit(solution)/shard_map/scores/pallas_call | solution.py:245
  30.4 4.6 %collective-permute-start.5 = (bf16[256,256]{1,0:T(8,128)(2,1)S(1)}, bf16[256,256]{1,0:T(8,128)(2,1)S(1)}, u32[]{:S(2)}, u32[]{:S(2)}) collective-permute-start(bf16[256,256]{1,0:T(8,128)(2,1)S(1)} %get-tuple-element.33), channel_id=1, source_target_pairs={{1,0},{2,1},{3,2},{4,3},{5,4},{6,5},{7,6},{8,7},{9,8},{10,9},{11,1... | collective-permute-start | bytes 393224 | tf_op jit(solution)/shard_map/ppermute | solution.py:23
  35.0 0.0 collective-permute-done.1.two_ref
  35.0 0.0 copy-start.1
  35.0 3.3 %scores.2 = (bf16[128,2048]{1,0:T(8,128)(2,1)S(1)}, bf16[256,2048]{1,0:T(8,128)(2,1)S(1)}, bf16[256,256]{1,0:T(8,128)(2,1)S(1)}, f32[256,256]{1,0:T(8,128)S(1)}) custom-call(bf16[128,4096]{1,0:T(8,128)(2,1)S(1)} %copy-done, bf16[128,4096]{1,0:T(8,128)(2,1)S(1)} %copy-done.2, bf16[128,4096]{1,0:T(8,128)(2,1)S(1)} %get-tuple-element.21.qt_ref, ...), custom_call_target="tpu_custom_call" | custom-call | flops 805306368 | bytes 3145728 | tf_op jit(solution)/shard_map/scores/pallas_call | solution.py:245
  38.4 0.0 collective-permute-done.5.handed_ref
  38.4 7.3 %collective-permute-start.6 = (bf16[256,512]{1,0:T(8,128)(2,1)S(1)}, bf16[256,512]{1,0:T(8,128)(2,1)S(1)}, u32[]{:S(2)}, u32[]{:S(2)}) collective-permute-start(bf16[256,512]{1,0:T(8,128)(2,1)S(1)} %join.1), channel_id=1, source_target_pairs={{1,0},{2,1},{3,2},{4,3},{5,4},{6,5},{7,6},{8,7},{9,8},{10,9},{11,1... | collective-permute-start | bytes 786440 | tf_op jit(solution)/shard_map/ppermute | solution.py:23
  45.7 1.9 %collective-permute-start.2 = (bf16[256,256]{1,0:T(8,128)(2,1)S(1)}, bf16[256,256]{1,0:T(8,128)(2,1)S(1)}, u32[]{:S(2)}, u32[]{:S(2)}) collective-permute-start(bf16[256,256]{1,0:T(8,128)(2,1)S(1)} %get-tuple-element.26), channel_id=1, source_target_pairs={{2,0},{3,1},{4,2},{5,3},{6,4},{7,5},{8,6},{9,7},{10,8},{11,9},{12,... | collective-permute-start | bytes 393224 | tf_op jit(solution)/shard_map/ppermute | solution.py:23
  47.6 0.0 copy-done.1
  47.6 2.1 %rest.2 = (bf16[128,4096]{1,0:T(8,128)(2,1)}, f32[256,256]{1,0:T(8,128)S(1)}) custom-call(bf16[128,2048]{1,0:T(8,128)(2,1)S(1)} %get-tuple-element.28.p_ref, bf16[256,2048]{1,0:T(8,128)(2,1)S(1)} %get-tuple-element.29.ds_ref, bf16[128,4096]{1,0:T(8,128)(2,1)S(1)} %copy-done.1, bf16[128,4096]{1,0:T(8,128)(2,1)S(1)} %copy-done.2, ...), custom_call_target="tpu_custom_call" | custom-call | flops 402653184 | bytes 3145728 | tf_op jit(solution)/shard_map/rest/pallas_call | solution.py:277
  49.7 4.9 %collective-permute-done.2.refs_0_ = bf16[256,256]{1,0:T(8,128)(2,1)S(1)} collective-permute-done((bf16[256,256]{1,0:T(8,128)(2,1)S(1)}, bf16[256,256]{1,0:T(8,128)(2,1)S(1)}, u32[]{:S(2)}, u32[]{:S(2)}) %collective-permute-start.2) | collective-permute-done | bytes 131104 | tf_op jit(solution)/shard_map/ppermute | solution.py:23
  54.6 2.1 %rest.3 = (bf16[128,4096]{1,0:T(8,128)(2,1)}, f32[256,256]{1,0:T(8,128)S(1)}) custom-call(bf16[128,2048]{1,0:T(8,128)(2,1)S(1)} %get-tuple-element.24.p_ref, bf16[256,2048]{1,0:T(8,128)(2,1)S(1)} %get-tuple-element.25.ds_ref, bf16[128,4096]{1,0:T(8,128)(2,1)S(1)} %copy-done.1, bf16[128,4096]{1,0:T(8,128)(2,1)S(1)} %copy-done.2, ...), custom_call_target="tpu_custom_call", output_to_operand_aliasing={{0}: (8, {})} | custom-call | flops 402653184 | bytes 3145728 | tf_op jit(solution)/shard_map/rest/pallas_call | solution.py:277
  56.7 0.0 collective-permute-done.6.near_ref
  56.7 0.7 %final.1 = (bf16[128,512]{1,0:T(8,128)(2,1)}, bf16[128,512]{1,0:T(8,128)(2,1)}) custom-call(bf16[256,512]{1,0:T(8,128)(2,1)S(1)} %collective-permute-done.6.near_ref, f32[256,256]{1,0:T(8,128)S(1)} %get-tuple-element.35.refs_0_, f32[256,256]{1,0:T(8,128)S(1)} %get-tuple-element.36.refs_1_), custom_call_target="tpu_custom_call" | custom-call | bytes 1048576 | tf_op jit(solution)/shard_map/final/pallas_call | solution.py:303
  (1 shorter events, 0.0 us)
Async XLA Ops:
  1.6 16.7 %collective-permute-start = (bf16[272,256]{1,0:T(8,128)(2,1)S(1)}, bf16[272,256]{1,0:T(8,128)(2,1)S(1)}, u32[]{:S(2)}, u32[]{:S(2)}) collective-permute-start(bf16[272,256]{1,0:T(8,128)(2,1)S(1)} %get-tuple-element.23.own_ref), channel_id=1, source_target_pairs={{0,1},{1,2},{2,3},{3,4},{4,5},{5,6},{6,7},{7,8},{8,9},{9,10},{10,1... | collective-permute-start | bytes 417800 | tf_op jit(solution)/shard_map/ppermute | solution.py:23
  5.5 18.3 %collective-permute-start.4 = (bf16[272,256]{1,0:T(8,128)(2,1)S(1)}, bf16[272,256]{1,0:T(8,128)(2,1)S(1)}, u32[]{:S(2)}, u32[]{:S(2)}) collective-permute-start(bf16[272,256]{1,0:T(8,128)(2,1)S(1)} %get-tuple-element.27.own_ref), channel_id=1, source_target_pairs={{0,2},{1,3},{2,4},{3,5},{4,6},{5,7},{6,8},{7,9},{8,10},{9,11},{10,... | collective-permute-start | bytes 417800 | tf_op jit(solution)/shard_map/ppermute | solution.py:23
  10.7 16.5 %collective-permute-start.3 = (bf16[272,256]{1,0:T(8,128)(2,1)S(1)}, bf16[272,256]{1,0:T(8,128)(2,1)S(1)}, u32[]{:S(2)}, u32[]{:S(2)}) collective-permute-start(bf16[272,256]{1,0:T(8,128)(2,1)S(1)} %get-tuple-element.27.own_ref), channel_id=1, source_target_pairs={{0,1},{1,2},{2,3},{3,4},{4,5},{5,6},{6,7},{7,8},{8,9},{9,10},{10,1... | collective-permute-start | bytes 417800 | tf_op jit(solution)/shard_map/ppermute | solution.py:23
  18.3 16.7 %collective-permute-start.1 = (bf16[272,256]{1,0:T(8,128)(2,1)S(1)}, bf16[272,256]{1,0:T(8,128)(2,1)S(1)}, u32[]{:S(2)}, u32[]{:S(2)}) collective-permute-start(bf16[272,256]{1,0:T(8,128)(2,1)S(1)} %collective-permute-done.one_ref), channel_id=1, source_target_pairs={{0,1},{1,2},{2,3},{3,4},{4,5},{5,6},{6,7},{7,8},{8,9},{9,10},{10,1... | collective-permute-start | bytes 417800 | tf_op jit(solution)/shard_map/ppermute | solution.py:23
  20.2 1.2 %copy-start = (bf16[128,4096]{1,0:T(8,128)(2,1)S(1)}, bf16[128,4096]{1,0:T(8,128)(2,1)}, u32[]{:S(2)}) copy-start(bf16[128,4096]{1,0:T(8,128)(2,1)} %q_ref.9) | copy-start | bytes 3145732
  21.4 1.2 %copy-start.2 = (bf16[128,4096]{1,0:T(8,128)(2,1)S(1)}, bf16[128,4096]{1,0:T(8,128)(2,1)}, u32[]{:S(2)}) copy-start(bf16[128,4096]{1,0:T(8,128)(2,1)} %g_ref.9) | copy-start | bytes 3145732
  30.4 7.9 %collective-permute-start.5 = (bf16[256,256]{1,0:T(8,128)(2,1)S(1)}, bf16[256,256]{1,0:T(8,128)(2,1)S(1)}, u32[]{:S(2)}, u32[]{:S(2)}) collective-permute-start(bf16[256,256]{1,0:T(8,128)(2,1)S(1)} %get-tuple-element.33), channel_id=1, source_target_pairs={{1,0},{2,1},{3,2},{4,3},{5,4},{6,5},{7,6},{8,7},{9,8},{10,9},{11,1... | collective-permute-start | bytes 393224 | tf_op jit(solution)/shard_map/ppermute | solution.py:23
  35.0 12.6 %copy-start.1 = (bf16[128,4096]{1,0:T(8,128)(2,1)S(1)}, bf16[128,4096]{1,0:T(8,128)(2,1)}, u32[]{:S(2)}) copy-start(bf16[128,4096]{1,0:T(8,128)(2,1)} %q_ref.9) | copy-start | bytes 3145732
  38.4 18.3 %collective-permute-start.6 = (bf16[256,512]{1,0:T(8,128)(2,1)S(1)}, bf16[256,512]{1,0:T(8,128)(2,1)S(1)}, u32[]{:S(2)}, u32[]{:S(2)}) collective-permute-start(bf16[256,512]{1,0:T(8,128)(2,1)S(1)} %join.1), channel_id=1, source_target_pairs={{1,0},{2,1},{3,2},{4,3},{5,4},{6,5},{7,6},{8,7},{9,8},{10,9},{11,1... | collective-permute-start | bytes 786440 | tf_op jit(solution)/shard_map/ppermute | solution.py:23
  45.7 8.9 %collective-permute-start.2 = (bf16[256,256]{1,0:T(8,128)(2,1)S(1)}, bf16[256,256]{1,0:T(8,128)(2,1)S(1)}, u32[]{:S(2)}, u32[]{:S(2)}) collective-permute-start(bf16[256,256]{1,0:T(8,128)(2,1)S(1)} %get-tuple-element.26), channel_id=1, source_target_pairs={{2,0},{3,1},{4,2},{5,3},{6,4},{7,5},{8,6},{9,7},{10,8},{11,9},{12,... | collective-permute-start | bytes 393224 | tf_op jit(solution)/shard_map/ppermute | solution.py:23

commit v2 on v1

v2 whole, which is shorter than its diff:
```python
import functools

import jax
import jax.numpy as jnp
from jax import lax
from jax.experimental import pallas as pl
from jax.experimental.pallas import tpu as pltpu
from jax.sharding import PartitionSpec as P

HK = 4
HD = 128
SEG_ROWS = 16
NEG = -1e30
LOG2E = 1.4426950408889634
AXES = ("inner", "outer")
CHUNKS = 2
VMEM_LIMIT = 24 * 1024 * 1024


def shift(value, steps):
    count = lax.axis_size(AXES)
    first, last = max(0, -steps), min(count, count - steps)
    return lax.ppermute(value, AXES, [(i, i + steps) for i in range(first, last)])


def dot(a, b):
    return jnp.dot(a, b, preferred_element_type=jnp.float32)


def stacked(ref, first, count):
    return jnp.concatenate(
        [ref[:, (first + h) * HD : (first + h + 1) * HD] for h in range(count)], axis=0
    )


def sees_own(tokens, copies):
    key = lax.broadcasted_iota(jnp.int32, (tokens, tokens), 0)
    query = lax.broadcasted_iota(jnp.int32, (tokens, tokens), 1)
    return jnp.concatenate([key <= query] * copies, axis=1)


def segments(payload, tokens):
    coded = payload[2 * tokens : 2 * tokens + SEG_ROWS, :].astype(jnp.float32)
    row = coded[0:1] * 2.0 + coded[1:2]
    return jnp.broadcast_to(row, (tokens, tokens))


def pack_kernel(tokens, k_ref, v_ref, seg_ref, *refs):
    out_refs, seg_own, sems = refs[:-2], refs[-2], refs[-1]
    width = k_ref.shape[1] // len(out_refs)
    ids = pltpu.make_async_copy(seg_ref, seg_own, sems.at[0])
    ids.start()
    copies = []
    for index, out_ref in enumerate(out_refs):
        cols = pl.ds(index * width, width)
        for half, source in enumerate((k_ref, v_ref)):
            copies.append(
                pltpu.make_async_copy(
                    source.at[:, cols], out_ref.at[pl.ds(half * tokens, tokens), :],
                    sems.at[1 + 2 * index + half],
                )
            )
    for copy in copies:
        copy.start()
    ids.wait()
    seg = jnp.broadcast_to((seg_own[...] + 1)[None, :], (SEG_ROWS, tokens))
    row = lax.broadcasted_iota(jnp.int32, (SEG_ROWS, tokens), 0)
    coded = jnp.where(row == 0, seg >> 1, jnp.where(row == 1, seg & 1, 0))
    coded = coded.astype(jnp.float32).astype(jnp.bfloat16)
    out_refs[0][2 * tokens : 2 * tokens + SEG_ROWS, :] = jnp.concatenate([coded] * (width // tokens), axis=1)
    for copy in copies:
        copy.wait()


def turn_kernel(q_ref, g_ref, q_out, g_out, qt_ref, gt_ref, sems):
    width = q_ref.shape[1] // HK
    copies = []
    for part in range(HK):
        cols = pl.ds(part * width, width)
        for side, (source, target) in enumerate(((q_ref, q_out), (g_ref, g_out))):
            copies.append(pltpu.make_async_copy(source.at[:, cols], target.at[:, cols], sems.at[2 * part + side]))
    for copy in copies:
        copy.start()
    for part in range(HK):
        for side, (source, target) in enumerate(((q_out, qt_ref), (g_out, gt_ref))):
            copies[2 * part + side].wait()
            for h in range(width // HD):
                cols = slice(part * width + h * HD, part * width + (h + 1) * HD)
                target[:, cols] = jnp.transpose(source[:, cols])


def score_kernel(group, tokens, scale, known, offset, q_ref, g_ref, qt_ref, gt_ref, own_ref, one_ref, two_ref,
                 *refs):
    p_ref, ds_ref, far_ref, near_ref = refs[1:] if known else refs[:-1]
    bias_ref = refs[0] if known else refs[-1]
    if known:
        bias = bias_ref[...]
    else:
        ids = slice(0, HD)
        seg_query = segments(own_ref[:, ids], tokens)
        seg_own = jnp.transpose(seg_query)
        seg_one = jnp.transpose(segments(one_ref[:, ids], tokens))
        seg_two = jnp.transpose(segments(two_ref[:, ids], tokens))
        mixed = jnp.where(sees_own(tokens, 1), seg_own, seg_two)
        bias = jnp.concatenate(
            [jnp.where(mixed == seg_query, 0.0, NEG), jnp.where(seg_one == seg_query, 0.0, NEG)], axis=0
        )
        bias_ref[...] = bias
    bias_mix = jnp.concatenate([bias[0:tokens]] * 2, axis=1)
    bias_one = jnp.concatenate([bias[tokens:]] * 2, axis=1)
    tri = sees_own(tokens, 2)
    far_mask = jnp.where(tri, 0.0, 1.0).astype(jnp.bfloat16)
    factor = scale * LOG2E
    pairs = group // 2
    count = own_ref.shape[1] // HD

    def products(unit):
        part, pair = divmod(unit, pairs)
        cols = slice(part * HD, (part + 1) * HD)
        keys, vals = [
            jnp.concatenate([ref[rows, cols] for ref in (own_ref, one_ref, two_ref)], axis=0)
            for rows in (slice(0, tokens), slice(tokens, 2 * tokens))
        ]
        first = (offset + part) * group + 2 * pair
        both = slice(first * HD, (first + 2) * HD)
        return dot(keys, qt_ref[:, both]), dot(vals, gt_ref[:, both])

    ahead = products(0)
    for part in range(count):
        sum_k = jnp.zeros((2 * tokens, HD), jnp.float32)
        sum_v = jnp.zeros((2 * tokens, HD), jnp.float32)
        for pair in range(pairs):
            unit = part * pairs + pair
            raw, dp = ahead
            if unit + 1 < count * pairs:
                ahead = products(unit + 1)
            cols = slice(unit * 2 * HD, (unit + 1) * 2 * HD)
            first = (offset + part) * group + 2 * pair
            s_mix = jnp.where(tri, raw[0:tokens], raw[2 * tokens :]) + bias_mix
            s_one = raw[tokens : 2 * tokens] + bias_one
            top = jnp.max(jnp.maximum(s_mix, s_one), axis=0, keepdims=True)
            e_mix = jnp.exp2((s_mix - top) * factor)
            e_one = jnp.exp2((s_one - top) * factor)
            inverse = 1.0 / jnp.sum(e_mix + e_one, axis=0, keepdims=True)
            p_mix = e_mix * inverse
            p_one = e_one * inverse
            d_mix = jnp.where(tri, dp[0:tokens], dp[2 * tokens :])
            d_one = dp[tokens : 2 * tokens]
            delta = jnp.sum(p_mix * d_mix + p_one * d_one, axis=0, keepdims=True)
            ds_mix = (p_mix * (d_mix - delta)).astype(jnp.bfloat16)
            ds_one = (p_one * (d_one - delta)).astype(jnp.bfloat16)
            p_mix = p_mix.astype(jnp.bfloat16)
            p_one = p_one.astype(jnp.bfloat16)
            p_ref[:, cols] = p_mix
            ds_ref[0:tokens, cols] = ds_mix
            ds_ref[tokens : 2 * tokens, cols] = ds_one
            sum_k = sum_k + dot(jnp.concatenate([ds_one, ds_mix * far_mask], axis=0), stacked(q_ref, first, 2))
            sum_v = sum_v + dot(jnp.concatenate([p_one, p_mix * far_mask], axis=0), stacked(g_ref, first, 2))
        cols = slice(part * HD, (part + 1) * HD)
        near_ref[0:tokens, cols] = (sum_k[0:tokens] * scale).astype(near_ref.dtype)
        near_ref[tokens : 2 * tokens, cols] = sum_v[0:tokens].astype(near_ref.dtype)
        far_ref[0:tokens, cols] = (sum_k[tokens:] * scale).astype(far_ref.dtype)
        far_ref[tokens : 2 * tokens, cols] = sum_v[tokens:].astype(far_ref.dtype)


def rest_kernel(group, tokens, scale, *refs):
    per = 5
    q_ref, g_ref = refs[0:2]
    chunk_refs = [refs[2 + per * c : 2 + per * (c + 1)] for c in range(CHUNKS)]
    dq_out = refs[2 + per * CHUNKS]
    own_outs = refs[3 + per * CHUNKS : 3 + per * CHUNKS + CHUNKS]
    dq_ref, sems = refs[-2:]
    tri = sees_own(tokens, 2)
    own_mask = jnp.where(tri, 1.0, 0.0).astype(jnp.bfloat16)
    far_mask = jnp.where(tri, 0.0, 1.0).astype(jnp.bfloat16)
    wide = group * HD
    copies = []
    for chunk, (p_ref, ds_ref, own_ref, one_ref, two_ref) in enumerate(chunk_refs):
        count = own_ref.shape[1] // HD
        for part in range(count):
            inner = slice(part * HD, (part + 1) * HD)
            keys_t = jnp.concatenate(
                [jnp.transpose(ref[0:tokens, inner]) for ref in (own_ref, one_ref, two_ref)], axis=1
            )
            sum_k = jnp.zeros((tokens, HD), jnp.float32)
            sum_v = jnp.zeros((tokens, HD), jnp.float32)
            for pair in range(group // 2):
                cols = slice(part * wide + pair * 2 * HD, part * wide + (pair + 1) * 2 * HD)
                first = (chunk * count + part) * group + 2 * pair
                ds_mix = ds_ref[0:tokens, cols]
                ds_own = ds_mix * own_mask
                sum_k = sum_k + dot(ds_own, stacked(q_ref, first, 2))
                sum_v = sum_v + dot(p_ref[:, cols] * own_mask, stacked(g_ref, first, 2))
                rows = jnp.concatenate([ds_own, ds_ref[tokens : 2 * tokens, cols], ds_mix * far_mask], axis=0)
                dq_t = (dot(keys_t, rows) * scale).astype(jnp.bfloat16)
                for h in range(2):
                    dq_ref[:, (first + h) * HD : (first + h + 1) * HD] = jnp.transpose(
                        dq_t[:, h * HD : (h + 1) * HD]
                    )
            own_outs[chunk][0:tokens, inner] = sum_k * scale
            own_outs[chunk][tokens : 2 * tokens, inner] = sum_v
            index = chunk * count + part
            span = pl.ds(index * wide, wide)
            copies.append(pltpu.make_async_copy(dq_ref.at[:, span], dq_out.at[:, span], sems.at[index]))
            copies[-1].start()
    for copy in copies:
        copy.wait()


def final_kernel(tokens, *refs):
    count = (len(refs) - 2) // 3
    k_out, v_out = refs[-2:]
    for index in range(count):
        own_ref, near_ref, far_ref = refs[index : 3 * count : count]
        width = own_ref.shape[1]
        cols = slice(index * width, (index + 1) * width)
        total = own_ref[...] + near_ref[...].astype(jnp.float32) + far_ref[...].astype(jnp.float32)
        k_out[:, cols] = total[0:tokens].astype(k_out.dtype)
        v_out[:, cols] = total[tokens:].astype(v_out.dtype)


def bf16(*shape):
    return jax.ShapeDtypeStruct(shape, jnp.bfloat16)


def f32(*shape):
    return jax.ShapeDtypeStruct(shape, jnp.float32)


def cost(flops, bytes_accessed, transcendentals=0):
    return pl.CostEstimate(flops=flops, bytes_accessed=bytes_accessed, transcendentals=transcendentals)


PARAMS = pltpu.CompilerParams(vmem_limit_bytes=VMEM_LIMIT)


def pack_call(key_states, value_states, segment_ids):
    tokens, width = key_states.shape
    operands = [pltpu.with_memory_space_constraint(x, pltpu.HBM) for x in (key_states, value_states, segment_ids)]
    return pl.pallas_call(
        functools.partial(pack_kernel, tokens),
        in_specs=[pl.BlockSpec(memory_space=pltpu.HBM)] * 3,
        out_shape=[bf16(2 * tokens + (0 if c else SEG_ROWS), width // CHUNKS) for c in range(CHUNKS)],
        scratch_shapes=[
            pltpu.VMEM((tokens,), jnp.int32),
            pltpu.SemaphoreType.DMA((1 + 2 * CHUNKS,)),
        ],
        cost_estimate=cost(0, 8 * tokens * width),
        compiler_params=PARAMS,
        name="pack",
    )(*operands)


def turn_call(q, g):
    tokens, span = q.shape
    operands = [pltpu.with_memory_space_constraint(x, pltpu.HBM) for x in (q, g)]
    return pl.pallas_call(
        turn_kernel,
        in_specs=[pl.BlockSpec(memory_space=pltpu.HBM)] * 2,
        out_shape=[bf16(tokens, span)] * 2 + [bf16(HD, span)] * 2,
        scratch_shapes=[pltpu.SemaphoreType.DMA((2 * HK,))],
        cost_estimate=cost(0, 16 * tokens * span),
        compiler_params=PARAMS,
        name="turn",
    )(*operands)


def score_call(q, g, qt, gt, own, one, two, bias, offset, group, tokens, scale):
    count = own.shape[1] // HD
    span = count * group * HD
    known = bias is not None
    return pl.pallas_call(
        functools.partial(score_kernel, group, tokens, scale, known, offset),
        out_shape=[
            bf16(tokens, span),
            bf16(2 * tokens, span),
            bf16(2 * tokens, count * HD),
            bf16(2 * tokens, count * HD),
        ]
        + [f32(2 * tokens, tokens)] * (not known),
        cost_estimate=cost(2 * tokens * 3 * span * tokens * 4, 12 * tokens * span, 2 * tokens * span),
        compiler_params=PARAMS,
        name="scores",
    )(q, g, qt, gt, own, one, two, *([bias] if known else []))


def rest_call(q, g, parts, group, tokens, scale):
    count = parts[0][2].shape[1] // HD
    return pl.pallas_call(
        functools.partial(rest_kernel, group, tokens, scale),
        out_specs=[pl.BlockSpec(memory_space=pltpu.HBM)] + [pl.BlockSpec(memory_space=pltpu.VMEM)] * CHUNKS,
        out_shape=[bf16(*q.shape)] + [f32(2 * tokens, count * HD)] * CHUNKS,
        scratch_shapes=[pltpu.VMEM(q.shape, jnp.bfloat16), pltpu.SemaphoreType.DMA((HK,))],
        cost_estimate=cost(2 * tokens * 3 * q.shape[1] * tokens * 2, 12 * tokens * q.shape[1]),
        compiler_params=PARAMS,
        name="rest",
    )(q, g, *[x for part in parts for x in part])


def final_call(owns, nears, fars):
    tokens = owns[0].shape[0] // 2
    width = sum(x.shape[1] for x in owns)
    return pl.pallas_call(
        functools.partial(final_kernel, tokens),
        out_shape=[bf16(tokens, width)] * 2,
        cost_estimate=cost(0, 16 * tokens * width),
        compiler_params=PARAMS,
        name="final",
    )(*owns, *nears, *fars)


def shards(queries, key_states, value_states, out_grad, segment_ids):
    tokens = queries.shape[0]
    group = queries.shape[1] // (HK * HD)
    scale = HD ** (-0.5)
    chunks = range(CHUNKS)
    step = HK // CHUNKS
    own = pack_call(key_states, value_states, segment_ids)
    one, two = [], []
    for x in own:
        two.append(shift(x, 2))
        one.append(shift(x, 1))
    q, g, qt, gt = turn_call(queries, out_grad)
    first, near, far, bias = [], [], [], None
    for c in chunks:
        results = score_call(q, g, qt, gt, own[c], one[c], two[c], bias, c * step, group, tokens, scale)
        bias = results[4] if bias is None else bias
        first.append(results)
        far.append(shift(results[2], -2))
        near.append(shift(results[3], -1))
    ds = [x[1] for x in first]
    ds[0], ds[1], near[0], far[0] = lax.optimization_barrier((ds[0], ds[1], near[0], far[0]))
    query_grad, *parts = rest_call(
        q, g, [(first[c][0], ds[c], own[c], one[c], two[c]) for c in chunks], group, tokens, scale
    )
    key_grad, value_grad = final_call(parts, near, far)
    return query_grad, key_grad, value_grad


def solution(mesh):
    rows = P(AXES, None)
    return jax.shard_map(
        shards,
        mesh=mesh,
        in_specs=(rows, rows, rows, rows, P(AXES)),
        out_specs=(rows, rows, rows),
        check_vma=False,
    )
```

time: 57.9 us -> 52.4 us (0.905)
  waiting for transfers between devices: 10.8 us -> 6.76 us
  starting transfers between devices: 29.7 us -> 33.2 us
  Pallas kernels: 13.8 us -> 11.1 us
  local copies, waits for them, and re-layouts: 2.45 us -> 0 us
    ppermute x7 -> x8, waiting for transfers between devices: 10.8 us -> 6.76 us  [shift(): lax.ppermute(value, AXES, [(i, i + steps) for i in range(first, last)])]
    ppermute x7 -> x8, starting transfers between devices: 29.7 us -> 33.2 us  [shift(): lax.ppermute(value, AXES, [(i, i + steps) for i in range(first, last)])]
    pallas_call x6 -> x4, Pallas kernels: 12 us -> 9.33 us  [the longest x2 5.11 us: score_call(): pl.pallas_call(functools.partial(score_kernel, group, tokens, scale, know...]
    unnamed x6 -> x0, local copies, waits for them, and re-layouts: 2.45 us -> none
  transfers between devices with their start and end apart: 7 -> 8, of which waited for: 3 -> 2; matrix products, arithmetic and copies ran while one was open for 0% -> 0% of each run, Pallas kernels for 21% -> 18%
where the time goes in v2:
time: 52.4 us; the launch traced here: 51.8 us
  starting transfers between devices  33.2 us (63%)
  Pallas kernels  11.1 us (21%)
  waiting for transfers between devices  6.76 us (13%)
  between operations  0.77 us (1%)
    ppermute x8, starting transfers between devices, shift(): lax.ppermute(value, AXES, [(i, i + steps) for i in range(first, last)])  33.2 us
    ppermute x8, waiting for transfers between devices, shift(): lax.ppermute(value, AXES, [(i, i + steps) for i in range(first, last)])  6.76 us
    pallas_call x2, Pallas kernels, score_call(): pl.pallas_call(functools.partial(score_kernel, group, tokens, scale, know...  5.11 us
    pallas_call x1, Pallas kernels, rest_call(): pl.pallas_call(functools.partial(rest_kernel, group, tokens, scale), out_...  2.19 us
    pallas_call x1, Pallas kernels, turn_call(): pl.pallas_call(turn_kernel, in_specs=[pl.BlockSpec(memory_space=pltpu.HBM...  2.02 us
  transfers between devices with their start and end apart: 8, of which 2 were waited for; matrix products, arithmetic and copies ran while one was open for 0% of the time, Pallas kernels for 18%

profile of v2, /device:TPU:4, one launch (start us, length us, event | category | flops | bytes accessed | tf_op | source)
XLA Modules:
  0.0 51.8 jit_solution(3352212215683503749)
XLA Ops:
  0.6 1.0 %pack.1 = (bf16[272,256]{1,0:T(8,128)(2,1)S(1)}, bf16[256,256]{1,0:T(8,128)(2,1)S(1)}) custom-call(bf16[128,512]{1,0:T(8,128)(2,1)} %k_ref.1, bf16[128,512]{1,0:T(8,128)(2,1)} %v_ref.1, s32[128]{0:T(128)} %seg_ref.1), custom_call_target="tpu_custom_call" | custom-call | bytes 524288 | tf_op jit(solution)/shard_map/pack/pallas_call | solution.py:240
  1.6 5.2 %collective-permute-start.1 = (bf16[272,256]{1,0:T(8,128)(2,1)S(1)}, bf16[272,256]{1,0:T(8,128)(2,1)S(1)}, u32[]{:S(2)}, u32[]{:S(2)}) collective-permute-start(bf16[272,256]{1,0:T(8,128)(2,1)S(1)} %get-tuple-element.31.own_ref.refs_4_), channel_id=1, source_target_pairs={{0,2},{1,3},{2,4},{3,5},{4,6},{5,7},{6,8},{7,9},{8,10},{9,11},{10,... | collective-permute-start | bytes 417800 | tf_op jit(solution)/shard_map/ppermute | solution.py:23
  6.8 3.8 %collective-permute-start = (bf16[272,256]{1,0:T(8,128)(2,1)S(1)}, bf16[272,256]{1,0:T(8,128)(2,1)S(1)}, u32[]{:S(2)}, u32[]{:S(2)}) collective-permute-start(bf16[272,256]{1,0:T(8,128)(2,1)S(1)} %get-tuple-element.31.own_ref.refs_4_), channel_id=1, source_target_pairs={{0,1},{1,2},{2,3},{3,4},{4,5},{5,6},{6,7},{7,8},{8,9},{9,10},{10,1... | collective-permute-start | bytes 417800 | tf_op jit(solution)/shard_map/ppermute | solution.py:23
  10.7 6.4 %collective-permute-start.3 = (bf16[256,256]{1,0:T(8,128)(2,1)S(1)}, bf16[256,256]{1,0:T(8,128)(2,1)S(1)}, u32[]{:S(2)}, u32[]{:S(2)}) collective-permute-start(bf16[256,256]{1,0:T(8,128)(2,1)S(1)} %get-tuple-element.34.own_ref.refs_9_), channel_id=1, source_target_pairs={{0,2},{1,3},{2,4},{3,5},{4,6},{5,7},{6,8},{7,9},{8,10},{9,11},{10,... | collective-permute-start | bytes 393224 | tf_op jit(solution)/shard_map/ppermute | solution.py:23
  17.1 3.8 %collective-permute-start.2 = (bf16[256,256]{1,0:T(8,128)(2,1)S(1)}, bf16[256,256]{1,0:T(8,128)(2,1)S(1)}, u32[]{:S(2)}, u32[]{:S(2)}) collective-permute-start(bf16[256,256]{1,0:T(8,128)(2,1)S(1)} %get-tuple-element.34.own_ref.refs_9_), channel_id=1, source_target_pairs={{0,1},{1,2},{2,3},{3,4},{4,5},{5,6},{6,7},{7,8},{8,9},{9,10},{10,1... | collective-permute-start | bytes 393224 | tf_op jit(solution)/shard_map/ppermute | solution.py:23
  20.9 2.0 %turn.1 = (bf16[128,4096]{1,0:T(8,128)(2,1)S(1)}, bf16[128,4096]{1,0:T(8,128)(2,1)S(1)}, bf16[128,4096]{1,0:T(8,128)(2,1)S(1)}, bf16[128,4096]{1,0:T(8,128)(2,1)S(1)}) custom-call(bf16[128,4096]{1,0:T(8,128)(2,1)} %q_ref.1, bf16[128,4096]{1,0:T(8,128)(2,1)} %g_ref.1), custom_call_target="tpu_custom_call" | custom-call | bytes 8388608 | tf_op jit(solution)/shard_map/turn/pallas_call | solution.py:257
  22.9 0.0 collective-permute-done.1.two_ref.refs_6_
  22.9 1.6 %collective-permute-done.one_ref.refs_5_ = bf16[272,256]{1,0:T(8,128)(2,1)S(1)} collective-permute-done((bf16[272,256]{1,0:T(8,128)(2,1)S(1)}, bf16[272,256]{1,0:T(8,128)(2,1)S(1)}, u32[]{:S(2)}, u32[]{:S(2)}) %collective-permute-start) | collective-permute-done | bytes 139296 | tf_op jit(solution)/shard_map/ppermute | solution.py:23
  24.6 2.5 %scores.2 = (bf16[128,2048]{1,0:T(8,128)(2,1)S(1)}, bf16[256,2048]{1,0:T(8,128)(2,1)S(1)}, bf16[256,256]{1,0:T(8,128)(2,1)S(1)}, bf16[256,256]{1,0:T(8,128)(2,1)S(1)}, f32[256,128]{1,0:T(8,128)S(1)}) custom-call(bf16[128,4096]{1,0:T(8,128)(2,1)S(1)} %get-tuple-element.27.q_ref.refs_0_, bf16[128,4096]{1,0:T(8,128)(2,1)S(1)} %get-tuple-element.28.g_ref.refs_1_, ...), custom_call_target="tpu_custom_call" | custom-call | flops 805306368 | bytes 3145728 | tf_op jit(solution)/shard_map/scores/pallas_call | solution.py:272
  27.1 4.3 %collective-permute-start.4 = (bf16[256,256]{1,0:T(8,128)(2,1)S(1)}, bf16[256,256]{1,0:T(8,128)(2,1)S(1)}, u32[]{:S(2)}, u32[]{:S(2)}) collective-permute-start(bf16[256,256]{1,0:T(8,128)(2,1)S(1)} %get-tuple-element.37), channel_id=1, source_target_pairs={{1,0},{2,1},{3,2},{4,3},{5,4},{6,5},{7,6},{8,7},{9,8},{10,9},{11,1... | collective-permute-start | bytes 393224 | tf_op jit(solution)/shard_map/ppermute | solution.py:23
  31.4 2.3 %collective-permute-start.5 = (bf16[256,256]{1,0:T(8,128)(2,1)S(1)}, bf16[256,256]{1,0:T(8,128)(2,1)S(1)}, u32[]{:S(2)}, u32[]{:S(2)}) collective-permute-start(bf16[256,256]{1,0:T(8,128)(2,1)S(1)} %get-tuple-element.38), channel_id=1, source_target_pairs={{2,0},{3,1},{4,2},{5,3},{6,4},{7,5},{8,6},{9,7},{10,8},{11,9},{12,... | collective-permute-start | bytes 393224 | tf_op jit(solution)/shard_map/ppermute | solution.py:23
  33.7 0.0 collective-permute-done.3.two_ref.refs_11_
  33.7 0.0 collective-permute-done.2.one_ref.refs_10_
  33.8 2.6 %scores.3 = (bf16[128,2048]{1,0:T(8,128)(2,1)S(1)}, bf16[256,2048]{1,0:T(8,128)(2,1)S(1)}, bf16[256,256]{1,0:T(8,128)(2,1)S(1)}, bf16[256,256]{1,0:T(8,128)(2,1)S(1)}) custom-call(bf16[128,4096]{1,0:T(8,128)(2,1)S(1)} %get-tuple-element.27.q_ref.refs_0_, bf16[128,4096]{1,0:T(8,128)(2,1)S(1)} %get-tuple-element.28.g_ref.refs_1_, ...), custom_call_target="tpu_custom_call" | custom-call | flops 805306368 | bytes 3145728 | tf_op jit(solution)/shard_map/scores/pallas_call | solution.py:272
  36.3 4.0 %collective-permute-start.6 = (bf16[256,256]{1,0:T(8,128)(2,1)S(1)}, bf16[256,256]{1,0:T(8,128)(2,1)S(1)}, u32[]{:S(2)}, u32[]{:S(2)}) collective-permute-start(bf16[256,256]{1,0:T(8,128)(2,1)S(1)} %get-tuple-element.46), channel_id=1, source_target_pairs={{1,0},{2,1},{3,2},{4,3},{5,4},{6,5},{7,6},{8,7},{9,8},{10,9},{11,1... | collective-permute-start | bytes 393224 | tf_op jit(solution)/shard_map/ppermute | solution.py:23
  40.4 3.3 %collective-permute-start.7 = (bf16[256,256]{1,0:T(8,128)(2,1)S(1)}, bf16[256,256]{1,0:T(8,128)(2,1)S(1)}, u32[]{:S(2)}, u32[]{:S(2)}) collective-permute-start(bf16[256,256]{1,0:T(8,128)(2,1)S(1)} %get-tuple-element.48), channel_id=1, source_target_pairs={{2,0},{3,1},{4,2},{5,3},{6,4},{7,5},{8,6},{9,7},{10,8},{11,9},{12,... | collective-permute-start | bytes 393224 | tf_op jit(solution)/shard_map/ppermute | solution.py:23
  43.7 0.0 collective-permute-done.4.refs_2_
  43.7 0.0 collective-permute-done.5.refs_4_
  43.7 2.2 %rest.1 = (bf16[128,4096]{1,0:T(8,128)(2,1)}, f32[256,256]{1,0:T(8,128)S(1)}, f32[256,256]{1,0:T(8,128)S(1)}) custom-call(bf16[128,4096]{1,0:T(8,128)(2,1)S(1)} %get-tuple-element.27.q_ref.refs_0_, bf16[128,4096]{1,0:T(8,128)(2,1)S(1)} %get-tuple-element.28.g_ref.refs_1_, bf16[128,2048]{1,0:T(8,128)(2,1)S(1)} %get-tuple-element.32.refs_2_, ...), custom_call_target="tpu_custom_call" | custom-call | flops 805306368 | bytes 6291456 | tf_op jit(solution)/shard_map/rest/pallas_call | solution.py:289
  45.9 0.0 collective-permute-done.6.refs_3_
  45.9 5.1 %collective-permute-done.7.refs_5_ = bf16[256,256]{1,0:T(8,128)(2,1)S(1)} collective-permute-done((bf16[256,256]{1,0:T(8,128)(2,1)S(1)}, bf16[256,256]{1,0:T(8,128)(2,1)S(1)}, u32[]{:S(2)}, u32[]{:S(2)}) %collective-permute-start.7) | collective-permute-done | bytes 131104 | tf_op jit(solution)/shard_map/ppermute | solution.py:23
  51.0 0.8 %final.1 = (bf16[128,512]{1,0:T(8,128)(2,1)}, bf16[128,512]{1,0:T(8,128)(2,1)}) custom-call(f32[256,256]{1,0:T(8,128)S(1)} %get-tuple-element.43.refs_0_, f32[256,256]{1,0:T(8,128)S(1)} %get-tuple-element.44.refs_1_, bf16[256,256]{1,0:T(8,128)(2,1)S(1)} %collective-permute-done.4.refs_2_, bf16[256,256]{1,0:T(8,128)(2,1)S(1)} %collective-permute-done.6.refs_3_, ...), custom_call_target="tpu_custom_call" | custom-call | bytes 1048576 | tf_op jit(solution)/shard_map/final/pallas_call | solution.py:303
Async XLA Ops:
  1.6 21.3 %collective-permute-start.1 = (bf16[272,256]{1,0:T(8,128)(2,1)S(1)}, bf16[272,256]{1,0:T(8,128)(2,1)S(1)}, u32[]{:S(2)}, u32[]{:S(2)}) collective-permute-start(bf16[272,256]{1,0:T(8,128)(2,1)S(1)} %get-tuple-element.31.own_ref.refs_4_), channel_id=1, source_target_pairs={{0,2},{1,3},{2,4},{3,5},{4,6},{5,7},{6,8},{7,9},{8,10},{9,11},{10,... | collective-permute-start | bytes 417800 | tf_op jit(solution)/shard_map/ppermute | solution.py:23
  6.8 17.7 %collective-permute-start = (bf16[272,256]{1,0:T(8,128)(2,1)S(1)}, bf16[272,256]{1,0:T(8,128)(2,1)S(1)}, u32[]{:S(2)}, u32[]{:S(2)}) collective-permute-start(bf16[272,256]{1,0:T(8,128)(2,1)S(1)} %get-tuple-element.31.own_ref.refs_4_), channel_id=1, source_target_pairs={{0,1},{1,2},{2,3},{3,4},{4,5},{5,6},{6,7},{7,8},{8,9},{9,10},{10,1... | collective-permute-start | bytes 417800 | tf_op jit(solution)/shard_map/ppermute | solution.py:23
  10.7 23.1 %collective-permute-start.3 = (bf16[256,256]{1,0:T(8,128)(2,1)S(1)}, bf16[256,256]{1,0:T(8,128)(2,1)S(1)}, u32[]{:S(2)}, u32[]{:S(2)}) collective-permute-start(bf16[256,256]{1,0:T(8,128)(2,1)S(1)} %get-tuple-element.34.own_ref.refs_9_), channel_id=1, source_target_pairs={{0,2},{1,3},{2,4},{3,5},{4,6},{5,7},{6,8},{7,9},{8,10},{9,11},{10,... | collective-permute-start | bytes 393224 | tf_op jit(solution)/shard_map/ppermute | solution.py:23
  17.1 16.7 %collective-permute-start.2 = (bf16[256,256]{1,0:T(8,128)(2,1)S(1)}, bf16[256,256]{1,0:T(8,128)(2,1)S(1)}, u32[]{:S(2)}, u32[]{:S(2)}) collective-permute-start(bf16[256,256]{1,0:T(8,128)(2,1)S(1)} %get-tuple-element.34.own_ref.refs_9_), channel_id=1, source_target_pairs={{0,1},{1,2},{2,3},{3,4},{4,5},{5,6},{6,7},{7,8},{8,9},{9,10},{10,1... | collective-permute-start | bytes 393224 | tf_op jit(solution)/shard_map/ppermute | solution.py:23
  27.1 16.6 %collective-permute-start.4 = (bf16[256,256]{1,0:T(8,128)(2,1)S(1)}, bf16[256,256]{1,0:T(8,128)(2,1)S(1)}, u32[]{:S(2)}, u32[]{:S(2)}) collective-permute-start(bf16[256,256]{1,0:T(8,128)(2,1)S(1)} %get-tuple-element.37), channel_id=1, source_target_pairs={{1,0},{2,1},{3,2},{4,3},{5,4},{6,5},{7,6},{8,7},{9,8},{10,9},{11,1... | collective-permute-start | bytes 393224 | tf_op jit(solution)/shard_map/ppermute | solution.py:23
  31.4 12.3 %collective-permute-start.5 = (bf16[256,256]{1,0:T(8,128)(2,1)S(1)}, bf16[256,256]{1,0:T(8,128)(2,1)S(1)}, u32[]{:S(2)}, u32[]{:S(2)}) collective-permute-start(bf16[256,256]{1,0:T(8,128)(2,1)S(1)} %get-tuple-element.38), channel_id=1, source_target_pairs={{2,0},{3,1},{4,2},{5,3},{6,4},{7,5},{8,6},{9,7},{10,8},{11,9},{12,... | collective-permute-start | bytes 393224 | tf_op jit(solution)/shard_map/ppermute | solution.py:23
  36.3 9.6 %collective-permute-start.6 = (bf16[256,256]{1,0:T(8,128)(2,1)S(1)}, bf16[256,256]{1,0:T(8,128)(2,1)S(1)}, u32[]{:S(2)}, u32[]{:S(2)}) collective-permute-start(bf16[256,256]{1,0:T(8,128)(2,1)S(1)} %get-tuple-element.46), channel_id=1, source_target_pairs={{1,0},{2,1},{3,2},{4,3},{5,4},{6,5},{7,6},{8,7},{9,8},{10,9},{11,1... | collective-permute-start | bytes 393224 | tf_op jit(solution)/shard_map/ppermute | solution.py:23
  40.4 10.6 %collective-permute-start.7 = (bf16[256,256]{1,0:T(8,128)(2,1)S(1)}, bf16[256,256]{1,0:T(8,128)(2,1)S(1)}, u32[]{:S(2)}, u32[]{:S(2)}) collective-permute-start(bf16[256,256]{1,0:T(8,128)(2,1)S(1)} %get-tuple-element.48), channel_id=1, source_target_pairs={{2,0},{3,1},{4,2},{5,3},{6,4},{7,5},{8,6},{9,7},{10,8},{11,9},{12,... | collective-permute-start | bytes 393224 | tf_op jit(solution)/shard_map/ppermute | solution.py:23

commit v3 on v2

--- a/solution.py
+++ b/solution.py
@@ -45,21 +45,19 @@
     return jnp.broadcast_to(row, (tokens, tokens))
 
 
-def pack_kernel(tokens, k_ref, v_ref, seg_ref, *refs):
-    out_refs, seg_own, sems = refs[:-2], refs[-2], refs[-1]
-    width = k_ref.shape[1] // len(out_refs)
-    ids = pltpu.make_async_copy(seg_ref, seg_own, sems.at[0])
+def half_copies(index, tokens, k_ref, v_ref, out_ref, sems):
+    width = out_ref.shape[1]
+    cols = pl.ds(index * width, width)
+    return [
+        pltpu.make_async_copy(source.at[:, cols], out_ref.at[pl.ds(half * tokens, tokens), :], sems.at[half])
+        for half, source in enumerate((k_ref, v_ref))
+    ]
+
+
+def pack_kernel(tokens, k_ref, v_ref, seg_ref, out_ref, seg_own, sems):
+    ids = pltpu.make_async_copy(seg_ref, seg_own, sems.at[2])
     ids.start()
-    copies = []
-    for index, out_ref in enumerate(out_refs):
-        cols = pl.ds(index * width, width)
-        for half, source in enumerate((k_ref, v_ref)):
-            copies.append(
-                pltpu.make_async_copy(
-                    source.at[:, cols], out_ref.at[pl.ds(half * tokens, tokens), :],
-                    sems.at[1 + 2 * index + half],
-                )
-            )
+    copies = half_copies(0, tokens, k_ref, v_ref, out_ref, sems)
     for copy in copies:
         copy.start()
     ids.wait()
@@ -67,19 +65,21 @@
     row = lax.broadcasted_iota(jnp.int32, (SEG_ROWS, tokens), 0)
     coded = jnp.where(row == 0, seg >> 1, jnp.where(row == 1, seg & 1, 0))
     coded = coded.astype(jnp.float32).astype(jnp.bfloat16)
-    out_refs[0][2 * tokens : 2 * tokens + SEG_ROWS, :] = jnp.concatenate([coded] * (width // tokens), axis=1)
+    repeats = out_ref.shape[1] // tokens
+    out_ref[2 * tokens : 2 * tokens + SEG_ROWS, :] = jnp.concatenate([coded] * repeats, axis=1)
     for copy in copies:
         copy.wait()
 
 
-def turn_kernel(q_ref, g_ref, q_out, g_out, qt_ref, gt_ref, sems):
+def turn_kernel(q_ref, g_ref, k_ref, v_ref, q_out, g_out, qt_ref, gt_ref, kv_out, sems, kv_sems):
     width = q_ref.shape[1] // HK
+    halves = half_copies(1, q_ref.shape[0], k_ref, v_ref, kv_out, kv_sems)
     copies = []
     for part in range(HK):
         cols = pl.ds(part * width, width)
         for side, (source, target) in enumerate(((q_ref, q_out), (g_ref, g_out))):
             copies.append(pltpu.make_async_copy(source.at[:, cols], target.at[:, cols], sems.at[2 * part + side]))
-    for copy in copies:
+    for copy in halves + copies:
         copy.start()
     for part in range(HK):
         for side, (source, target) in enumerate(((q_out, qt_ref), (g_out, gt_ref))):
@@ -87,6 +87,8 @@
             for h in range(width // HD):
                 cols = slice(part * width + h * HD, part * width + (h + 1) * HD)
                 target[:, cols] = jnp.transpose(source[:, cols])
+    for copy in halves:
+        copy.wait()
 
 
 def score_kernel(group, tokens, scale, known, offset, q_ref, g_ref, qt_ref, gt_ref, own_ref, one_ref, two_ref,
@@ -234,35 +236,36 @@
 PARAMS = pltpu.CompilerParams(vmem_limit_bytes=VMEM_LIMIT)
 
 
+def in_hbm(*arrays):
+    return [pltpu.with_memory_space_constraint(x, pltpu.HBM) for x in arrays]
+
+
 def pack_call(key_states, value_states, segment_ids):
     tokens, width = key_states.shape
-    operands = [pltpu.with_memory_space_constraint(x, pltpu.HBM) for x in (key_states, value_states, segment_ids)]
     return pl.pallas_call(
         functools.partial(pack_kernel, tokens),
         in_specs=[pl.BlockSpec(memory_space=pltpu.HBM)] * 3,
-        out_shape=[bf16(2 * tokens + (0 if c else SEG_ROWS), width // CHUNKS) for c in range(CHUNKS)],
-        scratch_shapes=[
-            pltpu.VMEM((tokens,), jnp.int32),
-            pltpu.SemaphoreType.DMA((1 + 2 * CHUNKS,)),
-        ],
-        cost_estimate=cost(0, 8 * tokens * width),
+        out_shape=bf16(2 * tokens + SEG_ROWS, width // CHUNKS),
+        scratch_shapes=[pltpu.VMEM((tokens,), jnp.int32), pltpu.SemaphoreType.DMA((3,))],
+        cost_estimate=cost(0, 4 * tokens * width),
         compiler_params=PARAMS,
         name="pack",
-    )(*operands)
-
-
-def turn_call(q, g):
+    )(*in_hbm(key_states, value_states, segment_ids))
+
+
+def turn_call(q, g, key_states, value_states):
     tokens, span = q.shape
-    operands = [pltpu.with_memory_space_constraint(x, pltpu.HBM) for x in (q, g)]
     return pl.pallas_call(
         turn_kernel,
-        in_specs=[pl.BlockSpec(memory_space=pltpu.HBM)] * 2,
-        out_shape=[bf16(tokens, span)] * 2 + [bf16(HD, span)] * 2,
-        scratch_shapes=[pltpu.SemaphoreType.DMA((2 * HK,))],
+        in_specs=[pl.BlockSpec(memory_space=pltpu.HBM)] * 4,
+        out_shape=[bf16(tokens, span)] * 2
+        + [bf16(HD, span)] * 2
+        + [bf16(2 * tokens, key_states.shape[1] // CHUNKS)],
+        scratch_shapes=[pltpu.SemaphoreType.DMA((2 * HK,)), pltpu.SemaphoreType.DMA((2,))],
         cost_estimate=cost(0, 16 * tokens * span),
         compiler_params=PARAMS,
         name="turn",
-    )(*operands)
+    )(*in_hbm(q, g, key_states, value_states))
 
 
 def score_call(q, g, qt, gt, own, one, two, bias, offset, group, tokens, scale):
@@ -315,12 +318,11 @@
     scale = HD ** (-0.5)
     chunks = range(CHUNKS)
     step = HK // CHUNKS
-    own = pack_call(key_states, value_states, segment_ids)
-    one, two = [], []
-    for x in own:
-        two.append(shift(x, 2))
-        one.append(shift(x, 1))
-    q, g, qt, gt = turn_call(queries, out_grad)
+    own = [pack_call(key_states, value_states, segment_ids)]
+    q, g, qt, gt, later = turn_call(queries, out_grad, key_states, value_states)
+    own.append(later)
+    two = [shift(x, 2) for x in own]
+    one = [shift(x, 1) for x in own]
     first, near, far, bias = [], [], [], None
     for c in chunks:
         results = score_call(q, g, qt, gt, own[c], one[c], two[c], bias, c * step, group, tokens, scale)

time: 52.4 us -> 52.4 us (level)
  no operation moved by 1% of the time
where the time goes in v3:
time: 52.4 us; the launch traced here: 51.7 us
  starting transfers between devices  33.1 us (63%)
  Pallas kernels  10.9 us (21%)
  waiting for transfers between devices  6.97 us (13%)
  between operations  0.77 us (1%)
    ppermute x8, starting transfers between devices, shift(): lax.ppermute(value, AXES, [(i, i + steps) for i in range(first, last)])  33.1 us
    ppermute x8, waiting for transfers between devices, shift(): lax.ppermute(value, AXES, [(i, i + steps) for i in range(first, last)])  6.97 us
    pallas_call x2, Pallas kernels, score_call(): pl.pallas_call(functools.partial(score_kernel, group, tokens, scale, know...  5.04 us
    pallas_call x1, Pallas kernels, rest_call(): pl.pallas_call(functools.partial(rest_kernel, group, tokens, scale), out_...  2.16 us
    pallas_call x1, Pallas kernels, turn_call(): pl.pallas_call(turn_kernel, in_specs=[pl.BlockSpec(memory_space=pltpu.HBM...  2.04 us
  transfers between devices with their start and end apart: 8, of which 2 were waited for; matrix products, arithmetic and copies ran while one was open for 0% of the time, Pallas kernels for 18%

profile of v3, /device:TPU:4, one launch (start us, length us, event | category | flops | bytes accessed | tf_op | source)
XLA Modules:
  0.0 51.7 jit_solution(3064848908133768720)
XLA Ops:
  0.6 0.9 %pack.1.own_ref.refs_4_ = bf16[272,256]{1,0:T(8,128)(2,1)S(1)} custom-call(bf16[128,512]{1,0:T(8,128)(2,1)} %k_ref.3, bf16[128,512]{1,0:T(8,128)(2,1)} %v_ref.3, s32[128]{0:T(128)} %seg_ref.1), custom_call_target="tpu_custom_call" | custom-call | bytes 262144 | tf_op jit(solution)/shard_map/pack/pallas_call | solution.py:245
  1.6 5.2 %collective-permute-start.1 = (bf16[272,256]{1,0:T(8,128)(2,1)S(1)}, bf16[272,256]{1,0:T(8,128)(2,1)S(1)}, u32[]{:S(2)}, u32[]{:S(2)}) collective-permute-start(bf16[272,256]{1,0:T(8,128)(2,1)S(1)} %pack.1.own_ref.refs_4_), channel_id=1, source_target_pairs={{0,2},{1,3},{2,4},{3,5},{4,6},{5,7},{6,8},{7,9},{8,10},{9,11},{10,... | collective-permute-start | bytes 417800 | tf_op jit(solution)/shard_map/ppermute | solution.py:23
  6.7 3.8 %collective-permute-start = (bf16[272,256]{1,0:T(8,128)(2,1)S(1)}, bf16[272,256]{1,0:T(8,128)(2,1)S(1)}, u32[]{:S(2)}, u32[]{:S(2)}) collective-permute-start(bf16[272,256]{1,0:T(8,128)(2,1)S(1)} %pack.1.own_ref.refs_4_), channel_id=1, source_target_pairs={{0,1},{1,2},{2,3},{3,4},{4,5},{5,6},{6,7},{7,8},{8,9},{9,10},{10,1... | collective-permute-start | bytes 417800 | tf_op jit(solution)/shard_map/ppermute | solution.py:23
  10.6 2.0 %turn.1 = (bf16[128,4096]{1,0:T(8,128)(2,1)S(1)}, bf16[128,4096]{1,0:T(8,128)(2,1)S(1)}, bf16[128,4096]{1,0:T(8,128)(2,1)S(1)}, bf16[128,4096]{1,0:T(8,128)(2,1)S(1)}, bf16[256,256]{1,0:T(8,128)(2,1)S(1)}) custom-call(bf16[128,4096]{1,0:T(8,128)(2,1)} %q_ref.1, bf16[128,4096]{1,0:T(8,128)(2,1)} %g_ref.1, bf16[128,512]{1,0:T(8,128)(2,1)} %k_ref.3, ...), custom_call_target="tpu_custom_call" | custom-call | bytes 8388608 | tf_op jit(solution)/shard_map/turn/pallas_call | solution.py:258
  12.6 6.4 %collective-permute-start.3 = (bf16[256,256]{1,0:T(8,128)(2,1)S(1)}, bf16[256,256]{1,0:T(8,128)(2,1)S(1)}, u32[]{:S(2)}, u32[]{:S(2)}) collective-permute-start(bf16[256,256]{1,0:T(8,128)(2,1)S(1)} %get-tuple-element.32.own_ref.refs_9_), channel_id=1, source_target_pairs={{0,2},{1,3},{2,4},{3,5},{4,6},{5,7},{6,8},{7,9},{8,10},{9,11},{10,... | collective-permute-start | bytes 393224 | tf_op jit(solution)/shard_map/ppermute | solution.py:23
  19.0 3.8 %collective-permute-start.2 = (bf16[256,256]{1,0:T(8,128)(2,1)S(1)}, bf16[256,256]{1,0:T(8,128)(2,1)S(1)}, u32[]{:S(2)}, u32[]{:S(2)}) collective-permute-start(bf16[256,256]{1,0:T(8,128)(2,1)S(1)} %get-tuple-element.32.own_ref.refs_9_), channel_id=1, source_target_pairs={{0,1},{1,2},{2,3},{3,4},{4,5},{5,6},{6,7},{7,8},{8,9},{9,10},{10,1... | collective-permute-start | bytes 393224 | tf_op jit(solution)/shard_map/ppermute | solution.py:23
  22.9 0.0 collective-permute-done.1.two_ref.refs_6_
  22.9 1.6 %collective-permute-done.one_ref.refs_5_ = bf16[272,256]{1,0:T(8,128)(2,1)S(1)} collective-permute-done((bf16[272,256]{1,0:T(8,128)(2,1)S(1)}, bf16[272,256]{1,0:T(8,128)(2,1)S(1)}, u32[]{:S(2)}, u32[]{:S(2)}) %collective-permute-start) | collective-permute-done | bytes 139296 | tf_op jit(solution)/shard_map/ppermute | solution.py:23
  24.5 2.5 %scores.2 = (bf16[128,2048]{1,0:T(8,128)(2,1)S(1)}, bf16[256,2048]{1,0:T(8,128)(2,1)S(1)}, bf16[256,256]{1,0:T(8,128)(2,1)S(1)}, bf16[256,256]{1,0:T(8,128)(2,1)S(1)}, f32[256,128]{1,0:T(8,128)S(1)}) custom-call(bf16[128,4096]{1,0:T(8,128)(2,1)S(1)} %get-tuple-element.26.q_ref.refs_0_, bf16[128,4096]{1,0:T(8,128)(2,1)S(1)} %get-tuple-element.27.g_ref.refs_1_, ...), custom_call_target="tpu_custom_call" | custom-call | flops 805306368 | bytes 3145728 | tf_op jit(solution)/shard_map/scores/pallas_call | solution.py:275
  27.0 4.3 %collective-permute-start.4 = (bf16[256,256]{1,0:T(8,128)(2,1)S(1)}, bf16[256,256]{1,0:T(8,128)(2,1)S(1)}, u32[]{:S(2)}, u32[]{:S(2)}) collective-permute-start(bf16[256,256]{1,0:T(8,128)(2,1)S(1)} %get-tuple-element.35), channel_id=1, source_target_pairs={{1,0},{2,1},{3,2},{4,3},{5,4},{6,5},{7,6},{8,7},{9,8},{10,9},{11,1... | collective-permute-start | bytes 393224 | tf_op jit(solution)/shard_map/ppermute | solution.py:23
  31.4 2.3 %collective-permute-start.5 = (bf16[256,256]{1,0:T(8,128)(2,1)S(1)}, bf16[256,256]{1,0:T(8,128)(2,1)S(1)}, u32[]{:S(2)}, u32[]{:S(2)}) collective-permute-start(bf16[256,256]{1,0:T(8,128)(2,1)S(1)} %get-tuple-element.36), channel_id=1, source_target_pairs={{2,0},{3,1},{4,2},{5,3},{6,4},{7,5},{8,6},{9,7},{10,8},{11,9},{12,... | collective-permute-start | bytes 393224 | tf_op jit(solution)/shard_map/ppermute | solution.py:23
  33.6 0.0 collective-permute-done.3.two_ref.refs_11_
  33.7 0.0 collective-permute-done.2.one_ref.refs_10_
  33.7 2.5 %scores.3 = (bf16[128,2048]{1,0:T(8,128)(2,1)S(1)}, bf16[256,2048]{1,0:T(8,128)(2,1)S(1)}, bf16[256,256]{1,0:T(8,128)(2,1)S(1)}, bf16[256,256]{1,0:T(8,128)(2,1)S(1)}) custom-call(bf16[128,4096]{1,0:T(8,128)(2,1)S(1)} %get-tuple-element.26.q_ref.refs_0_, bf16[128,4096]{1,0:T(8,128)(2,1)S(1)} %get-tuple-element.27.g_ref.refs_1_, ...), custom_call_target="tpu_custom_call" | custom-call | flops 805306368 | bytes 3145728 | tf_op jit(solution)/shard_map/scores/pallas_call | solution.py:275
  36.2 4.0 %collective-permute-start.6 = (bf16[256,256]{1,0:T(8,128)(2,1)S(1)}, bf16[256,256]{1,0:T(8,128)(2,1)S(1)}, u32[]{:S(2)}, u32[]{:S(2)}) collective-permute-start(bf16[256,256]{1,0:T(8,128)(2,1)S(1)} %get-tuple-element.44), channel_id=1, source_target_pairs={{1,0},{2,1},{3,2},{4,3},{5,4},{6,5},{7,6},{8,7},{9,8},{10,9},{11,1... | collective-permute-start | bytes 393224 | tf_op jit(solution)/shard_map/ppermute | solution.py:23
  40.2 3.2 %collective-permute-start.7 = (bf16[256,256]{1,0:T(8,128)(2,1)S(1)}, bf16[256,256]{1,0:T(8,128)(2,1)S(1)}, u32[]{:S(2)}, u32[]{:S(2)}) collective-permute-start(bf16[256,256]{1,0:T(8,128)(2,1)S(1)} %get-tuple-element.46), channel_id=1, source_target_pairs={{2,0},{3,1},{4,2},{5,3},{6,4},{7,5},{8,6},{9,7},{10,8},{11,9},{12,... | collective-permute-start | bytes 393224 | tf_op jit(solution)/shard_map/ppermute | solution.py:23
  43.4 0.0 collective-permute-done.4.refs_2_
  43.4 0.0 collective-permute-done.5.refs_4_
  43.5 2.2 %rest.1 = (bf16[128,4096]{1,0:T(8,128)(2,1)}, f32[256,256]{1,0:T(8,128)S(1)}, f32[256,256]{1,0:T(8,128)S(1)}) custom-call(bf16[128,4096]{1,0:T(8,128)(2,1)S(1)} %get-tuple-element.26.q_ref.refs_0_, bf16[128,4096]{1,0:T(8,128)(2,1)S(1)} %get-tuple-element.27.g_ref.refs_1_, bf16[128,2048]{1,0:T(8,128)(2,1)S(1)} %get-tuple-element.30.refs_2_, ...), custom_call_target="tpu_custom_call" | custom-call | flops 805306368 | bytes 6291456 | tf_op jit(solution)/shard_map/rest/pallas_call | solution.py:292
  45.6 0.0 collective-permute-done.6.refs_3_
  45.6 5.3 %collective-permute-done.7.refs_5_ = bf16[256,256]{1,0:T(8,128)(2,1)S(1)} collective-permute-done((bf16[256,256]{1,0:T(8,128)(2,1)S(1)}, bf16[256,256]{1,0:T(8,128)(2,1)S(1)}, u32[]{:S(2)}, u32[]{:S(2)}) %collective-permute-start.7) | collective-permute-done | bytes 131104 | tf_op jit(solution)/shard_map/ppermute | solution.py:23
  51.0 0.8 %final.1 = (bf16[128,512]{1,0:T(8,128)(2,1)}, bf16[128,512]{1,0:T(8,128)(2,1)}) custom-call(f32[256,256]{1,0:T(8,128)S(1)} %get-tuple-element.41.refs_0_, f32[256,256]{1,0:T(8,128)S(1)} %get-tuple-element.42.refs_1_, bf16[256,256]{1,0:T(8,128)(2,1)S(1)} %collective-permute-done.4.refs_2_, bf16[256,256]{1,0:T(8,128)(2,1)S(1)} %collective-permute-done.6.refs_3_, ...), custom_call_target="tpu_custom_call" | custom-call | bytes 1048576 | tf_op jit(solution)/shard_map/final/pallas_call | solution.py:306
Async XLA Ops:
  1.6 21.3 %collective-permute-start.1 = (bf16[272,256]{1,0:T(8,128)(2,1)S(1)}, bf16[272,256]{1,0:T(8,128)(2,1)S(1)}, u32[]{:S(2)}, u32[]{:S(2)}) collective-permute-start(bf16[272,256]{1,0:T(8,128)(2,1)S(1)} %pack.1.own_ref.refs_4_), channel_id=1, source_target_pairs={{0,2},{1,3},{2,4},{3,5},{4,6},{5,7},{6,8},{7,9},{8,10},{9,11},{10,... | collective-permute-start | bytes 417800 | tf_op jit(solution)/shard_map/ppermute | solution.py:23
  6.7 17.7 %collective-permute-start = (bf16[272,256]{1,0:T(8,128)(2,1)S(1)}, bf16[272,256]{1,0:T(8,128)(2,1)S(1)}, u32[]{:S(2)}, u32[]{:S(2)}) collective-permute-start(bf16[272,256]{1,0:T(8,128)(2,1)S(1)} %pack.1.own_ref.refs_4_), channel_id=1, source_target_pairs={{0,1},{1,2},{2,3},{3,4},{4,5},{5,6},{6,7},{7,8},{8,9},{9,10},{10,1... | collective-permute-start | bytes 417800 | tf_op jit(solution)/shard_map/ppermute | solution.py:23
  12.6 21.0 %collective-permute-start.3 = (bf16[256,256]{1,0:T(8,128)(2,1)S(1)}, bf16[256,256]{1,0:T(8,128)(2,1)S(1)}, u32[]{:S(2)}, u32[]{:S(2)}) collective-permute-start(bf16[256,256]{1,0:T(8,128)(2,1)S(1)} %get-tuple-element.32.own_ref.refs_9_), channel_id=1, source_target_pairs={{0,2},{1,3},{2,4},{3,5},{4,6},{5,7},{6,8},{7,9},{8,10},{9,11},{10,... | collective-permute-start | bytes 393224 | tf_op jit(solution)/shard_map/ppermute | solution.py:23
  19.0 14.6 %collective-permute-start.2 = (bf16[256,256]{1,0:T(8,128)(2,1)S(1)}, bf16[256,256]{1,0:T(8,128)(2,1)S(1)}, u32[]{:S(2)}, u32[]{:S(2)}) collective-permute-start(bf16[256,256]{1,0:T(8,128)(2,1)S(1)} %get-tuple-element.32.own_ref.refs_9_), channel_id=1, source_target_pairs={{0,1},{1,2},{2,3},{3,4},{4,5},{5,6},{6,7},{7,8},{8,9},{9,10},{10,1... | collective-permute-start | bytes 393224 | tf_op jit(solution)/shard_map/ppermute | solution.py:23
  27.0 16.4 %collective-permute-start.4 = (bf16[256,256]{1,0:T(8,128)(2,1)S(1)}, bf16[256,256]{1,0:T(8,128)(2,1)S(1)}, u32[]{:S(2)}, u32[]{:S(2)}) collective-permute-start(bf16[256,256]{1,0:T(8,128)(2,1)S(1)} %get-tuple-element.35), channel_id=1, source_target_pairs={{1,0},{2,1},{3,2},{4,3},{5,4},{6,5},{7,6},{8,7},{9,8},{10,9},{11,1... | collective-permute-start | bytes 393224 | tf_op jit(solution)/shard_map/ppermute | solution.py:23
  31.4 12.1 %collective-permute-start.5 = (bf16[256,256]{1,0:T(8,128)(2,1)S(1)}, bf16[256,256]{1,0:T(8,128)(2,1)S(1)}, u32[]{:S(2)}, u32[]{:S(2)}) collective-permute-start(bf16[256,256]{1,0:T(8,128)(2,1)S(1)} %get-tuple-element.36), channel_id=1, source_target_pairs={{2,0},{3,1},{4,2},{5,3},{6,4},{7,5},{8,6},{9,7},{10,8},{11,9},{12,... | collective-permute-start | bytes 393224 | tf_op jit(solution)/shard_map/ppermute | solution.py:23
  36.2 9.4 %collective-permute-start.6 = (bf16[256,256]{1,0:T(8,128)(2,1)S(1)}, bf16[256,256]{1,0:T(8,128)(2,1)S(1)}, u32[]{:S(2)}, u32[]{:S(2)}) collective-permute-start(bf16[256,256]{1,0:T(8,128)(2,1)S(1)} %get-tuple-element.44), channel_id=1, source_target_pairs={{1,0},{2,1},{3,2},{4,3},{5,4},{6,5},{7,6},{8,7},{9,8},{10,9},{11,1... | collective-permute-start | bytes 393224 | tf_op jit(solution)/shard_map/ppermute | solution.py:23
  40.2 10.7 %collective-permute-start.7 = (bf16[256,256]{1,0:T(8,128)(2,1)S(1)}, bf16[256,256]{1,0:T(8,128)(2,1)S(1)}, u32[]{:S(2)}, u32[]{:S(2)}) collective-permute-start(bf16[256,256]{1,0:T(8,128)(2,1)S(1)} %get-tuple-element.46), channel_id=1, source_target_pairs={{2,0},{3,1},{4,2},{5,3},{6,4},{7,5},{8,6},{9,7},{10,8},{11,9},{12,... | collective-permute-start | bytes 393224 | tf_op jit(solution)/shard_map/ppermute | solution.py:23

commit v4 on v3

--- a/solution.py
+++ b/solution.py
@@ -39,41 +39,51 @@
     return jnp.concatenate([key <= query] * copies, axis=1)
 
 
-def segments(payload, tokens):
-    coded = payload[2 * tokens : 2 * tokens + SEG_ROWS, :].astype(jnp.float32)
+def dot_nt(a, b):
+    return lax.dot_general(a, b, (((1,), (1,)), ((), ())), preferred_element_type=jnp.float32)
+
+
+def segments(ref, first, tokens):
+    coded = ref[first : first + SEG_ROWS, :].astype(jnp.float32)
     row = coded[0:1] * 2.0 + coded[1:2]
     return jnp.broadcast_to(row, (tokens, tokens))
 
 
-def half_copies(index, tokens, k_ref, v_ref, out_ref, sems):
-    width = out_ref.shape[1]
-    cols = pl.ds(index * width, width)
+def payload_copies(chunk, tokens, k_ref, v_ref, out_ref, sems):
+    count = HK // CHUNKS
     return [
-        pltpu.make_async_copy(source.at[:, cols], out_ref.at[pl.ds(half * tokens, tokens), :], sems.at[half])
+        pltpu.make_async_copy(
+            source.at[:, pl.ds((chunk * count + part) * HD, HD)],
+            out_ref.at[pl.ds((half * count + part) * tokens, tokens), :],
+            sems.at[half * count + part],
+        )
         for half, source in enumerate((k_ref, v_ref))
+        for part in range(count)
     ]
 
 
-def pack_kernel(tokens, k_ref, v_ref, seg_ref, out_ref, seg_own, sems):
-    ids = pltpu.make_async_copy(seg_ref, seg_own, sems.at[2])
+def pack_kernel(tokens, k_ref, v_ref, seg_ref, out_ref, seg_own, sems, seg_sem):
+    ids = pltpu.make_async_copy(seg_ref, seg_own, seg_sem.at[0])
     ids.start()
-    copies = half_copies(0, tokens, k_ref, v_ref, out_ref, sems)
+    copies = payload_copies(0, tokens, k_ref, v_ref, out_ref, sems)
     for copy in copies:
         copy.start()
     ids.wait()
     seg = jnp.broadcast_to((seg_own[...] + 1)[None, :], (SEG_ROWS, tokens))
     row = lax.broadcasted_iota(jnp.int32, (SEG_ROWS, tokens), 0)
     coded = jnp.where(row == 0, seg >> 1, jnp.where(row == 1, seg & 1, 0))
-    coded = coded.astype(jnp.float32).astype(jnp.bfloat16)
-    repeats = out_ref.shape[1] // tokens
-    out_ref[2 * tokens : 2 * tokens + SEG_ROWS, :] = jnp.concatenate([coded] * repeats, axis=1)
+    first = out_ref.shape[0] - SEG_ROWS
+    out_ref[first : first + SEG_ROWS, :] = coded.astype(jnp.float32).astype(jnp.bfloat16)
     for copy in copies:
         copy.wait()
 
 
-def turn_kernel(q_ref, g_ref, k_ref, v_ref, q_out, g_out, qt_ref, gt_ref, kv_out, sems, kv_sems):
-    width = q_ref.shape[1] // HK
-    halves = half_copies(1, q_ref.shape[0], k_ref, v_ref, kv_out, kv_sems)
+def turn_kernel(group, q_ref, g_ref, k_ref, v_ref, own_ref, q_out, g_out, qt_ref, gt_ref, kv_out, s_own, d_own,
+                sems, kv_sems):
+    tokens = q_ref.shape[0]
+    width = group * HD
+    count = HK // CHUNKS
+    halves = payload_copies(1, tokens, k_ref, v_ref, kv_out, kv_sems)
     copies = []
     for part in range(HK):
         cols = pl.ds(part * width, width)
@@ -81,28 +91,35 @@
             copies.append(pltpu.make_async_copy(source.at[:, cols], target.at[:, cols], sems.at[2 * part + side]))
     for copy in halves + copies:
         copy.start()
-    for part in range(HK):
-        for side, (source, target) in enumerate(((q_out, qt_ref), (g_out, gt_ref))):
-            copies[2 * part + side].wait()
-            for h in range(width // HD):
-                cols = slice(part * width + h * HD, part * width + (h + 1) * HD)
-                target[:, cols] = jnp.transpose(source[:, cols])
     for copy in halves:
         copy.wait()
-
-
-def score_kernel(group, tokens, scale, known, offset, q_ref, g_ref, qt_ref, gt_ref, own_ref, one_ref, two_ref,
-                 *refs):
+    for part in range(HK):
+        payload = (own_ref, kv_out)[part // count]
+        for side, (source, target, product) in enumerate(((q_out, qt_ref, s_own), (g_out, gt_ref, d_own))):
+            copies[2 * part + side].wait()
+            first = (side * count + part % count) * tokens
+            block = payload[first : first + tokens, :]
+            for pair in range(group // 2):
+                cols = slice(part * width + pair * 2 * HD, part * width + (pair + 1) * 2 * HD)
+                turned = jnp.concatenate(
+                    [jnp.transpose(source[:, cols.start + h * HD : cols.start + (h + 1) * HD]) for h in range(2)],
+                    axis=1,
+                )
+                target[:, cols] = turned
+                product[:, cols] = dot(block, turned)
+
+
+def score_kernel(group, tokens, scale, known, offset, qt_ref, gt_ref, s_own, d_own, own_ref, one_ref, two_ref, *refs):
     p_ref, ds_ref, far_ref, near_ref = refs[1:] if known else refs[:-1]
     bias_ref = refs[0] if known else refs[-1]
     if known:
         bias = bias_ref[...]
     else:
-        ids = slice(0, HD)
-        seg_query = segments(own_ref[:, ids], tokens)
+        ids = own_ref.shape[0] - SEG_ROWS
+        seg_query = segments(own_ref, ids, tokens)
         seg_own = jnp.transpose(seg_query)
-        seg_one = jnp.transpose(segments(one_ref[:, ids], tokens))
-        seg_two = jnp.transpose(segments(two_ref[:, ids], tokens))
+        seg_one = jnp.transpose(segments(one_ref, ids, tokens))
+        seg_two = jnp.transpose(segments(two_ref, ids, tokens))
         mixed = jnp.where(sees_own(tokens, 1), seg_own, seg_two)
         bias = jnp.concatenate(
             [jnp.where(mixed == seg_query, 0.0, NEG), jnp.where(seg_one == seg_query, 0.0, NEG)], axis=0
@@ -114,40 +131,40 @@
     far_mask = jnp.where(tri, 0.0, 1.0).astype(jnp.bfloat16)
     factor = scale * LOG2E
     pairs = group // 2
-    count = own_ref.shape[1] // HD
+    count = HK // CHUNKS
+
+    def span(unit):
+        first = offset * group * HD + unit * 2 * HD
+        return slice(first, first + 2 * HD)
 
     def products(unit):
-        part, pair = divmod(unit, pairs)
-        cols = slice(part * HD, (part + 1) * HD)
+        part = unit // pairs
         keys, vals = [
-            jnp.concatenate([ref[rows, cols] for ref in (own_ref, one_ref, two_ref)], axis=0)
-            for rows in (slice(0, tokens), slice(tokens, 2 * tokens))
+            jnp.concatenate([ref[first : first + tokens, :] for ref in (one_ref, two_ref)], axis=0)
+            for first in (part * tokens, (count + part) * tokens)
         ]
-        first = (offset + part) * group + 2 * pair
-        both = slice(first * HD, (first + 2) * HD)
-        return dot(keys, qt_ref[:, both]), dot(vals, gt_ref[:, both])
+        return dot(keys, qt_ref[:, span(unit)]), dot(vals, gt_ref[:, span(unit)])
 
     ahead = products(0)
     for part in range(count):
-        sum_k = jnp.zeros((2 * tokens, HD), jnp.float32)
-        sum_v = jnp.zeros((2 * tokens, HD), jnp.float32)
+        sum_k = jnp.zeros((HD, 2 * tokens), jnp.float32)
+        sum_v = jnp.zeros((HD, 2 * tokens), jnp.float32)
         for pair in range(pairs):
             unit = part * pairs + pair
             raw, dp = ahead
             if unit + 1 < count * pairs:
                 ahead = products(unit + 1)
             cols = slice(unit * 2 * HD, (unit + 1) * 2 * HD)
-            first = (offset + part) * group + 2 * pair
-            s_mix = jnp.where(tri, raw[0:tokens], raw[2 * tokens :]) + bias_mix
-            s_one = raw[tokens : 2 * tokens] + bias_one
+            s_mix = jnp.where(tri, s_own[:, span(unit)], raw[tokens:]) + bias_mix
+            s_one = raw[0:tokens] + bias_one
             top = jnp.max(jnp.maximum(s_mix, s_one), axis=0, keepdims=True)
             e_mix = jnp.exp2((s_mix - top) * factor)
             e_one = jnp.exp2((s_one - top) * factor)
             inverse = 1.0 / jnp.sum(e_mix + e_one, axis=0, keepdims=True)
             p_mix = e_mix * inverse
             p_one = e_one * inverse
-            d_mix = jnp.where(tri, dp[0:tokens], dp[2 * tokens :])
-            d_one = dp[tokens : 2 * tokens]
+            d_mix = jnp.where(tri, d_own[:, span(unit)], dp[tokens:])
+            d_one = dp[0:tokens]
             delta = jnp.sum(p_mix * d_mix + p_one * d_one, axis=0, keepdims=True)
             ds_mix = (p_mix * (d_mix - delta)).astype(jnp.bfloat16)
             ds_one = (p_one * (d_one - delta)).astype(jnp.bfloat16)
@@ -156,13 +173,12 @@
             p_ref[:, cols] = p_mix
             ds_ref[0:tokens, cols] = ds_mix
             ds_ref[tokens : 2 * tokens, cols] = ds_one
-            sum_k = sum_k + dot(jnp.concatenate([ds_one, ds_mix * far_mask], axis=0), stacked(q_ref, first, 2))
-            sum_v = sum_v + dot(jnp.concatenate([p_one, p_mix * far_mask], axis=0), stacked(g_ref, first, 2))
+            sum_k = sum_k + dot_nt(qt_ref[:, span(unit)], jnp.concatenate([ds_one, ds_mix * far_mask], axis=0))
+            sum_v = sum_v + dot_nt(gt_ref[:, span(unit)], jnp.concatenate([p_one, p_mix * far_mask], axis=0))
         cols = slice(part * HD, (part + 1) * HD)
-        near_ref[0:tokens, cols] = (sum_k[0:tokens] * scale).astype(near_ref.dtype)
-        near_ref[tokens : 2 * tokens, cols] = sum_v[0:tokens].astype(near_ref.dtype)
-        far_ref[0:tokens, cols] = (sum_k[tokens:] * scale).astype(far_ref.dtype)
-        far_ref[tokens : 2 * tokens, cols] = sum_v[tokens:].astype(far_ref.dtype)
+        for ref, first in ((near_ref, 0), (far_ref, tokens)):
+            ref[0:tokens, cols] = jnp.transpose(sum_k[:, first : first + tokens] * scale).astype(ref.dtype)
+            ref[tokens : 2 * tokens, cols] = jnp.transpose(sum_v[:, first : first + tokens]).astype(ref.dtype)
 
 
 def rest_kernel(group, tokens, scale, *refs):
@@ -178,12 +194,11 @@
     wide = group * HD
     copies = []
     for chunk, (p_ref, ds_ref, own_ref, one_ref, two_ref) in enumerate(chunk_refs):
-        count = own_ref.shape[1] // HD
+        count = HK // CHUNKS
         for part in range(count):
             inner = slice(part * HD, (part + 1) * HD)
-            keys_t = jnp.concatenate(
-                [jnp.transpose(ref[0:tokens, inner]) for ref in (own_ref, one_ref, two_ref)], axis=1
-            )
+            block = slice(part * tokens, (part + 1) * tokens)
+            keys_t = jnp.concatenate([jnp.transpose(ref[block, :]) for ref in (own_ref, one_ref, two_ref)], axis=1)
             sum_k = jnp.zeros((tokens, HD), jnp.float32)
             sum_v = jnp.zeros((tokens, HD), jnp.float32)
             for pair in range(group // 2):
@@ -241,35 +256,41 @@
 
 
 def pack_call(key_states, value_states, segment_ids):
-    tokens, width = key_states.shape
+    tokens, count = key_states.shape[0], HK // CHUNKS
     return pl.pallas_call(
         functools.partial(pack_kernel, tokens),
         in_specs=[pl.BlockSpec(memory_space=pltpu.HBM)] * 3,
-        out_shape=bf16(2 * tokens + SEG_ROWS, width // CHUNKS),
-        scratch_shapes=[pltpu.VMEM((tokens,), jnp.int32), pltpu.SemaphoreType.DMA((3,))],
-        cost_estimate=cost(0, 4 * tokens * width),
+        out_shape=bf16(2 * count * tokens + SEG_ROWS, HD),
+        scratch_shapes=[
+            pltpu.VMEM((tokens,), jnp.int32),
+            pltpu.SemaphoreType.DMA((2 * count,)),
+            pltpu.SemaphoreType.DMA((1,)),
+        ],
+        cost_estimate=cost(0, 8 * tokens * count * HD),
         compiler_params=PARAMS,
         name="pack",
     )(*in_hbm(key_states, value_states, segment_ids))
 
 
-def turn_call(q, g, key_states, value_states):
+def turn_call(q, g, key_states, value_states, own, group):
     tokens, span = q.shape
-    return pl.pallas_call(
-        turn_kernel,
-        in_specs=[pl.BlockSpec(memory_space=pltpu.HBM)] * 4,
+    count = HK // CHUNKS
+    return pl.pallas_call(
+        functools.partial(turn_kernel, group),
+        in_specs=[pl.BlockSpec(memory_space=pltpu.HBM)] * 4 + [pl.BlockSpec(memory_space=pltpu.VMEM)],
         out_shape=[bf16(tokens, span)] * 2
         + [bf16(HD, span)] * 2
-        + [bf16(2 * tokens, key_states.shape[1] // CHUNKS)],
-        scratch_shapes=[pltpu.SemaphoreType.DMA((2 * HK,)), pltpu.SemaphoreType.DMA((2,))],
-        cost_estimate=cost(0, 16 * tokens * span),
+        + [bf16(2 * count * tokens, HD)]
+        + [f32(tokens, span)] * 2,
+        scratch_shapes=[pltpu.SemaphoreType.DMA((2 * HK,)), pltpu.SemaphoreType.DMA((2 * count,))],
+        cost_estimate=cost(4 * tokens * span * HD, 16 * tokens * span),
         compiler_params=PARAMS,
         name="turn",
-    )(*in_hbm(q, g, key_states, value_states))
-
-
-def score_call(q, g, qt, gt, own, one, two, bias, offset, group, tokens, scale):
-    count = own.shape[1] // HD
+    )(*in_hbm(q, g, key_states, value_states), own)
+
+
+def score_call(qt, gt, s_own, d_own, own, one, two, bias, offset, group, tokens, scale):
+    count = HK // CHUNKS
     span = count * group * HD
     known = bias is not None
     return pl.pallas_call(
@@ -281,14 +302,14 @@
             bf16(2 * tokens, count * HD),
         ]
         + [f32(2 * tokens, tokens)] * (not known),
-        cost_estimate=cost(2 * tokens * 3 * span * tokens * 4, 12 * tokens * span, 2 * tokens * span),
+        cost_estimate=cost(2 * tokens * 2 * span * tokens * 4, 12 * tokens * span, 2 * tokens * span),
         compiler_params=PARAMS,
         name="scores",
-    )(q, g, qt, gt, own, one, two, *([bias] if known else []))
+    )(qt, gt, s_own, d_own, own, one, two, *([bias] if known else []))
 
 
 def rest_call(q, g, parts, group, tokens, scale):
-    count = parts[0][2].shape[1] // HD
+    count = HK // CHUNKS
     return pl.pallas_call(
         functools.partial(rest_kernel, group, tokens, scale),
         out_specs=[pl.BlockSpec(memory_space=pltpu.HBM)] + [pl.BlockSpec(memory_space=pltpu.VMEM)] * CHUNKS,
@@ -319,13 +340,13 @@
     chunks = range(CHUNKS)
     step = HK // CHUNKS
     own = [pack_call(key_states, value_states, segment_ids)]
-    q, g, qt, gt, later = turn_call(queries, out_grad, key_states, value_states)
+    q, g, qt, gt, later, s_own, d_own = turn_call(queries, out_grad, key_states, value_states, own[0], group)
     own.append(later)
+    one = [shift(x, 1) for x in own]
     two = [shift(x, 2) for x in own]
-    one = [shift(x, 1) for x in own]
     first, near, far, bias = [], [], [], None
     for c in chunks:
-        results = score_call(q, g, qt, gt, own[c], one[c], two[c], bias, c * step, group, tokens, scale)
+        results = score_call(qt, gt, s_own, d_own, own[c], one[c], two[c], bias, c * step, group, tokens, scale)
         bias = results[4] if bias is None else bias
         first.append(results)
         far.append(shift(results[2], -2))

time: 52.4 us -> 52.4 us (level)
  the two profiles are of different devices: /device:TPU:4 before, /device:TPU:1 now
where the time goes in v4:
time: 52.4 us; the launch traced here: 52.1 us
  starting transfers between devices  35.9 us (69%)
  Pallas kernels  12.6 us (24%)
  waiting for transfers between devices  2.75 us (5%)
  between operations  0.79 us (2%)
    ppermute x8, starting transfers between devices, shift(): lax.ppermute(value, AXES, [(i, i + steps) for i in range(first, last)])  35.9 us
    pallas_call x2, Pallas kernels, score_call(): pl.pallas_call(functools.partial(score_kernel, group, tokens, scale, know...  5 us
    pallas_call x1, Pallas kernels, turn_call(): pl.pallas_call(functools.partial(turn_kernel, group), in_specs=[pl.BlockS...  3.79 us
    ppermute x8, waiting for transfers between devices, shift(): lax.ppermute(value, AXES, [(i, i + steps) for i in range(first, last)])  2.75 us
    pallas_call x1, Pallas kernels, rest_call(): pl.pallas_call(functools.partial(rest_kernel, group, tokens, scale), out_...  2.19 us
  transfers between devices with their start and end apart: 8, of which 1 were waited for; matrix products, arithmetic and copies ran while one was open for 0% of the time, Pallas kernels for 21%

profile of v4, /device:TPU:1, one launch (start us, length us, event | category | flops | bytes accessed | tf_op | source)
XLA Modules:
  0.0 52.1 jit_solution(1409119380254748077)
XLA Ops:
  0.6 0.9 %pack.1.own_ref.refs_4_ = bf16[528,128]{1,0:T(8,128)(2,1)S(1)} custom-call(bf16[128,512]{1,0:T(8,128)(2,1)} %k_ref.3, bf16[128,512]{1,0:T(8,128)(2,1)} %v_ref.3, s32[128]{0:T(128)} %seg_ref.1), custom_call_target="tpu_custom_call" | custom-call | bytes 262144 | tf_op jit(solution)/shard_map/pack/pallas_call | solution.py:260
  1.5 5.7 %collective-permute-start.1 = (bf16[528,128]{1,0:T(8,128)(2,1)S(1)}, bf16[528,128]{1,0:T(8,128)(2,1)S(1)}, u32[]{:S(2)}, u32[]{:S(2)}) collective-permute-start(bf16[528,128]{1,0:T(8,128)(2,1)S(1)} %pack.1.own_ref.refs_4_), channel_id=1, source_target_pairs={{0,2},{1,3},{2,4},{3,5},{4,6},{5,7},{6,8},{7,9},{8,10},{9,11},{10,... | collective-permute-start | bytes 405512 | tf_op jit(solution)/shard_map/ppermute | solution.py:23
  7.2 3.5 %collective-permute-start = (bf16[528,128]{1,0:T(8,128)(2,1)S(1)}, bf16[528,128]{1,0:T(8,128)(2,1)S(1)}, u32[]{:S(2)}, u32[]{:S(2)}) collective-permute-start(bf16[528,128]{1,0:T(8,128)(2,1)S(1)} %pack.1.own_ref.refs_4_), channel_id=1, source_target_pairs={{0,1},{1,2},{2,3},{3,4},{4,5},{5,6},{6,7},{7,8},{8,9},{9,10},{10,1... | collective-permute-start | bytes 405512 | tf_op jit(solution)/shard_map/ppermute | solution.py:23
  10.8 3.8 %turn.1 = (bf16[128,4096]{1,0:T(8,128)(2,1)S(1)}, bf16[128,4096]{1,0:T(8,128)(2,1)S(1)}, bf16[128,4096]{1,0:T(8,128)(2,1)S(1)}, bf16[128,4096]{1,0:T(8,128)(2,1)...) custom-call(bf16[128,4096]{1,0:T(8,128)(2,1)} %q_ref.1, ...), custom_call_target="tpu_custom_call" | custom-call | flops 268435456 | bytes 8388608 | tf_op jit(solution)/shard_map/turn/pallas_call | solution.py:278
  14.6 6.1 %collective-permute-start.3 = (bf16[512,128]{1,0:T(8,128)(2,1)S(1)}, bf16[512,128]{1,0:T(8,128)(2,1)S(1)}, u32[]{:S(2)}, u32[]{:S(2)}) collective-permute-start(bf16[512,128]{1,0:T(8,128)(2,1)S(1)} %get-tuple-element.36.own_ref.refs_9_), channel_id=1, source_target_pairs={{0,2},{1,3},{2,4},{3,5},{4,6},{5,7},{6,8},{7,9},{8,10},{9,11},{10,... | collective-permute-start | bytes 393224 | tf_op jit(solution)/shard_map/ppermute | solution.py:23
  20.7 3.6 %collective-permute-start.2 = (bf16[512,128]{1,0:T(8,128)(2,1)S(1)}, bf16[512,128]{1,0:T(8,128)(2,1)S(1)}, u32[]{:S(2)}, u32[]{:S(2)}) collective-permute-start(bf16[512,128]{1,0:T(8,128)(2,1)S(1)} %get-tuple-element.36.own_ref.refs_9_), channel_id=1, source_target_pairs={{0,1},{1,2},{2,3},{3,4},{4,5},{5,6},{6,7},{7,8},{8,9},{9,10},{10,1... | collective-permute-start | bytes 393224 | tf_op jit(solution)/shard_map/ppermute | solution.py:23
  24.3 0.0 collective-permute-done.1.two_ref.refs_6_
  24.3 0.0 collective-permute-done.one_ref.refs_5_
  24.3 2.5 %scores.2 = (bf16[128,2048]{1,0:T(8,128)(2,1)S(1)}, bf16[256,2048]{1,0:T(8,128)(2,1)S(1)}, bf16[256,256]{1,0:T(8,128)(2,1)S(1)}, bf16[256,256]{1,0:T(8,128)(2,1)S(1)}, f32[256,128]{1,0:T(8,128)S(1)}) custom-call(bf16[128,4096]{1,0:T(8,128)(2,1)S(1)} %get-tuple-element.30.qt_ref, bf16[128,4096]{1,0:T(8,128)(2,1)S(1)} %get-tuple-element.31.gt_ref, ...), custom_call_target="tpu_custom_call" | custom-call | flops 536870912 | bytes 3145728 | tf_op jit(solution)/shard_map/scores/pallas_call | solution.py:296
  26.8 4.1 %collective-permute-start.4 = (bf16[256,256]{1,0:T(8,128)(2,1)S(1)}, bf16[256,256]{1,0:T(8,128)(2,1)S(1)}, u32[]{:S(2)}, u32[]{:S(2)}) collective-permute-start(bf16[256,256]{1,0:T(8,128)(2,1)S(1)} %get-tuple-element.39), channel_id=1, source_target_pairs={{1,0},{2,1},{3,2},{4,3},{5,4},{6,5},{7,6},{8,7},{9,8},{10,9},{11,1... | collective-permute-start | bytes 393224 | tf_op jit(solution)/shard_map/ppermute | solution.py:23
  30.9 3.7 %collective-permute-start.5 = (bf16[256,256]{1,0:T(8,128)(2,1)S(1)}, bf16[256,256]{1,0:T(8,128)(2,1)S(1)}, u32[]{:S(2)}, u32[]{:S(2)}) collective-permute-start(bf16[256,256]{1,0:T(8,128)(2,1)S(1)} %get-tuple-element.40), channel_id=1, source_target_pairs={{2,0},{3,1},{4,2},{5,3},{6,4},{7,5},{8,6},{9,7},{10,8},{11,9},{12,... | collective-permute-start | bytes 393224 | tf_op jit(solution)/shard_map/ppermute | solution.py:23
  34.6 0.0 collective-permute-done.3.two_ref.refs_11_
  34.6 0.0 collective-permute-done.2.one_ref.refs_10_
  34.7 2.5 %scores.3 = (bf16[128,2048]{1,0:T(8,128)(2,1)S(1)}, bf16[256,2048]{1,0:T(8,128)(2,1)S(1)}, bf16[256,256]{1,0:T(8,128)(2,1)S(1)}, bf16[256,256]{1,0:T(8,128)(2,1)S(1)}) custom-call(bf16[128,4096]{1,0:T(8,128)(2,1)S(1)} %get-tuple-element.30.qt_ref, bf16[128,4096]{1,0:T(8,128)(2,1)S(1)} %get-tuple-element.31.gt_ref, f32[128,4096]{1,0:T(8,128)S(1)} %get-tuple-element.32.s_own, ...), custom_call_target="tpu_custom_call" | custom-call | flops 536870912 | bytes 3145728 | tf_op jit(solution)/shard_map/scores/pallas_call | solution.py:296
  37.2 3.8 %collective-permute-start.6 = (bf16[256,256]{1,0:T(8,128)(2,1)S(1)}, bf16[256,256]{1,0:T(8,128)(2,1)S(1)}, u32[]{:S(2)}, u32[]{:S(2)}) collective-permute-start(bf16[256,256]{1,0:T(8,128)(2,1)S(1)} %get-tuple-element.48), channel_id=1, source_target_pairs={{1,0},{2,1},{3,2},{4,3},{5,4},{6,5},{7,6},{8,7},{9,8},{10,9},{11,1... | collective-permute-start | bytes 393224 | tf_op jit(solution)/shard_map/ppermute | solution.py:23
  41.0 5.4 %collective-permute-start.7 = (bf16[256,256]{1,0:T(8,128)(2,1)S(1)}, bf16[256,256]{1,0:T(8,128)(2,1)S(1)}, u32[]{:S(2)}, u32[]{:S(2)}) collective-permute-start(bf16[256,256]{1,0:T(8,128)(2,1)S(1)} %get-tuple-element.50), channel_id=1, source_target_pairs={{2,0},{3,1},{4,2},{5,3},{6,4},{7,5},{8,6},{9,7},{10,8},{11,9},{12,... | collective-permute-start | bytes 393224 | tf_op jit(solution)/shard_map/ppermute | solution.py:23
  46.3 0.0 collective-permute-done.4.refs_2_
  46.3 0.0 collective-permute-done.5.refs_4_
  46.4 2.2 %rest.1 = (bf16[128,4096]{1,0:T(8,128)(2,1)}, f32[256,256]{1,0:T(8,128)S(1)}, f32[256,256]{1,0:T(8,128)S(1)}) custom-call(bf16[128,4096]{1,0:T(8,128)(2,1)S(1)} %get-tuple-element.28.refs_0_, bf16[128,4096]{1,0:T(8,128)(2,1)S(1)} %get-tuple-element.29.refs_1_, bf16[128,2048]{1,0:T(8,128)(2,1)S(1)} %get-tuple-element.34.refs_2_, ...), custom_call_target="tpu_custom_call" | custom-call | flops 805306368 | bytes 6291456 | tf_op jit(solution)/shard_map/rest/pallas_call | solution.py:313
  48.6 0.0 collective-permute-done.6.refs_3_
  48.6 2.7 %collective-permute-done.7.refs_5_ = bf16[256,256]{1,0:T(8,128)(2,1)S(1)} collective-permute-done((bf16[256,256]{1,0:T(8,128)(2,1)S(1)}, bf16[256,256]{1,0:T(8,128)(2,1)S(1)}, u32[]{:S(2)}, u32[]{:S(2)}) %collective-permute-start.7) | collective-permute-done | bytes 131104 | tf_op jit(solution)/shard_map/ppermute | solution.py:23
  51.3 0.8 %final.1 = (bf16[128,512]{1,0:T(8,128)(2,1)}, bf16[128,512]{1,0:T(8,128)(2,1)}) custom-call(f32[256,256]{1,0:T(8,128)S(1)} %get-tuple-element.45.refs_0_, f32[256,256]{1,0:T(8,128)S(1)} %get-tuple-element.46.refs_1_, bf16[256,256]{1,0:T(8,128)(2,1)S(1)} %collective-permute-done.4.refs_2_, bf16[256,256]{1,0:T(8,128)(2,1)S(1)} %collective-permute-done.6.refs_3_, ...), custom_call_target="tpu_custom_call" | custom-call | bytes 1048576 | tf_op jit(solution)/shard_map/final/pallas_call | solution.py:327
Async XLA Ops:
  1.5 22.8 %collective-permute-start.1 = (bf16[528,128]{1,0:T(8,128)(2,1)S(1)}, bf16[528,128]{1,0:T(8,128)(2,1)S(1)}, u32[]{:S(2)}, u32[]{:S(2)}) collective-permute-start(bf16[528,128]{1,0:T(8,128)(2,1)S(1)} %pack.1.own_ref.refs_4_), channel_id=1, source_target_pairs={{0,2},{1,3},{2,4},{3,5},{4,6},{5,7},{6,8},{7,9},{8,10},{9,11},{10,... | collective-permute-start | bytes 405512 | tf_op jit(solution)/shard_map/ppermute | solution.py:23
  7.2 17.0 %collective-permute-start = (bf16[528,128]{1,0:T(8,128)(2,1)S(1)}, bf16[528,128]{1,0:T(8,128)(2,1)S(1)}, u32[]{:S(2)}, u32[]{:S(2)}) collective-permute-start(bf16[528,128]{1,0:T(8,128)(2,1)S(1)} %pack.1.own_ref.refs_4_), channel_id=1, source_target_pairs={{0,1},{1,2},{2,3},{3,4},{4,5},{5,6},{6,7},{7,8},{8,9},{9,10},{10,1... | collective-permute-start | bytes 405512 | tf_op jit(solution)/shard_map/ppermute | solution.py:23
  14.6 20.0 %collective-permute-start.3 = (bf16[512,128]{1,0:T(8,128)(2,1)S(1)}, bf16[512,128]{1,0:T(8,128)(2,1)S(1)}, u32[]{:S(2)}, u32[]{:S(2)}) collective-permute-start(bf16[512,128]{1,0:T(8,128)(2,1)S(1)} %get-tuple-element.36.own_ref.refs_9_), channel_id=1, source_target_pairs={{0,2},{1,3},{2,4},{3,5},{4,6},{5,7},{6,8},{7,9},{8,10},{9,11},{10,... | collective-permute-start | bytes 393224 | tf_op jit(solution)/shard_map/ppermute | solution.py:23
  20.7 13.9 %collective-permute-start.2 = (bf16[512,128]{1,0:T(8,128)(2,1)S(1)}, bf16[512,128]{1,0:T(8,128)(2,1)S(1)}, u32[]{:S(2)}, u32[]{:S(2)}) collective-permute-start(bf16[512,128]{1,0:T(8,128)(2,1)S(1)} %get-tuple-element.36.own_ref.refs_9_), channel_id=1, source_target_pairs={{0,1},{1,2},{2,3},{3,4},{4,5},{5,6},{6,7},{7,8},{8,9},{9,10},{10,1... | collective-permute-start | bytes 393224 | tf_op jit(solution)/shard_map/ppermute | solution.py:23
  26.8 19.5 %collective-permute-start.4 = (bf16[256,256]{1,0:T(8,128)(2,1)S(1)}, bf16[256,256]{1,0:T(8,128)(2,1)S(1)}, u32[]{:S(2)}, u32[]{:S(2)}) collective-permute-start(bf16[256,256]{1,0:T(8,128)(2,1)S(1)} %get-tuple-element.39), channel_id=1, source_target_pairs={{1,0},{2,1},{3,2},{4,3},{5,4},{6,5},{7,6},{8,7},{9,8},{10,9},{11,1... | collective-permute-start | bytes 393224 | tf_op jit(solution)/shard_map/ppermute | solution.py:23
  30.9 15.4 %collective-permute-start.5 = (bf16[256,256]{1,0:T(8,128)(2,1)S(1)}, bf16[256,256]{1,0:T(8,128)(2,1)S(1)}, u32[]{:S(2)}, u32[]{:S(2)}) collective-permute-start(bf16[256,256]{1,0:T(8,128)(2,1)S(1)} %get-tuple-element.40), channel_id=1, source_target_pairs={{2,0},{3,1},{4,2},{5,3},{6,4},{7,5},{8,6},{9,7},{10,8},{11,9},{12,... | collective-permute-start | bytes 393224 | tf_op jit(solution)/shard_map/ppermute | solution.py:23
  37.2 11.4 %collective-permute-start.6 = (bf16[256,256]{1,0:T(8,128)(2,1)S(1)}, bf16[256,256]{1,0:T(8,128)(2,1)S(1)}, u32[]{:S(2)}, u32[]{:S(2)}) collective-permute-start(bf16[256,256]{1,0:T(8,128)(2,1)S(1)} %get-tuple-element.48), channel_id=1, source_target_pairs={{1,0},{2,1},{3,2},{4,3},{5,4},{6,5},{7,6},{8,7},{9,8},{10,9},{11,1... | collective-permute-start | bytes 393224 | tf_op jit(solution)/shard_map/ppermute | solution.py:23
  41.0 10.3 %collective-permute-start.7 = (bf16[256,256]{1,0:T(8,128)(2,1)S(1)}, bf16[256,256]{1,0:T(8,128)(2,1)S(1)}, u32[]{:S(2)}, u32[]{:S(2)}) collective-permute-start(bf16[256,256]{1,0:T(8,128)(2,1)S(1)} %get-tuple-element.50), channel_id=1, source_target_pairs={{2,0},{3,1},{4,2},{5,3},{6,4},{7,5},{8,6},{9,7},{10,8},{11,9},{12,... | collective-permute-start | bytes 393224 | tf_op jit(solution)/shard_map/ppermute | solution.py:23

commit v5 on v4

--- a/solution.py
+++ b/solution.py
@@ -37,10 +37,6 @@
     key = lax.broadcasted_iota(jnp.int32, (tokens, tokens), 0)
     query = lax.broadcasted_iota(jnp.int32, (tokens, tokens), 1)
     return jnp.concatenate([key <= query] * copies, axis=1)
-
-
-def dot_nt(a, b):
-    return lax.dot_general(a, b, (((1,), (1,)), ((), ())), preferred_element_type=jnp.float32)
 
 
 def segments(ref, first, tokens):
@@ -78,12 +74,9 @@
         copy.wait()
 
 
-def turn_kernel(group, q_ref, g_ref, k_ref, v_ref, own_ref, q_out, g_out, qt_ref, gt_ref, kv_out, s_own, d_own,
-                sems, kv_sems):
-    tokens = q_ref.shape[0]
+def turn_kernel(group, q_ref, g_ref, k_ref, v_ref, q_out, g_out, qt_ref, gt_ref, kv_out, sems, kv_sems):
     width = group * HD
-    count = HK // CHUNKS
-    halves = payload_copies(1, tokens, k_ref, v_ref, kv_out, kv_sems)
+    halves = payload_copies(1, q_ref.shape[0], k_ref, v_ref, kv_out, kv_sems)
     copies = []
     for part in range(HK):
         cols = pl.ds(part * width, width)
@@ -91,94 +84,88 @@
             copies.append(pltpu.make_async_copy(source.at[:, cols], target.at[:, cols], sems.at[2 * part + side]))
     for copy in halves + copies:
         copy.start()
+    for part in range(HK):
+        for side, (source, target) in enumerate(((q_out, qt_ref), (g_out, gt_ref))):
+            copies[2 * part + side].wait()
+            for h in range(group):
+                cols = slice(part * width + h * HD, part * width + (h + 1) * HD)
+                target[:, cols] = jnp.transpose(source[:, cols])
     for copy in halves:
         copy.wait()
-    for part in range(HK):
-        payload = (own_ref, kv_out)[part // count]
-        for side, (source, target, product) in enumerate(((q_out, qt_ref, s_own), (g_out, gt_ref, d_own))):
-            copies[2 * part + side].wait()
-            first = (side * count + part % count) * tokens
-            block = payload[first : first + tokens, :]
-            for pair in range(group // 2):
-                cols = slice(part * width + pair * 2 * HD, part * width + (pair + 1) * 2 * HD)
-                turned = jnp.concatenate(
-                    [jnp.transpose(source[:, cols.start + h * HD : cols.start + (h + 1) * HD]) for h in range(2)],
-                    axis=1,
-                )
-                target[:, cols] = turned
-                product[:, cols] = dot(block, turned)
-
-
-def score_kernel(group, tokens, scale, known, offset, qt_ref, gt_ref, s_own, d_own, own_ref, one_ref, two_ref, *refs):
+
+
+def score_kernel(group, tokens, scale, known, offset, q_ref, g_ref, qt_ref, gt_ref, own_ref, one_ref, two_ref, *refs):
     p_ref, ds_ref, far_ref, near_ref = refs[1:] if known else refs[:-1]
     bias_ref = refs[0] if known else refs[-1]
-    if known:
-        bias = bias_ref[...]
-    else:
+    tri = sees_own(tokens, 1)
+    if not known:
         ids = own_ref.shape[0] - SEG_ROWS
         seg_query = segments(own_ref, ids, tokens)
         seg_own = jnp.transpose(seg_query)
         seg_one = jnp.transpose(segments(one_ref, ids, tokens))
         seg_two = jnp.transpose(segments(two_ref, ids, tokens))
-        mixed = jnp.where(sees_own(tokens, 1), seg_own, seg_two)
-        bias = jnp.concatenate(
-            [jnp.where(mixed == seg_query, 0.0, NEG), jnp.where(seg_one == seg_query, 0.0, NEG)], axis=0
-        )
-        bias_ref[...] = bias
-    bias_mix = jnp.concatenate([bias[0:tokens]] * 2, axis=1)
-    bias_one = jnp.concatenate([bias[tokens:]] * 2, axis=1)
-    tri = sees_own(tokens, 2)
+        mixed = jnp.where(tri, seg_own, seg_two)
+        bias_ref[0:tokens, :] = jnp.where(mixed == seg_query, 0.0, NEG)
+        bias_ref[tokens : 2 * tokens, :] = jnp.where(seg_one == seg_query, 0.0, NEG)
     far_mask = jnp.where(tri, 0.0, 1.0).astype(jnp.bfloat16)
     factor = scale * LOG2E
     pairs = group // 2
     count = HK // CHUNKS
 
-    def span(unit):
-        first = offset * group * HD + unit * 2 * HD
-        return slice(first, first + 2 * HD)
-
     def products(unit):
         part = unit // pairs
         keys, vals = [
-            jnp.concatenate([ref[first : first + tokens, :] for ref in (one_ref, two_ref)], axis=0)
+            jnp.concatenate([ref[first : first + tokens, :] for ref in (own_ref, one_ref, two_ref)], axis=0)
             for first in (part * tokens, (count + part) * tokens)
         ]
-        return dot(keys, qt_ref[:, span(unit)]), dot(vals, gt_ref[:, span(unit)])
+        first = (offset * group + 2 * unit) * HD
+        both = slice(first, first + 2 * HD)
+        return dot(keys, qt_ref[:, both]), dot(vals, gt_ref[:, both])
+
+    def head(raw, dp, cols):
+        s_mix = jnp.where(tri, raw[0:tokens], raw[2 * tokens :]) + bias_ref[0:tokens, :]
+        s_one = raw[tokens : 2 * tokens] + bias_ref[tokens : 2 * tokens, :]
+        top = jnp.max(jnp.maximum(s_mix, s_one), axis=0, keepdims=True)
+        e_mix = jnp.exp2((s_mix - top) * factor)
+        e_one = jnp.exp2((s_one - top) * factor)
+        inverse = 1.0 / jnp.sum(e_mix + e_one, axis=0, keepdims=True)
+        p_mix = e_mix * inverse
+        p_one = e_one * inverse
+        d_mix = jnp.where(tri, dp[0:tokens], dp[2 * tokens :])
+        d_one = dp[tokens : 2 * tokens]
+        delta = jnp.sum(p_mix * d_mix + p_one * d_one, axis=0, keepdims=True)
+        ds_mix = (p_mix * (d_mix - delta)).astype(jnp.bfloat16)
+        ds_one = (p_one * (d_one - delta)).astype(jnp.bfloat16)
+        p_mix = p_mix.astype(jnp.bfloat16)
+        p_one = p_one.astype(jnp.bfloat16)
+        p_ref[:, cols] = p_mix
+        ds_ref[0:tokens, cols] = ds_mix
+        ds_ref[tokens : 2 * tokens, cols] = ds_one
+        return (
+            jnp.concatenate([p_one, p_mix * far_mask], axis=0),
+            jnp.concatenate([ds_one, ds_mix * far_mask], axis=0),
+        )
 
     ahead = products(0)
     for part in range(count):
-        sum_k = jnp.zeros((HD, 2 * tokens), jnp.float32)
-        sum_v = jnp.zeros((HD, 2 * tokens), jnp.float32)
+        probs, grads = [], []
         for pair in range(pairs):
             unit = part * pairs + pair
             raw, dp = ahead
             if unit + 1 < count * pairs:
                 ahead = products(unit + 1)
-            cols = slice(unit * 2 * HD, (unit + 1) * 2 * HD)
-            s_mix = jnp.where(tri, s_own[:, span(unit)], raw[tokens:]) + bias_mix
-            s_one = raw[0:tokens] + bias_one
-            top = jnp.max(jnp.maximum(s_mix, s_one), axis=0, keepdims=True)
-            e_mix = jnp.exp2((s_mix - top) * factor)
-            e_one = jnp.exp2((s_one - top) * factor)
-            inverse = 1.0 / jnp.sum(e_mix + e_one, axis=0, keepdims=True)
-            p_mix = e_mix * inverse
-            p_one = e_one * inverse
-            d_mix = jnp.where(tri, d_own[:, span(unit)], dp[tokens:])
-            d_one = dp[0:tokens]
-            delta = jnp.sum(p_mix * d_mix + p_one * d_one, axis=0, keepdims=True)
-            ds_mix = (p_mix * (d_mix - delta)).astype(jnp.bfloat16)
-            ds_one = (p_one * (d_one - delta)).astype(jnp.bfloat16)
-            p_mix = p_mix.astype(jnp.bfloat16)
-            p_one = p_one.astype(jnp.bfloat16)
-            p_ref[:, cols] = p_mix
-            ds_ref[0:tokens, cols] = ds_mix
-            ds_ref[tokens : 2 * tokens, cols] = ds_one
-            sum_k = sum_k + dot_nt(qt_ref[:, span(unit)], jnp.concatenate([ds_one, ds_mix * far_mask], axis=0))
-            sum_v = sum_v + dot_nt(gt_ref[:, span(unit)], jnp.concatenate([p_one, p_mix * far_mask], axis=0))
+            for h in range(2):
+                inner = slice(h * HD, (h + 1) * HD)
+                p, ds = head(raw[:, inner], dp[:, inner], slice((2 * unit + h) * HD, (2 * unit + h + 1) * HD))
+                probs.append(p)
+                grads.append(ds)
+        first = (offset + part) * group
+        sum_k = dot(jnp.concatenate(grads, axis=1), stacked(q_ref, first, group)) * scale
+        sum_v = dot(jnp.concatenate(probs, axis=1), stacked(g_ref, first, group))
         cols = slice(part * HD, (part + 1) * HD)
-        for ref, first in ((near_ref, 0), (far_ref, tokens)):
-            ref[0:tokens, cols] = jnp.transpose(sum_k[:, first : first + tokens] * scale).astype(ref.dtype)
-            ref[tokens : 2 * tokens, cols] = jnp.transpose(sum_v[:, first : first + tokens]).astype(ref.dtype)
+        for ref, row in ((near_ref, 0), (far_ref, tokens)):
+            ref[0:tokens, cols] = sum_k[row : row + tokens].astype(ref.dtype)
+            ref[tokens : 2 * tokens, cols] = sum_v[row : row + tokens].astype(ref.dtype)
 
 
 def rest_kernel(group, tokens, scale, *refs):
@@ -272,24 +259,21 @@
     )(*in_hbm(key_states, value_states, segment_ids))
 
 
-def turn_call(q, g, key_states, value_states, own, group):
+def turn_call(q, g, key_states, value_states, group):
     tokens, span = q.shape
     count = HK // CHUNKS
     return pl.pallas_call(
         functools.partial(turn_kernel, group),
-        in_specs=[pl.BlockSpec(memory_space=pltpu.HBM)] * 4 + [pl.BlockSpec(memory_space=pltpu.VMEM)],
-        out_shape=[bf16(tokens, span)] * 2
-        + [bf16(HD, span)] * 2
-        + [bf16(2 * count * tokens, HD)]
-        + [f32(tokens, span)] * 2,
+        in_specs=[pl.BlockSpec(memory_space=pltpu.HBM)] * 4,
+        out_shape=[bf16(tokens, span)] * 2 + [bf16(HD, span)] * 2 + [bf16(2 * count * tokens, HD)],
         scratch_shapes=[pltpu.SemaphoreType.DMA((2 * HK,)), pltpu.SemaphoreType.DMA((2 * count,))],
-        cost_estimate=cost(4 * tokens * span * HD, 16 * tokens * span),
+        cost_estimate=cost(0, 16 * tokens * span),
         compiler_params=PARAMS,
         name="turn",
-    )(*in_hbm(q, g, key_states, value_states), own)
-
-
-def score_call(qt, gt, s_own, d_own, own, one, two, bias, offset, group, tokens, scale):
+    )(*in_hbm(q, g, key_states, value_states))
+
+
+def score_call(q, g, qt, gt, own, one, two, bias, offset, group, tokens, scale):
     count = HK // CHUNKS
     span = count * group * HD
     known = bias is not None
@@ -302,10 +286,10 @@
             bf16(2 * tokens, count * HD),
         ]
         + [f32(2 * tokens, tokens)] * (not known),
-        cost_estimate=cost(2 * tokens * 2 * span * tokens * 4, 12 * tokens * span, 2 * tokens * span),
+        cost_estimate=cost(2 * tokens * 3 * span * tokens * 4, 12 * tokens * span, 2 * tokens * span),
         compiler_params=PARAMS,
         name="scores",
-    )(qt, gt, s_own, d_own, own, one, two, *([bias] if known else []))
+    )(q, g, qt, gt, own, one, two, *([bias] if known else []))
 
 
 def rest_call(q, g, parts, group, tokens, scale):
@@ -340,13 +324,13 @@
     chunks = range(CHUNKS)
     step = HK // CHUNKS
     own = [pack_call(key_states, value_states, segment_ids)]
-    q, g, qt, gt, later, s_own, d_own = turn_call(queries, out_grad, key_states, value_states, own[0], group)
+    q, g, qt, gt, later = turn_call(queries, out_grad, key_states, value_states, group)
     own.append(later)
     one = [shift(x, 1) for x in own]
     two = [shift(x, 2) for x in own]
     first, near, far, bias = [], [], [], None
     for c in chunks:
-        results = score_call(qt, gt, s_own, d_own, own[c], one[c], two[c], bias, c * step, group, tokens, scale)
+        results = score_call(q, g, qt, gt, own[c], one[c], two[c], bias, c * step, group, tokens, scale)
         bias = results[4] if bias is None else bias
         first.append(results)
         far.append(shift(results[2], -2))

time: 52.4 us -> 52.9 us (level)
  the two profiles are of different devices: /device:TPU:1 before, /device:TPU:4 now
where the time goes in v5:
time: 52.9 us; the launch traced here: 52.3 us
  starting transfers between devices  33 us (62%)
  Pallas kernels  11.3 us (21%)
  waiting for transfers between devices  7.17 us (14%)
  between operations  0.77 us (1%)
    ppermute x8, starting transfers between devices, shift(): lax.ppermute(value, AXES, [(i, i + steps) for i in range(first, last)])  33 us
    ppermute x8, waiting for transfers between devices, shift(): lax.ppermute(value, AXES, [(i, i + steps) for i in range(first, last)])  7.17 us
    pallas_call x2, Pallas kernels, score_call(): pl.pallas_call(functools.partial(score_kernel, group, tokens, scale, know...  5.37 us
    pallas_call x1, Pallas kernels, rest_call(): pl.pallas_call(functools.partial(rest_kernel, group, tokens, scale), out_...  2.2 us
    pallas_call x1, Pallas kernels, turn_call(): pl.pallas_call(functools.partial(turn_kernel, group), in_specs=[pl.BlockS...  2.07 us
  transfers between devices with their start and end apart: 8, of which 2 were waited for; matrix products, arithmetic and copies ran while one was open for 0% of the time, Pallas kernels for 18%

profile of v5, /device:TPU:4, one launch (start us, length us, event | category | flops | bytes accessed | tf_op | source)
XLA Modules:
  0.0 52.3 jit_solution(18398553226277728879)
XLA Ops:
  0.6 0.9 %pack.1.own_ref.refs_4_ = bf16[528,128]{1,0:T(8,128)(2,1)S(1)} custom-call(bf16[128,512]{1,0:T(8,128)(2,1)} %k_ref.3, bf16[128,512]{1,0:T(8,128)(2,1)} %v_ref.3, s32[128]{0:T(128)} %seg_ref.1), custom_call_target="tpu_custom_call" | custom-call | bytes 262144 | tf_op jit(solution)/shard_map/pack/pallas_call | solution.py:247
  1.5 5.2 %collective-permute-start.1 = (bf16[528,128]{1,0:T(8,128)(2,1)S(1)}, bf16[528,128]{1,0:T(8,128)(2,1)S(1)}, u32[]{:S(2)}, u32[]{:S(2)}) collective-permute-start(bf16[528,128]{1,0:T(8,128)(2,1)S(1)} %pack.1.own_ref.refs_4_), channel_id=1, source_target_pairs={{0,2},{1,3},{2,4},{3,5},{4,6},{5,7},{6,8},{7,9},{8,10},{9,11},{10,... | collective-permute-start | bytes 405512 | tf_op jit(solution)/shard_map/ppermute | solution.py:23
  6.7 3.8 %collective-permute-start = (bf16[528,128]{1,0:T(8,128)(2,1)S(1)}, bf16[528,128]{1,0:T(8,128)(2,1)S(1)}, u32[]{:S(2)}, u32[]{:S(2)}) collective-permute-start(bf16[528,128]{1,0:T(8,128)(2,1)S(1)} %pack.1.own_ref.refs_4_), channel_id=1, source_target_pairs={{0,1},{1,2},{2,3},{3,4},{4,5},{5,6},{6,7},{7,8},{8,9},{9,10},{10,1... | collective-permute-start | bytes 405512 | tf_op jit(solution)/shard_map/ppermute | solution.py:23
  10.5 2.1 %turn.1 = (bf16[128,4096]{1,0:T(8,128)(2,1)S(1)}, bf16[128,4096]{1,0:T(8,128)(2,1)S(1)}, bf16[128,4096]{1,0:T(8,128)(2,1)S(1)}, bf16[128,4096]{1,0:T(8,128)(2,1)S(1)}, bf16[512,128]{1,0:T(8,128)(2,1)S(1)}) custom-call(bf16[128,4096]{1,0:T(8,128)(2,1)} %q_ref.1, bf16[128,4096]{1,0:T(8,128)(2,1)} %g_ref.1, bf16[128,512]{1,0:T(8,128)(2,1)} %k_ref.3, ...), custom_call_target="tpu_custom_call" | custom-call | bytes 8388608 | tf_op jit(solution)/shard_map/turn/pallas_call | solution.py:265
  12.6 6.4 %collective-permute-start.3 = (bf16[512,128]{1,0:T(8,128)(2,1)S(1)}, bf16[512,128]{1,0:T(8,128)(2,1)S(1)}, u32[]{:S(2)}, u32[]{:S(2)}) collective-permute-start(bf16[512,128]{1,0:T(8,128)(2,1)S(1)} %get-tuple-element.32.own_ref.refs_9_), channel_id=1, source_target_pairs={{0,2},{1,3},{2,4},{3,5},{4,6},{5,7},{6,8},{7,9},{8,10},{9,11},{10,... | collective-permute-start | bytes 393224 | tf_op jit(solution)/shard_map/ppermute | solution.py:23
  19.0 3.8 %collective-permute-start.2 = (bf16[512,128]{1,0:T(8,128)(2,1)S(1)}, bf16[512,128]{1,0:T(8,128)(2,1)S(1)}, u32[]{:S(2)}, u32[]{:S(2)}) collective-permute-start(bf16[512,128]{1,0:T(8,128)(2,1)S(1)} %get-tuple-element.32.own_ref.refs_9_), channel_id=1, source_target_pairs={{0,1},{1,2},{2,3},{3,4},{4,5},{5,6},{6,7},{7,8},{8,9},{9,10},{10,1... | collective-permute-start | bytes 393224 | tf_op jit(solution)/shard_map/ppermute | solution.py:23
  22.8 0.0 collective-permute-done.1.two_ref.refs_6_
  22.8 1.3 %collective-permute-done.one_ref.refs_5_ = bf16[528,128]{1,0:T(8,128)(2,1)S(1)} collective-permute-done((bf16[528,128]{1,0:T(8,128)(2,1)S(1)}, bf16[528,128]{1,0:T(8,128)(2,1)S(1)}, u32[]{:S(2)}, u32[]{:S(2)}) %collective-permute-start) | collective-permute-done | bytes 135200 | tf_op jit(solution)/shard_map/ppermute | solution.py:23
  24.2 2.7 %scores.2 = (bf16[128,2048]{1,0:T(8,128)(2,1)S(1)}, bf16[256,2048]{1,0:T(8,128)(2,1)S(1)}, bf16[256,256]{1,0:T(8,128)(2,1)S(1)}, bf16[256,256]{1,0:T(8,128)(2,1)S(1)}, f32[256,128]{1,0:T(8,128)S(1)}) custom-call(bf16[128,4096]{1,0:T(8,128)(2,1)S(1)} %get-tuple-element.26.q_ref.refs_0_, bf16[128,4096]{1,0:T(8,128)(2,1)S(1)} %get-tuple-element.27.g_ref.refs_1_, ...), custom_call_target="tpu_custom_call" | custom-call | flops 805306368 | bytes 3145728 | tf_op jit(solution)/shard_map/scores/pallas_call | solution.py:280
  26.9 4.6 %collective-permute-start.4 = (bf16[256,256]{1,0:T(8,128)(2,1)S(1)}, bf16[256,256]{1,0:T(8,128)(2,1)S(1)}, u32[]{:S(2)}, u32[]{:S(2)}) collective-permute-start(bf16[256,256]{1,0:T(8,128)(2,1)S(1)} %get-tuple-element.35), channel_id=1, source_target_pairs={{1,0},{2,1},{3,2},{4,3},{5,4},{6,5},{7,6},{8,7},{9,8},{10,9},{11,1... | collective-permute-start | bytes 393224 | tf_op jit(solution)/shard_map/ppermute | solution.py:23
  31.5 2.1 %collective-permute-start.5 = (bf16[256,256]{1,0:T(8,128)(2,1)S(1)}, bf16[256,256]{1,0:T(8,128)(2,1)S(1)}, u32[]{:S(2)}, u32[]{:S(2)}) collective-permute-start(bf16[256,256]{1,0:T(8,128)(2,1)S(1)} %get-tuple-element.36), channel_id=1, source_target_pairs={{2,0},{3,1},{4,2},{5,3},{6,4},{7,5},{8,6},{9,7},{10,8},{11,9},{12,... | collective-permute-start | bytes 393224 | tf_op jit(solution)/shard_map/ppermute | solution.py:23
  33.6 0.0 collective-permute-done.3.two_ref.refs_11_
  33.6 0.0 collective-permute-done.2.one_ref.refs_10_
  33.6 2.7 %scores.3 = (bf16[128,2048]{1,0:T(8,128)(2,1)S(1)}, bf16[256,2048]{1,0:T(8,128)(2,1)S(1)}, bf16[256,256]{1,0:T(8,128)(2,1)S(1)}, bf16[256,256]{1,0:T(8,128)(2,1)S(1)}) custom-call(bf16[128,4096]{1,0:T(8,128)(2,1)S(1)} %get-tuple-element.26.q_ref.refs_0_, bf16[128,4096]{1,0:T(8,128)(2,1)S(1)} %get-tuple-element.27.g_ref.refs_1_, ...), custom_call_target="tpu_custom_call" | custom-call | flops 805306368 | bytes 3145728 | tf_op jit(solution)/shard_map/scores/pallas_call | solution.py:280
  36.3 4.0 %collective-permute-start.6 = (bf16[256,256]{1,0:T(8,128)(2,1)S(1)}, bf16[256,256]{1,0:T(8,128)(2,1)S(1)}, u32[]{:S(2)}, u32[]{:S(2)}) collective-permute-start(bf16[256,256]{1,0:T(8,128)(2,1)S(1)} %get-tuple-element.44), channel_id=1, source_target_pairs={{1,0},{2,1},{3,2},{4,3},{5,4},{6,5},{7,6},{8,7},{9,8},{10,9},{11,1... | collective-permute-start | bytes 393224 | tf_op jit(solution)/shard_map/ppermute | solution.py:23
  40.3 3.2 %collective-permute-start.7 = (bf16[256,256]{1,0:T(8,128)(2,1)S(1)}, bf16[256,256]{1,0:T(8,128)(2,1)S(1)}, u32[]{:S(2)}, u32[]{:S(2)}) collective-permute-start(bf16[256,256]{1,0:T(8,128)(2,1)S(1)} %get-tuple-element.46), channel_id=1, source_target_pairs={{2,0},{3,1},{4,2},{5,3},{6,4},{7,5},{8,6},{9,7},{10,8},{11,9},{12,... | collective-permute-start | bytes 393224 | tf_op jit(solution)/shard_map/ppermute | solution.py:23
  43.4 0.0 collective-permute-done.4.refs_2_
  43.4 0.0 collective-permute-done.5.refs_4_
  43.5 2.2 %rest.1 = (bf16[128,4096]{1,0:T(8,128)(2,1)}, f32[256,256]{1,0:T(8,128)S(1)}, f32[256,256]{1,0:T(8,128)S(1)}) custom-call(bf16[128,4096]{1,0:T(8,128)(2,1)S(1)} %get-tuple-element.26.q_ref.refs_0_, bf16[128,4096]{1,0:T(8,128)(2,1)S(1)} %get-tuple-element.27.g_ref.refs_1_, bf16[128,2048]{1,0:T(8,128)(2,1)S(1)} %get-tuple-element.30.refs_2_, ...), custom_call_target="tpu_custom_call" | custom-call | flops 805306368 | bytes 6291456 | tf_op jit(solution)/shard_map/rest/pallas_call | solution.py:297
  45.7 0.0 collective-permute-done.6.refs_3_
  45.7 5.8 %collective-permute-done.7.refs_5_ = bf16[256,256]{1,0:T(8,128)(2,1)S(1)} collective-permute-done((bf16[256,256]{1,0:T(8,128)(2,1)S(1)}, bf16[256,256]{1,0:T(8,128)(2,1)S(1)}, u32[]{:S(2)}, u32[]{:S(2)}) %collective-permute-start.7) | collective-permute-done | bytes 131104 | tf_op jit(solution)/shard_map/ppermute | solution.py:23
  51.5 0.8 %final.1 = (bf16[128,512]{1,0:T(8,128)(2,1)}, bf16[128,512]{1,0:T(8,128)(2,1)}) custom-call(f32[256,256]{1,0:T(8,128)S(1)} %get-tuple-element.41.refs_0_, f32[256,256]{1,0:T(8,128)S(1)} %get-tuple-element.42.refs_1_, bf16[256,256]{1,0:T(8,128)(2,1)S(1)} %collective-permute-done.4.refs_2_, bf16[256,256]{1,0:T(8,128)(2,1)S(1)} %collective-permute-done.6.refs_3_, ...), custom_call_target="tpu_custom_call" | custom-call | bytes 1048576 | tf_op jit(solution)/shard_map/final/pallas_call | solution.py:311
Async XLA Ops:
  1.5 21.3 %collective-permute-start.1 = (bf16[528,128]{1,0:T(8,128)(2,1)S(1)}, bf16[528,128]{1,0:T(8,128)(2,1)S(1)}, u32[]{:S(2)}, u32[]{:S(2)}) collective-permute-start(bf16[528,128]{1,0:T(8,128)(2,1)S(1)} %pack.1.own_ref.refs_4_), channel_id=1, source_target_pairs={{0,2},{1,3},{2,4},{3,5},{4,6},{5,7},{6,8},{7,9},{8,10},{9,11},{10,... | collective-permute-start | bytes 405512 | tf_op jit(solution)/shard_map/ppermute | solution.py:23
  6.7 17.5 %collective-permute-start = (bf16[528,128]{1,0:T(8,128)(2,1)S(1)}, bf16[528,128]{1,0:T(8,128)(2,1)S(1)}, u32[]{:S(2)}, u32[]{:S(2)}) collective-permute-start(bf16[528,128]{1,0:T(8,128)(2,1)S(1)} %pack.1.own_ref.refs_4_), channel_id=1, source_target_pairs={{0,1},{1,2},{2,3},{3,4},{4,5},{5,6},{6,7},{7,8},{8,9},{9,10},{10,1... | collective-permute-start | bytes 405512 | tf_op jit(solution)/shard_map/ppermute | solution.py:23
  12.6 21.0 %collective-permute-start.3 = (bf16[512,128]{1,0:T(8,128)(2,1)S(1)}, bf16[512,128]{1,0:T(8,128)(2,1)S(1)}, u32[]{:S(2)}, u32[]{:S(2)}) collective-permute-start(bf16[512,128]{1,0:T(8,128)(2,1)S(1)} %get-tuple-element.32.own_ref.refs_9_), channel_id=1, source_target_pairs={{0,2},{1,3},{2,4},{3,5},{4,6},{5,7},{6,8},{7,9},{8,10},{9,11},{10,... | collective-permute-start | bytes 393224 | tf_op jit(solution)/shard_map/ppermute | solution.py:23
  19.0 14.6 %collective-permute-start.2 = (bf16[512,128]{1,0:T(8,128)(2,1)S(1)}, bf16[512,128]{1,0:T(8,128)(2,1)S(1)}, u32[]{:S(2)}, u32[]{:S(2)}) collective-permute-start(bf16[512,128]{1,0:T(8,128)(2,1)S(1)} %get-tuple-element.32.own_ref.refs_9_), channel_id=1, source_target_pairs={{0,1},{1,2},{2,3},{3,4},{4,5},{5,6},{6,7},{7,8},{8,9},{9,10},{10,1... | collective-permute-start | bytes 393224 | tf_op jit(solution)/shard_map/ppermute | solution.py:23
  26.9 16.6 %collective-permute-start.4 = (bf16[256,256]{1,0:T(8,128)(2,1)S(1)}, bf16[256,256]{1,0:T(8,128)(2,1)S(1)}, u32[]{:S(2)}, u32[]{:S(2)}) collective-permute-start(bf16[256,256]{1,0:T(8,128)(2,1)S(1)} %get-tuple-element.35), channel_id=1, source_target_pairs={{1,0},{2,1},{3,2},{4,3},{5,4},{6,5},{7,6},{8,7},{9,8},{10,9},{11,1... | collective-permute-start | bytes 393224 | tf_op jit(solution)/shard_map/ppermute | solution.py:23
  31.5 11.9 %collective-permute-start.5 = (bf16[256,256]{1,0:T(8,128)(2,1)S(1)}, bf16[256,256]{1,0:T(8,128)(2,1)S(1)}, u32[]{:S(2)}, u32[]{:S(2)}) collective-permute-start(bf16[256,256]{1,0:T(8,128)(2,1)S(1)} %get-tuple-element.36), channel_id=1, source_target_pairs={{2,0},{3,1},{4,2},{5,3},{6,4},{7,5},{8,6},{9,7},{10,8},{11,9},{12,... | collective-permute-start | bytes 393224 | tf_op jit(solution)/shard_map/ppermute | solution.py:23
  36.3 9.4 %collective-permute-start.6 = (bf16[256,256]{1,0:T(8,128)(2,1)S(1)}, bf16[256,256]{1,0:T(8,128)(2,1)S(1)}, u32[]{:S(2)}, u32[]{:S(2)}) collective-permute-start(bf16[256,256]{1,0:T(8,128)(2,1)S(1)} %get-tuple-element.44), channel_id=1, source_target_pairs={{1,0},{2,1},{3,2},{4,3},{5,4},{6,5},{7,6},{8,7},{9,8},{10,9},{11,1... | collective-permute-start | bytes 393224 | tf_op jit(solution)/shard_map/ppermute | solution.py:23
  40.3 11.2 %collective-permute-start.7 = (bf16[256,256]{1,0:T(8,128)(2,1)S(1)}, bf16[256,256]{1,0:T(8,128)(2,1)S(1)}, u32[]{:S(2)}, u32[]{:S(2)}) collective-permute-start(bf16[256,256]{1,0:T(8,128)(2,1)S(1)} %get-tuple-element.46), channel_id=1, source_target_pairs={{2,0},{3,1},{4,2},{5,3},{6,4},{7,5},{8,6},{9,7},{10,8},{11,9},{12,... | collective-permute-start | bytes 393224 | tf_op jit(solution)/shard_map/ppermute | solution.py:23

commit v6 on v5

--- a/solution.py
+++ b/solution.py
@@ -14,6 +14,7 @@
 LOG2E = 1.4426950408889634
 AXES = ("inner", "outer")
 CHUNKS = 2
+UNIT = 4
 VMEM_LIMIT = 24 * 1024 * 1024
 
 
@@ -94,7 +95,7 @@
         copy.wait()
 
 
-def score_kernel(group, tokens, scale, known, offset, q_ref, g_ref, qt_ref, gt_ref, own_ref, one_ref, two_ref, *refs):
+def score_kernel(group, tokens, scale, known, offset, q_ref, g_ref, qt_ref, gt_ref, own_ref, two_ref, one_ref, *refs):
     p_ref, ds_ref, far_ref, near_ref = refs[1:] if known else refs[:-1]
     bias_ref = refs[0] if known else refs[-1]
     tri = sees_own(tokens, 1)
@@ -107,83 +108,89 @@
         mixed = jnp.where(tri, seg_own, seg_two)
         bias_ref[0:tokens, :] = jnp.where(mixed == seg_query, 0.0, NEG)
         bias_ref[tokens : 2 * tokens, :] = jnp.where(seg_one == seg_query, 0.0, NEG)
+    wide = UNIT * HD
+    tri = sees_own(tokens, UNIT)
     far_mask = jnp.where(tri, 0.0, 1.0).astype(jnp.bfloat16)
+    bias_mix = jnp.concatenate([bias_ref[0:tokens, :]] * UNIT, axis=1)
+    bias_one = jnp.concatenate([bias_ref[tokens : 2 * tokens, :]] * UNIT, axis=1)
     factor = scale * LOG2E
-    pairs = group // 2
+    units = group // UNIT
     count = HK // CHUNKS
 
     def products(unit):
-        part = unit // pairs
+        part = unit // units
         keys, vals = [
             jnp.concatenate([ref[first : first + tokens, :] for ref in (own_ref, one_ref, two_ref)], axis=0)
             for first in (part * tokens, (count + part) * tokens)
         ]
-        first = (offset * group + 2 * unit) * HD
-        both = slice(first, first + 2 * HD)
-        return dot(keys, qt_ref[:, both]), dot(vals, gt_ref[:, both])
-
-    def head(raw, dp, cols):
-        s_mix = jnp.where(tri, raw[0:tokens], raw[2 * tokens :]) + bias_ref[0:tokens, :]
-        s_one = raw[tokens : 2 * tokens] + bias_ref[tokens : 2 * tokens, :]
-        top = jnp.max(jnp.maximum(s_mix, s_one), axis=0, keepdims=True)
-        e_mix = jnp.exp2((s_mix - top) * factor)
-        e_one = jnp.exp2((s_one - top) * factor)
-        inverse = 1.0 / jnp.sum(e_mix + e_one, axis=0, keepdims=True)
-        p_mix = e_mix * inverse
-        p_one = e_one * inverse
-        d_mix = jnp.where(tri, dp[0:tokens], dp[2 * tokens :])
-        d_one = dp[tokens : 2 * tokens]
-        delta = jnp.sum(p_mix * d_mix + p_one * d_one, axis=0, keepdims=True)
-        ds_mix = (p_mix * (d_mix - delta)).astype(jnp.bfloat16)
-        ds_one = (p_one * (d_one - delta)).astype(jnp.bfloat16)
-        p_mix = p_mix.astype(jnp.bfloat16)
-        p_one = p_one.astype(jnp.bfloat16)
-        p_ref[:, cols] = p_mix
-        ds_ref[0:tokens, cols] = ds_mix
-        ds_ref[tokens : 2 * tokens, cols] = ds_one
-        return (
-            jnp.concatenate([p_one, p_mix * far_mask], axis=0),
-            jnp.concatenate([ds_one, ds_mix * far_mask], axis=0),
-        )
+        first = offset * group * HD + unit * wide
+        return dot(keys, qt_ref[:, first : first + wide]), dot(vals, gt_ref[:, first : first + wide])
 
     ahead = products(0)
     for part in range(count):
-        probs, grads = [], []
-        for pair in range(pairs):
-            unit = part * pairs + pair
+        sum_k = jnp.zeros((2 * tokens, HD), jnp.float32)
+        sum_v = jnp.zeros((2 * tokens, HD), jnp.float32)
+        for step in range(units):
+            unit = part * units + step
             raw, dp = ahead
-            if unit + 1 < count * pairs:
+            if unit + 1 < count * units:
                 ahead = products(unit + 1)
-            for h in range(2):
-                inner = slice(h * HD, (h + 1) * HD)
-                p, ds = head(raw[:, inner], dp[:, inner], slice((2 * unit + h) * HD, (2 * unit + h + 1) * HD))
-                probs.append(p)
-                grads.append(ds)
-        first = (offset + part) * group
-        sum_k = dot(jnp.concatenate(grads, axis=1), stacked(q_ref, first, group)) * scale
-        sum_v = dot(jnp.concatenate(probs, axis=1), stacked(g_ref, first, group))
+            cols = slice(unit * wide, (unit + 1) * wide)
+            s_mix = jnp.where(tri, raw[0:tokens], raw[2 * tokens :]) + bias_mix
+            s_one = raw[tokens : 2 * tokens] + bias_one
+            top = jnp.max(jnp.maximum(s_mix, s_one), axis=0, keepdims=True)
+            e_mix = jnp.exp2((s_mix - top) * factor)
+            e_one = jnp.exp2((s_one - top) * factor)
+            inverse = 1.0 / jnp.sum(e_mix + e_one, axis=0, keepdims=True)
+            p_mix = e_mix * inverse
+            p_one = e_one * inverse
+            d_mix = jnp.where(tri, dp[0:tokens], dp[2 * tokens :])
+            d_one = dp[tokens : 2 * tokens]
+            delta = jnp.sum(p_mix * d_mix + p_one * d_one, axis=0, keepdims=True)
+            ds_mix = (p_mix * (d_mix - delta)).astype(jnp.bfloat16)
+            ds_one = (p_one * (d_one - delta)).astype(jnp.bfloat16)
+            p_mix = p_mix.astype(jnp.bfloat16)
+            p_one = p_one.astype(jnp.bfloat16)
+            p_ref[:, cols] = p_mix
+            ds_ref[0:tokens, cols] = ds_mix
+            ds_ref[tokens : 2 * tokens, cols] = ds_one
+            first = offset * group + unit * UNIT
+            sum_k = sum_k + dot(jnp.concatenate([ds_one, ds_mix * far_mask], axis=0), stacked(q_ref, first, UNIT))
+            sum_v = sum_v + dot(jnp.concatenate([p_one, p_mix * far_mask], axis=0), stacked(g_ref, first, UNIT))
+        sum_k = sum_k * scale
         cols = slice(part * HD, (part + 1) * HD)
         for ref, row in ((near_ref, 0), (far_ref, tokens)):
             ref[0:tokens, cols] = sum_k[row : row + tokens].astype(ref.dtype)
             ref[tokens : 2 * tokens, cols] = sum_v[row : row + tokens].astype(ref.dtype)
 
 
-def rest_kernel(group, tokens, scale, *refs):
+def leave(total, index, tokens, kv_ref, k_out, v_out, sems):
+    width = total.shape[1]
+    kv_ref[...] = total.astype(kv_ref.dtype)
+    copies = [
+        pltpu.make_async_copy(
+            kv_ref.at[pl.ds(half * tokens, tokens), :], out.at[:, pl.ds(index * width, width)], sems.at[half]
+        )
+        for half, out in enumerate((k_out, v_out))
+    ]
+    for copy in copies:
+        copy.start()
+    return copies
+
+
+def rest_kernel(group, tokens, scale, q_ref, g_ref, far_ref, near_ref, *refs):
     per = 5
-    q_ref, g_ref = refs[0:2]
-    chunk_refs = [refs[2 + per * c : 2 + per * (c + 1)] for c in range(CHUNKS)]
-    dq_out = refs[2 + per * CHUNKS]
-    own_outs = refs[3 + per * CHUNKS : 3 + per * CHUNKS + CHUNKS]
-    dq_ref, sems = refs[-2:]
+    chunk_refs = [refs[per * c : per * (c + 1)] for c in range(CHUNKS)]
+    dq_out, k_out, v_out, own_out, dq_ref, kv_ref, sems, kv_sems = refs[per * CHUNKS :]
     tri = sees_own(tokens, 2)
     own_mask = jnp.where(tri, 1.0, 0.0).astype(jnp.bfloat16)
     far_mask = jnp.where(tri, 0.0, 1.0).astype(jnp.bfloat16)
     wide = group * HD
+    count = HK // CHUNKS
     copies = []
-    for chunk, (p_ref, ds_ref, own_ref, one_ref, two_ref) in enumerate(chunk_refs):
-        count = HK // CHUNKS
+    for chunk, (p_ref, ds_ref, own_ref, two_ref, one_ref) in enumerate(chunk_refs):
+        sums = []
         for part in range(count):
-            inner = slice(part * HD, (part + 1) * HD)
             block = slice(part * tokens, (part + 1) * tokens)
             keys_t = jnp.concatenate([jnp.transpose(ref[block, :]) for ref in (own_ref, one_ref, two_ref)], axis=1)
             sum_k = jnp.zeros((tokens, HD), jnp.float32)
@@ -201,26 +208,25 @@
                     dq_ref[:, (first + h) * HD : (first + h + 1) * HD] = jnp.transpose(
                         dq_t[:, h * HD : (h + 1) * HD]
                     )
-            own_outs[chunk][0:tokens, inner] = sum_k * scale
-            own_outs[chunk][tokens : 2 * tokens, inner] = sum_v
+            sums.append(jnp.concatenate([sum_k * scale, sum_v], axis=0))
             index = chunk * count + part
             span = pl.ds(index * wide, wide)
             copies.append(pltpu.make_async_copy(dq_ref.at[:, span], dq_out.at[:, span], sems.at[index]))
             copies[-1].start()
+        total = jnp.concatenate(sums, axis=1)
+        if chunk == 0:
+            total = total + near_ref[...].astype(jnp.float32) + far_ref[...].astype(jnp.float32)
+            copies += leave(total, 0, tokens, kv_ref, k_out, v_out, kv_sems)
+        else:
+            own_out[...] = total
     for copy in copies:
         copy.wait()
 
 
-def final_kernel(tokens, *refs):
-    count = (len(refs) - 2) // 3
-    k_out, v_out = refs[-2:]
-    for index in range(count):
-        own_ref, near_ref, far_ref = refs[index : 3 * count : count]
-        width = own_ref.shape[1]
-        cols = slice(index * width, (index + 1) * width)
-        total = own_ref[...] + near_ref[...].astype(jnp.float32) + far_ref[...].astype(jnp.float32)
-        k_out[:, cols] = total[0:tokens].astype(k_out.dtype)
-        v_out[:, cols] = total[tokens:].astype(v_out.dtype)
+def final_kernel(tokens, own_ref, far_ref, near_ref, k_before, v_before, k_out, v_out, kv_ref, sems):
+    total = own_ref[...] + near_ref[...].astype(jnp.float32) + far_ref[...].astype(jnp.float32)
+    for copy in leave(total, 1, tokens, kv_ref, k_out, v_out, sems):
+        copy.wait()
 
 
 def bf16(*shape):
@@ -273,7 +279,7 @@
     )(*in_hbm(q, g, key_states, value_states))
 
 
-def score_call(q, g, qt, gt, own, one, two, bias, offset, group, tokens, scale):
+def score_call(q, g, qt, gt, own, two, one, bias, offset, group, tokens, scale):
     count = HK // CHUNKS
     span = count * group * HD
     known = bias is not None
@@ -289,32 +295,44 @@
         cost_estimate=cost(2 * tokens * 3 * span * tokens * 4, 12 * tokens * span, 2 * tokens * span),
         compiler_params=PARAMS,
         name="scores",
-    )(q, g, qt, gt, own, one, two, *([bias] if known else []))
-
-
-def rest_call(q, g, parts, group, tokens, scale):
-    count = HK // CHUNKS
+    )(q, g, qt, gt, own, two, one, *([bias] if known else []))
+
+
+ON_CHIP = pl.BlockSpec(memory_space=pltpu.VMEM)
+IN_HBM = pl.BlockSpec(memory_space=pltpu.HBM)
+
+
+def rest_call(q, g, far, near, parts, group, tokens, scale):
+    grads = bf16(tokens, HK * HD)
+    chunk = (2 * tokens, HK // CHUNKS * HD)
     return pl.pallas_call(
         functools.partial(rest_kernel, group, tokens, scale),
-        out_specs=[pl.BlockSpec(memory_space=pltpu.HBM)] + [pl.BlockSpec(memory_space=pltpu.VMEM)] * CHUNKS,
-        out_shape=[bf16(*q.shape)] + [f32(2 * tokens, count * HD)] * CHUNKS,
-        scratch_shapes=[pltpu.VMEM(q.shape, jnp.bfloat16), pltpu.SemaphoreType.DMA((HK,))],
+        out_specs=[IN_HBM] * 3 + [ON_CHIP],
+        out_shape=[bf16(*q.shape), grads, grads, f32(*chunk)],
+        scratch_shapes=[
+            pltpu.VMEM(q.shape, jnp.bfloat16),
+            pltpu.VMEM(chunk, jnp.bfloat16),
+            pltpu.SemaphoreType.DMA((HK,)),
+            pltpu.SemaphoreType.DMA((2,)),
+        ],
         cost_estimate=cost(2 * tokens * 3 * q.shape[1] * tokens * 2, 12 * tokens * q.shape[1]),
         compiler_params=PARAMS,
         name="rest",
-    )(q, g, *[x for part in parts for x in part])
-
-
-def final_call(owns, nears, fars):
-    tokens = owns[0].shape[0] // 2
-    width = sum(x.shape[1] for x in owns)
-    return pl.pallas_call(
-        functools.partial(final_kernel, tokens),
-        out_shape=[bf16(tokens, width)] * 2,
-        cost_estimate=cost(0, 16 * tokens * width),
+    )(q, g, far, near, *[x for part in parts for x in part])
+
+
+def final_call(own, far, near, key_grad, value_grad):
+    return pl.pallas_call(
+        functools.partial(final_kernel, key_grad.shape[0]),
+        in_specs=[ON_CHIP] * 3 + [IN_HBM] * 2,
+        out_specs=[IN_HBM] * 2,
+        out_shape=[bf16(*key_grad.shape)] * 2,
+        scratch_shapes=[pltpu.VMEM(own.shape, jnp.bfloat16), pltpu.SemaphoreType.DMA((2,))],
+        input_output_aliases={3: 0, 4: 1},
+        cost_estimate=cost(0, 16 * own.shape[0] * own.shape[1]),
         compiler_params=PARAMS,
         name="final",
-    )(*owns, *nears, *fars)
+    )(own, far, near, key_grad, value_grad)
 
 
 def shards(queries, key_states, value_states, out_grad, segment_ids):
@@ -326,21 +344,20 @@
     own = [pack_call(key_states, value_states, segment_ids)]
     q, g, qt, gt, later = turn_call(queries, out_grad, key_states, value_states, group)
     own.append(later)
+    two = [shift(x, 2) for x in own]
     one = [shift(x, 1) for x in own]
-    two = [shift(x, 2) for x in own]
     first, near, far, bias = [], [], [], None
     for c in chunks:
-        results = score_call(q, g, qt, gt, own[c], one[c], two[c], bias, c * step, group, tokens, scale)
+        results = score_call(q, g, qt, gt, own[c], two[c], one[c], bias, c * step, group, tokens, scale)
         bias = results[4] if bias is None else bias
         first.append(results)
         far.append(shift(results[2], -2))
         near.append(shift(results[3], -1))
-    ds = [x[1] for x in first]
-    ds[0], ds[1], near[0], far[0] = lax.optimization_barrier((ds[0], ds[1], near[0], far[0]))
-    query_grad, *parts = rest_call(
-        q, g, [(first[c][0], ds[c], own[c], one[c], two[c]) for c in chunks], group, tokens, scale
+    query_grad, key_grad, value_grad, own_terms = rest_call(
+        q, g, far[0], near[0], [(first[c][0], first[c][1], own[c], two[c], one[c]) for c in chunks],
+        group, tokens, scale,
     )
-    key_grad, value_grad = final_call(parts, near, far)
+    key_grad, value_grad = final_call(own_terms, far[1], near[1], key_grad, value_grad)
     return query_grad, key_grad, value_grad
 
 

time: 52.9 us -> 51.5 us (0.974)
  waiting for transfers between devices: 7.17 us -> 6.32 us
  Pallas kernels: 11.3 us -> 10.7 us
    ppermute x8, waiting for transfers between devices: 7.17 us -> 6.32 us  [shift(): lax.ppermute(value, AXES, [(i, i + steps) for i in range(first, last)])]
    pallas_call x2, Pallas kernels: 5.37 us -> 4.76 us  [score_call(): pl.pallas_call(functools.partial(score_kernel, group, tokens, scale, know...]
  transfers between devices with their start and end apart: 8 -> 8, of which waited for: 2 -> 3; matrix products, arithmetic and copies ran while one was open for 0% -> 0% of each run, Pallas kernels for 18% -> 18%
where the time goes in v6:
time: 51.5 us; the launch traced here: 50.8 us
  starting transfers between devices  33 us (64%)
  Pallas kernels  10.7 us (21%)
  waiting for transfers between devices  6.32 us (12%)
  between operations  0.77 us (1%)
    ppermute x8, starting transfers between devices, shift(): lax.ppermute(value, AXES, [(i, i + steps) for i in range(first, last)])  33 us
    ppermute x8, waiting for transfers between devices, shift(): lax.ppermute(value, AXES, [(i, i + steps) for i in range(first, last)])  6.32 us
    pallas_call x2, Pallas kernels, score_call(): pl.pallas_call(functools.partial(score_kernel, group, tokens, scale, know...  4.76 us
    pallas_call x1, Pallas kernels, rest_call(): pl.pallas_call(functools.partial(rest_kernel, group, tokens, scale), out_...  2.25 us
    pallas_call x1, Pallas kernels, turn_call(): pl.pallas_call(functools.partial(turn_kernel, group), in_specs=[pl.BlockS...  2.07 us
  transfers between devices with their start and end apart: 8, of which 3 were waited for; matrix products, arithmetic and copies ran while one was open for 0% of the time, Pallas kernels for 18%

profile of v6, /device:TPU:4, one launch (start us, length us, event | category | flops | bytes accessed | tf_op | source)
XLA Modules:
  0.0 50.8 jit_solution(5642923084595607544)
XLA Ops:
  0.6 0.9 %pack.1.own_ref.refs_2_ = bf16[528,128]{1,0:T(8,128)(2,1)S(1)} custom-call(bf16[128,512]{1,0:T(8,128)(2,1)} %k_ref.3, bf16[128,512]{1,0:T(8,128)(2,1)} %v_ref.3, s32[128]{0:T(128)} %seg_ref.1), custom_call_target="tpu_custom_call" | custom-call | bytes 262144 | tf_op jit(solution)/shard_map/pack/pallas_call | solution.py:253
  1.5 5.2 %collective-permute-start = (bf16[528,128]{1,0:T(8,128)(2,1)S(1)}, bf16[528,128]{1,0:T(8,128)(2,1)S(1)}, u32[]{:S(2)}, u32[]{:S(2)}) collective-permute-start(bf16[528,128]{1,0:T(8,128)(2,1)S(1)} %pack.1.own_ref.refs_2_), channel_id=1, source_target_pairs={{0,2},{1,3},{2,4},{3,5},{4,6},{5,7},{6,8},{7,9},{8,10},{9,11},{10,... | collective-permute-start | bytes 405512 | tf_op jit(solution)/shard_map/ppermute | solution.py:24
  6.7 3.8 %collective-permute-start.1 = (bf16[528,128]{1,0:T(8,128)(2,1)S(1)}, bf16[528,128]{1,0:T(8,128)(2,1)S(1)}, u32[]{:S(2)}, u32[]{:S(2)}) collective-permute-start(bf16[528,128]{1,0:T(8,128)(2,1)S(1)} %pack.1.own_ref.refs_2_), channel_id=1, source_target_pairs={{0,1},{1,2},{2,3},{3,4},{4,5},{5,6},{6,7},{7,8},{8,9},{9,10},{10,1... | collective-permute-start | bytes 405512 | tf_op jit(solution)/shard_map/ppermute | solution.py:24
  10.5 2.1 %turn.1 = (bf16[128,4096]{1,0:T(8,128)(2,1)S(1)}, bf16[128,4096]{1,0:T(8,128)(2,1)S(1)}, bf16[128,4096]{1,0:T(8,128)(2,1)S(1)}, bf16[128,4096]{1,0:T(8,128)(2,1)S(1)}, bf16[512,128]{1,0:T(8,128)(2,1)S(1)}) custom-call(bf16[128,4096]{1,0:T(8,128)(2,1)} %q_ref.1, bf16[128,4096]{1,0:T(8,128)(2,1)} %g_ref.1, bf16[128,512]{1,0:T(8,128)(2,1)} %k_ref.3, ...), custom_call_target="tpu_custom_call" | custom-call | bytes 8388608 | tf_op jit(solution)/shard_map/turn/pallas_call | solution.py:271
  12.6 6.4 %collective-permute-start.4 = (bf16[512,128]{1,0:T(8,128)(2,1)S(1)}, bf16[512,128]{1,0:T(8,128)(2,1)S(1)}, u32[]{:S(2)}, u32[]{:S(2)}) collective-permute-start(bf16[512,128]{1,0:T(8,128)(2,1)S(1)} %get-tuple-element.31.own_ref.refs_7_), channel_id=1, source_target_pairs={{0,2},{1,3},{2,4},{3,5},{4,6},{5,7},{6,8},{7,9},{8,10},{9,11},{10,... | collective-permute-start | bytes 393224 | tf_op jit(solution)/shard_map/ppermute | solution.py:24
  19.0 3.8 %collective-permute-start.5 = (bf16[512,128]{1,0:T(8,128)(2,1)S(1)}, bf16[512,128]{1,0:T(8,128)(2,1)S(1)}, u32[]{:S(2)}, u32[]{:S(2)}) collective-permute-start(bf16[512,128]{1,0:T(8,128)(2,1)S(1)} %get-tuple-element.31.own_ref.refs_7_), channel_id=1, source_target_pairs={{0,1},{1,2},{2,3},{3,4},{4,5},{5,6},{6,7},{7,8},{8,9},{9,10},{10,1... | collective-permute-start | bytes 393224 | tf_op jit(solution)/shard_map/ppermute | solution.py:24
  22.8 0.0 collective-permute-done.two_ref.refs_3_
  22.8 1.3 %collective-permute-done.1.one_ref.refs_4_ = bf16[528,128]{1,0:T(8,128)(2,1)S(1)} collective-permute-done((bf16[528,128]{1,0:T(8,128)(2,1)S(1)}, bf16[528,128]{1,0:T(8,128)(2,1)S(1)}, u32[]{:S(2)}, u32[]{:S(2)}) %collective-permute-start.1) | collective-permute-done | bytes 135200 | tf_op jit(solution)/shard_map/ppermute | solution.py:24
  24.2 2.4 %scores.2 = (bf16[128,2048]{1,0:T(8,128)(2,1)S(1)}, bf16[256,2048]{1,0:T(8,128)(2,1)S(1)}, bf16[256,256]{1,0:T(8,128)(2,1)S(1)}, bf16[256,256]{1,0:T(8,128)(2,1)S(1)}, f32[256,128]{1,0:T(8,128)S(1)}) custom-call(bf16[128,4096]{1,0:T(8,128)(2,1)S(1)} %get-tuple-element.23.q_ref, bf16[128,4096]{1,0:T(8,128)(2,1)S(1)} %get-tuple-element.24.g_ref, ...), custom_call_target="tpu_custom_call" | custom-call | flops 805306368 | bytes 3145728 | tf_op jit(solution)/shard_map/scores/pallas_call | solution.py:286
  26.6 4.2 %collective-permute-start.2 = (bf16[256,256]{1,0:T(8,128)(2,1)S(1)}, bf16[256,256]{1,0:T(8,128)(2,1)S(1)}, u32[]{:S(2)}, u32[]{:S(2)}) collective-permute-start(bf16[256,256]{1,0:T(8,128)(2,1)S(1)} %get-tuple-element.27), channel_id=1, source_target_pairs={{2,0},{3,1},{4,2},{5,3},{6,4},{7,5},{8,6},{9,7},{10,8},{11,9},{12,... | collective-permute-start | bytes 393224 | tf_op jit(solution)/shard_map/ppermute | solution.py:24
  30.8 2.5 %collective-permute-start.3 = (bf16[256,256]{1,0:T(8,128)(2,1)S(1)}, bf16[256,256]{1,0:T(8,128)(2,1)S(1)}, u32[]{:S(2)}, u32[]{:S(2)}) collective-permute-start(bf16[256,256]{1,0:T(8,128)(2,1)S(1)} %get-tuple-element.28), channel_id=1, source_target_pairs={{1,0},{2,1},{3,2},{4,3},{5,4},{6,5},{7,6},{8,7},{9,8},{10,9},{11,1... | collective-permute-start | bytes 393224 | tf_op jit(solution)/shard_map/ppermute | solution.py:24
  33.3 0.0 collective-permute-done.4.two_ref.refs_8_
  33.3 0.0 collective-permute-done.5.one_ref.refs_9_
  33.3 2.4 %scores.3 = (bf16[128,2048]{1,0:T(8,128)(2,1)S(1)}, bf16[256,2048]{1,0:T(8,128)(2,1)S(1)}, bf16[256,256]{1,0:T(8,128)(2,1)S(1)}, bf16[256,256]{1,0:T(8,128)(2,1)S(1)}) custom-call(bf16[128,4096]{1,0:T(8,128)(2,1)S(1)} %get-tuple-element.23.q_ref, bf16[128,4096]{1,0:T(8,128)(2,1)S(1)} %get-tuple-element.24.g_ref, ...), custom_call_target="tpu_custom_call" | custom-call | flops 805306368 | bytes 3145728 | tf_op jit(solution)/shard_map/scores/pallas_call | solution.py:286
  35.7 4.4 %collective-permute-start.6 = (bf16[256,256]{1,0:T(8,128)(2,1)S(1)}, bf16[256,256]{1,0:T(8,128)(2,1)S(1)}, u32[]{:S(2)}, u32[]{:S(2)}) collective-permute-start(bf16[256,256]{1,0:T(8,128)(2,1)S(1)} %get-tuple-element.37), channel_id=1, source_target_pairs={{2,0},{3,1},{4,2},{5,3},{6,4},{7,5},{8,6},{9,7},{10,8},{11,9},{12,... | collective-permute-start | bytes 393224 | tf_op jit(solution)/shard_map/ppermute | solution.py:24
  40.1 2.7 %collective-permute-start.7 = (bf16[256,256]{1,0:T(8,128)(2,1)S(1)}, bf16[256,256]{1,0:T(8,128)(2,1)S(1)}, u32[]{:S(2)}, u32[]{:S(2)}) collective-permute-start(bf16[256,256]{1,0:T(8,128)(2,1)S(1)} %get-tuple-element.38), channel_id=1, source_target_pairs={{1,0},{2,1},{3,2},{4,3},{5,4},{6,5},{7,6},{8,7},{9,8},{10,9},{11,1... | collective-permute-start | bytes 393224 | tf_op jit(solution)/shard_map/ppermute | solution.py:24
  42.8 0.0 collective-permute-done.2.far_ref
  42.8 0.0 collective-permute-done.3.near_ref
  42.9 2.3 %rest.1 = (bf16[128,4096]{1,0:T(8,128)(2,1)}, bf16[128,512]{1,0:T(8,128)(2,1)}, bf16[128,512]{1,0:T(8,128)(2,1)}, f32[256,256]{1,0:T(8,128)S(1)}) custom-call(bf16[128,4096]{1,0:T(8,128)(2,1)S(1)} %get-tuple-element.23.q_ref, bf16[128,4096]{1,0:T(8,128)(2,1)S(1)} %get-tuple-element.24.g_ref, bf16[256,256]{1,0:T(8,128)(2,1)S(1)} %collective-permute-done.2.far_ref, ...), custom_call_target="tpu_custom_call" | custom-call | flops 805306368 | bytes 6291456 | tf_op jit(solution)/shard_map/rest/pallas_call | solution.py:308
  45.1 2.4 %collective-permute-done.6.far_ref = bf16[256,256]{1,0:T(8,128)(2,1)S(1)} collective-permute-done((bf16[256,256]{1,0:T(8,128)(2,1)S(1)}, bf16[256,256]{1,0:T(8,128)(2,1)S(1)}, u32[]{:S(2)}, u32[]{:S(2)}) %collective-permute-start.6) | collective-permute-done | bytes 131104 | tf_op jit(solution)/shard_map/ppermute | solution.py:24
  47.5 2.6 %collective-permute-done.7.near_ref = bf16[256,256]{1,0:T(8,128)(2,1)S(1)} collective-permute-done((bf16[256,256]{1,0:T(8,128)(2,1)S(1)}, bf16[256,256]{1,0:T(8,128)(2,1)S(1)}, u32[]{:S(2)}, u32[]{:S(2)}) %collective-permute-start.7) | collective-permute-done | bytes 131104 | tf_op jit(solution)/shard_map/ppermute | solution.py:24
  50.1 0.7 %final.1 = (bf16[128,512]{1,0:T(8,128)(2,1)}, bf16[128,512]{1,0:T(8,128)(2,1)}) custom-call(f32[256,256]{1,0:T(8,128)S(1)} %get-tuple-element.36.own_ref, bf16[256,256]{1,0:T(8,128)(2,1)S(1)} %collective-permute-done.6.far_ref, bf16[256,256]{1,0:T(8,128)(2,1)S(1)} %collective-permute-done.7.near_ref, ...), custom_call_target="tpu_custom_call", output_to_operand_aliasing={{0}: (3, {}), {1}: (4, {})} | custom-call | bytes 1048576 | tf_op jit(solution)/shard_map/final/pallas_call | solution.py:325
Async XLA Ops:
  1.5 21.3 %collective-permute-start = (bf16[528,128]{1,0:T(8,128)(2,1)S(1)}, bf16[528,128]{1,0:T(8,128)(2,1)S(1)}, u32[]{:S(2)}, u32[]{:S(2)}) collective-permute-start(bf16[528,128]{1,0:T(8,128)(2,1)S(1)} %pack.1.own_ref.refs_2_), channel_id=1, source_target_pairs={{0,2},{1,3},{2,4},{3,5},{4,6},{5,7},{6,8},{7,9},{8,10},{9,11},{10,... | collective-permute-start | bytes 405512 | tf_op jit(solution)/shard_map/ppermute | solution.py:24
  6.7 17.5 %collective-permute-start.1 = (bf16[528,128]{1,0:T(8,128)(2,1)S(1)}, bf16[528,128]{1,0:T(8,128)(2,1)S(1)}, u32[]{:S(2)}, u32[]{:S(2)}) collective-permute-start(bf16[528,128]{1,0:T(8,128)(2,1)S(1)} %pack.1.own_ref.refs_2_), channel_id=1, source_target_pairs={{0,1},{1,2},{2,3},{3,4},{4,5},{5,6},{6,7},{7,8},{8,9},{9,10},{10,1... | collective-permute-start | bytes 405512 | tf_op jit(solution)/shard_map/ppermute | solution.py:24
  12.6 20.7 %collective-permute-start.4 = (bf16[512,128]{1,0:T(8,128)(2,1)S(1)}, bf16[512,128]{1,0:T(8,128)(2,1)S(1)}, u32[]{:S(2)}, u32[]{:S(2)}) collective-permute-start(bf16[512,128]{1,0:T(8,128)(2,1)S(1)} %get-tuple-element.31.own_ref.refs_7_), channel_id=1, source_target_pairs={{0,2},{1,3},{2,4},{3,5},{4,6},{5,7},{6,8},{7,9},{8,10},{9,11},{10,... | collective-permute-start | bytes 393224 | tf_op jit(solution)/shard_map/ppermute | solution.py:24
  19.0 14.3 %collective-permute-start.5 = (bf16[512,128]{1,0:T(8,128)(2,1)S(1)}, bf16[512,128]{1,0:T(8,128)(2,1)S(1)}, u32[]{:S(2)}, u32[]{:S(2)}) collective-permute-start(bf16[512,128]{1,0:T(8,128)(2,1)S(1)} %get-tuple-element.31.own_ref.refs_7_), channel_id=1, source_target_pairs={{0,1},{1,2},{2,3},{3,4},{4,5},{5,6},{6,7},{7,8},{8,9},{9,10},{10,1... | collective-permute-start | bytes 393224 | tf_op jit(solution)/shard_map/ppermute | solution.py:24
  26.6 16.3 %collective-permute-start.2 = (bf16[256,256]{1,0:T(8,128)(2,1)S(1)}, bf16[256,256]{1,0:T(8,128)(2,1)S(1)}, u32[]{:S(2)}, u32[]{:S(2)}) collective-permute-start(bf16[256,256]{1,0:T(8,128)(2,1)S(1)} %get-tuple-element.27), channel_id=1, source_target_pairs={{2,0},{3,1},{4,2},{5,3},{6,4},{7,5},{8,6},{9,7},{10,8},{11,9},{12,... | collective-permute-start | bytes 393224 | tf_op jit(solution)/shard_map/ppermute | solution.py:24
  30.8 12.1 %collective-permute-start.3 = (bf16[256,256]{1,0:T(8,128)(2,1)S(1)}, bf16[256,256]{1,0:T(8,128)(2,1)S(1)}, u32[]{:S(2)}, u32[]{:S(2)}) collective-permute-start(bf16[256,256]{1,0:T(8,128)(2,1)S(1)} %get-tuple-element.28), channel_id=1, source_target_pairs={{1,0},{2,1},{3,2},{4,3},{5,4},{6,5},{7,6},{8,7},{9,8},{10,9},{11,1... | collective-permute-start | bytes 393224 | tf_op jit(solution)/shard_map/ppermute | solution.py:24
  35.7 11.8 %collective-permute-start.6 = (bf16[256,256]{1,0:T(8,128)(2,1)S(1)}, bf16[256,256]{1,0:T(8,128)(2,1)S(1)}, u32[]{:S(2)}, u32[]{:S(2)}) collective-permute-start(bf16[256,256]{1,0:T(8,128)(2,1)S(1)} %get-tuple-element.37), channel_id=1, source_target_pairs={{2,0},{3,1},{4,2},{5,3},{6,4},{7,5},{8,6},{9,7},{10,8},{11,9},{12,... | collective-permute-start | bytes 393224 | tf_op jit(solution)/shard_map/ppermute | solution.py:24
  40.1 10.0 %collective-permute-start.7 = (bf16[256,256]{1,0:T(8,128)(2,1)S(1)}, bf16[256,256]{1,0:T(8,128)(2,1)S(1)}, u32[]{:S(2)}, u32[]{:S(2)}) collective-permute-start(bf16[256,256]{1,0:T(8,128)(2,1)S(1)} %get-tuple-element.38), channel_id=1, source_target_pairs={{1,0},{2,1},{3,2},{4,3},{5,4},{6,5},{7,6},{8,7},{9,8},{10,9},{11,1... | collective-permute-start | bytes 393224 | tf_op jit(solution)/shard_map/ppermute | solution.py:24

commit v7 on v6

--- a/solution.py
+++ b/solution.py
@@ -141,12 +141,12 @@
             top = jnp.max(jnp.maximum(s_mix, s_one), axis=0, keepdims=True)
             e_mix = jnp.exp2((s_mix - top) * factor)
             e_one = jnp.exp2((s_one - top) * factor)
+            d_mix = jnp.where(tri, dp[0:tokens], dp[2 * tokens :])
+            d_one = dp[tokens : 2 * tokens]
             inverse = 1.0 / jnp.sum(e_mix + e_one, axis=0, keepdims=True)
+            delta = jnp.sum(e_mix * d_mix + e_one * d_one, axis=0, keepdims=True) * inverse
             p_mix = e_mix * inverse
             p_one = e_one * inverse
-            d_mix = jnp.where(tri, dp[0:tokens], dp[2 * tokens :])
-            d_one = dp[tokens : 2 * tokens]
-            delta = jnp.sum(p_mix * d_mix + p_one * d_one, axis=0, keepdims=True)
             ds_mix = (p_mix * (d_mix - delta)).astype(jnp.bfloat16)
             ds_one = (p_one * (d_one - delta)).astype(jnp.bfloat16)
             p_mix = p_mix.astype(jnp.bfloat16)

time: 51.5 us -> 51.5 us (level)
  no operation moved by 1% of the time
where the time goes in v7:
time: 51.5 us; the launch traced here: 50.9 us
  starting transfers between devices  33 us (64%)
  Pallas kernels  10.7 us (21%)
  waiting for transfers between devices  6.3 us (12%)
  between operations  0.77 us (1%)
    ppermute x8, starting transfers between devices, shift(): lax.ppermute(value, AXES, [(i, i + steps) for i in range(first, last)])  33 us
    ppermute x8, waiting for transfers between devices, shift(): lax.ppermute(value, AXES, [(i, i + steps) for i in range(first, last)])  6.3 us
    pallas_call x2, Pallas kernels, score_call(): pl.pallas_call(functools.partial(score_kernel, group, tokens, scale, know...  4.83 us
    pallas_call x1, Pallas kernels, rest_call(): pl.pallas_call(functools.partial(rest_kernel, group, tokens, scale), out_...  2.26 us
    pallas_call x1, Pallas kernels, turn_call(): pl.pallas_call(functools.partial(turn_kernel, group), in_specs=[pl.BlockS...  2.07 us
  transfers between devices with their start and end apart: 8, of which 3 were waited for; matrix products, arithmetic and copies ran while one was open for 0% of the time, Pallas kernels for 18%

profile of v7, /device:TPU:4, one launch (start us, length us, event | category | flops | bytes accessed | tf_op | source)
XLA Modules:
  0.0 50.9 jit_solution(14169058775940924119)
XLA Ops:
  0.6 0.9 %pack.1.own_ref.refs_2_ = bf16[528,128]{1,0:T(8,128)(2,1)S(1)} custom-call(bf16[128,512]{1,0:T(8,128)(2,1)} %k_ref.3, bf16[128,512]{1,0:T(8,128)(2,1)} %v_ref.3, s32[128]{0:T(128)} %seg_ref.1), custom_call_target="tpu_custom_call" | custom-call | bytes 262144 | tf_op jit(solution)/shard_map/pack/pallas_call | solution.py:253
  1.5 5.2 %collective-permute-start = (bf16[528,128]{1,0:T(8,128)(2,1)S(1)}, bf16[528,128]{1,0:T(8,128)(2,1)S(1)}, u32[]{:S(2)}, u32[]{:S(2)}) collective-permute-start(bf16[528,128]{1,0:T(8,128)(2,1)S(1)} %pack.1.own_ref.refs_2_), channel_id=1, source_target_pairs={{0,2},{1,3},{2,4},{3,5},{4,6},{5,7},{6,8},{7,9},{8,10},{9,11},{10,... | collective-permute-start | bytes 405512 | tf_op jit(solution)/shard_map/ppermute | solution.py:24
  6.7 3.8 %collective-permute-start.1 = (bf16[528,128]{1,0:T(8,128)(2,1)S(1)}, bf16[528,128]{1,0:T(8,128)(2,1)S(1)}, u32[]{:S(2)}, u32[]{:S(2)}) collective-permute-start(bf16[528,128]{1,0:T(8,128)(2,1)S(1)} %pack.1.own_ref.refs_2_), channel_id=1, source_target_pairs={{0,1},{1,2},{2,3},{3,4},{4,5},{5,6},{6,7},{7,8},{8,9},{9,10},{10,1... | collective-permute-start | bytes 405512 | tf_op jit(solution)/shard_map/ppermute | solution.py:24
  10.5 2.1 %turn.1 = (bf16[128,4096]{1,0:T(8,128)(2,1)S(1)}, bf16[128,4096]{1,0:T(8,128)(2,1)S(1)}, bf16[128,4096]{1,0:T(8,128)(2,1)S(1)}, bf16[128,4096]{1,0:T(8,128)(2,1)S(1)}, bf16[512,128]{1,0:T(8,128)(2,1)S(1)}) custom-call(bf16[128,4096]{1,0:T(8,128)(2,1)} %q_ref.1, bf16[128,4096]{1,0:T(8,128)(2,1)} %g_ref.1, bf16[128,512]{1,0:T(8,128)(2,1)} %k_ref.3, ...), custom_call_target="tpu_custom_call" | custom-call | bytes 8388608 | tf_op jit(solution)/shard_map/turn/pallas_call | solution.py:271
  12.6 6.4 %collective-permute-start.4 = (bf16[512,128]{1,0:T(8,128)(2,1)S(1)}, bf16[512,128]{1,0:T(8,128)(2,1)S(1)}, u32[]{:S(2)}, u32[]{:S(2)}) collective-permute-start(bf16[512,128]{1,0:T(8,128)(2,1)S(1)} %get-tuple-element.31.own_ref.refs_7_), channel_id=1, source_target_pairs={{0,2},{1,3},{2,4},{3,5},{4,6},{5,7},{6,8},{7,9},{8,10},{9,11},{10,... | collective-permute-start | bytes 393224 | tf_op jit(solution)/shard_map/ppermute | solution.py:24
  19.0 3.8 %collective-permute-start.5 = (bf16[512,128]{1,0:T(8,128)(2,1)S(1)}, bf16[512,128]{1,0:T(8,128)(2,1)S(1)}, u32[]{:S(2)}, u32[]{:S(2)}) collective-permute-start(bf16[512,128]{1,0:T(8,128)(2,1)S(1)} %get-tuple-element.31.own_ref.refs_7_), channel_id=1, source_target_pairs={{0,1},{1,2},{2,3},{3,4},{4,5},{5,6},{6,7},{7,8},{8,9},{9,10},{10,1... | collective-permute-start | bytes 393224 | tf_op jit(solution)/shard_map/ppermute | solution.py:24
  22.8 0.0 collective-permute-done.two_ref.refs_3_
  22.8 1.3 %collective-permute-done.1.one_ref.refs_4_ = bf16[528,128]{1,0:T(8,128)(2,1)S(1)} collective-permute-done((bf16[528,128]{1,0:T(8,128)(2,1)S(1)}, bf16[528,128]{1,0:T(8,128)(2,1)S(1)}, u32[]{:S(2)}, u32[]{:S(2)}) %collective-permute-start.1) | collective-permute-done | bytes 135200 | tf_op jit(solution)/shard_map/ppermute | solution.py:24
  24.2 2.4 %scores.2 = (bf16[128,2048]{1,0:T(8,128)(2,1)S(1)}, bf16[256,2048]{1,0:T(8,128)(2,1)S(1)}, bf16[256,256]{1,0:T(8,128)(2,1)S(1)}, bf16[256,256]{1,0:T(8,128)(2,1)S(1)}, f32[256,128]{1,0:T(8,128)S(1)}) custom-call(bf16[128,4096]{1,0:T(8,128)(2,1)S(1)} %get-tuple-element.23.q_ref, bf16[128,4096]{1,0:T(8,128)(2,1)S(1)} %get-tuple-element.24.g_ref, ...), custom_call_target="tpu_custom_call" | custom-call | flops 805306368 | bytes 3145728 | tf_op jit(solution)/shard_map/scores/pallas_call | solution.py:286
  26.6 4.2 %collective-permute-start.2 = (bf16[256,256]{1,0:T(8,128)(2,1)S(1)}, bf16[256,256]{1,0:T(8,128)(2,1)S(1)}, u32[]{:S(2)}, u32[]{:S(2)}) collective-permute-start(bf16[256,256]{1,0:T(8,128)(2,1)S(1)} %get-tuple-element.27), channel_id=1, source_target_pairs={{2,0},{3,1},{4,2},{5,3},{6,4},{7,5},{8,6},{9,7},{10,8},{11,9},{12,... | collective-permute-start | bytes 393224 | tf_op jit(solution)/shard_map/ppermute | solution.py:24
  30.8 2.5 %collective-permute-start.3 = (bf16[256,256]{1,0:T(8,128)(2,1)S(1)}, bf16[256,256]{1,0:T(8,128)(2,1)S(1)}, u32[]{:S(2)}, u32[]{:S(2)}) collective-permute-start(bf16[256,256]{1,0:T(8,128)(2,1)S(1)} %get-tuple-element.28), channel_id=1, source_target_pairs={{1,0},{2,1},{3,2},{4,3},{5,4},{6,5},{7,6},{8,7},{9,8},{10,9},{11,1... | collective-permute-start | bytes 393224 | tf_op jit(solution)/shard_map/ppermute | solution.py:24
  33.3 0.0 collective-permute-done.4.two_ref.refs_8_
  33.3 0.0 collective-permute-done.5.one_ref.refs_9_
  33.3 2.4 %scores.3 = (bf16[128,2048]{1,0:T(8,128)(2,1)S(1)}, bf16[256,2048]{1,0:T(8,128)(2,1)S(1)}, bf16[256,256]{1,0:T(8,128)(2,1)S(1)}, bf16[256,256]{1,0:T(8,128)(2,1)S(1)}) custom-call(bf16[128,4096]{1,0:T(8,128)(2,1)S(1)} %get-tuple-element.23.q_ref, bf16[128,4096]{1,0:T(8,128)(2,1)S(1)} %get-tuple-element.24.g_ref, ...), custom_call_target="tpu_custom_call" | custom-call | flops 805306368 | bytes 3145728 | tf_op jit(solution)/shard_map/scores/pallas_call | solution.py:286
  35.8 4.4 %collective-permute-start.6 = (bf16[256,256]{1,0:T(8,128)(2,1)S(1)}, bf16[256,256]{1,0:T(8,128)(2,1)S(1)}, u32[]{:S(2)}, u32[]{:S(2)}) collective-permute-start(bf16[256,256]{1,0:T(8,128)(2,1)S(1)} %get-tuple-element.37), channel_id=1, source_target_pairs={{2,0},{3,1},{4,2},{5,3},{6,4},{7,5},{8,6},{9,7},{10,8},{11,9},{12,... | collective-permute-start | bytes 393224 | tf_op jit(solution)/shard_map/ppermute | solution.py:24
  40.2 2.7 %collective-permute-start.7 = (bf16[256,256]{1,0:T(8,128)(2,1)S(1)}, bf16[256,256]{1,0:T(8,128)(2,1)S(1)}, u32[]{:S(2)}, u32[]{:S(2)}) collective-permute-start(bf16[256,256]{1,0:T(8,128)(2,1)S(1)} %get-tuple-element.38), channel_id=1, source_target_pairs={{1,0},{2,1},{3,2},{4,3},{5,4},{6,5},{7,6},{8,7},{9,8},{10,9},{11,1... | collective-permute-start | bytes 393224 | tf_op jit(solution)/shard_map/ppermute | solution.py:24
  42.9 0.0 collective-permute-done.2.far_ref
  42.9 0.0 collective-permute-done.3.near_ref
  42.9 2.3 %rest.1 = (bf16[128,4096]{1,0:T(8,128)(2,1)}, bf16[128,512]{1,0:T(8,128)(2,1)}, bf16[128,512]{1,0:T(8,128)(2,1)}, f32[256,256]{1,0:T(8,128)S(1)}) custom-call(bf16[128,4096]{1,0:T(8,128)(2,1)S(1)} %get-tuple-element.23.q_ref, bf16[128,4096]{1,0:T(8,128)(2,1)S(1)} %get-tuple-element.24.g_ref, bf16[256,256]{1,0:T(8,128)(2,1)S(1)} %collective-permute-done.2.far_ref, ...), custom_call_target="tpu_custom_call" | custom-call | flops 805306368 | bytes 6291456 | tf_op jit(solution)/shard_map/rest/pallas_call | solution.py:308
  45.2 2.5 %collective-permute-done.6.far_ref = bf16[256,256]{1,0:T(8,128)(2,1)S(1)} collective-permute-done((bf16[256,256]{1,0:T(8,128)(2,1)S(1)}, bf16[256,256]{1,0:T(8,128)(2,1)S(1)}, u32[]{:S(2)}, u32[]{:S(2)}) %collective-permute-start.6) | collective-permute-done | bytes 131104 | tf_op jit(solution)/shard_map/ppermute | solution.py:24
  47.7 2.5 %collective-permute-done.7.near_ref = bf16[256,256]{1,0:T(8,128)(2,1)S(1)} collective-permute-done((bf16[256,256]{1,0:T(8,128)(2,1)S(1)}, bf16[256,256]{1,0:T(8,128)(2,1)S(1)}, u32[]{:S(2)}, u32[]{:S(2)}) %collective-permute-start.7) | collective-permute-done | bytes 131104 | tf_op jit(solution)/shard_map/ppermute | solution.py:24
  50.1 0.7 %final.1 = (bf16[128,512]{1,0:T(8,128)(2,1)}, bf16[128,512]{1,0:T(8,128)(2,1)}) custom-call(f32[256,256]{1,0:T(8,128)S(1)} %get-tuple-element.36.own_ref, bf16[256,256]{1,0:T(8,128)(2,1)S(1)} %collective-permute-done.6.far_ref, bf16[256,256]{1,0:T(8,128)(2,1)S(1)} %collective-permute-done.7.near_ref, ...), custom_call_target="tpu_custom_call", output_to_operand_aliasing={{0}: (3, {}), {1}: (4, {})} | custom-call | bytes 1048576 | tf_op jit(solution)/shard_map/final/pallas_call | solution.py:325
Async XLA Ops:
  1.5 21.3 %collective-permute-start = (bf16[528,128]{1,0:T(8,128)(2,1)S(1)}, bf16[528,128]{1,0:T(8,128)(2,1)S(1)}, u32[]{:S(2)}, u32[]{:S(2)}) collective-permute-start(bf16[528,128]{1,0:T(8,128)(2,1)S(1)} %pack.1.own_ref.refs_2_), channel_id=1, source_target_pairs={{0,2},{1,3},{2,4},{3,5},{4,6},{5,7},{6,8},{7,9},{8,10},{9,11},{10,... | collective-permute-start | bytes 405512 | tf_op jit(solution)/shard_map/ppermute | solution.py:24
  6.7 17.5 %collective-permute-start.1 = (bf16[528,128]{1,0:T(8,128)(2,1)S(1)}, bf16[528,128]{1,0:T(8,128)(2,1)S(1)}, u32[]{:S(2)}, u32[]{:S(2)}) collective-permute-start(bf16[528,128]{1,0:T(8,128)(2,1)S(1)} %pack.1.own_ref.refs_2_), channel_id=1, source_target_pairs={{0,1},{1,2},{2,3},{3,4},{4,5},{5,6},{6,7},{7,8},{8,9},{9,10},{10,1... | collective-permute-start | bytes 405512 | tf_op jit(solution)/shard_map/ppermute | solution.py:24
  12.6 20.7 %collective-permute-start.4 = (bf16[512,128]{1,0:T(8,128)(2,1)S(1)}, bf16[512,128]{1,0:T(8,128)(2,1)S(1)}, u32[]{:S(2)}, u32[]{:S(2)}) collective-permute-start(bf16[512,128]{1,0:T(8,128)(2,1)S(1)} %get-tuple-element.31.own_ref.refs_7_), channel_id=1, source_target_pairs={{0,2},{1,3},{2,4},{3,5},{4,6},{5,7},{6,8},{7,9},{8,10},{9,11},{10,... | collective-permute-start | bytes 393224 | tf_op jit(solution)/shard_map/ppermute | solution.py:24
  19.0 14.3 %collective-permute-start.5 = (bf16[512,128]{1,0:T(8,128)(2,1)S(1)}, bf16[512,128]{1,0:T(8,128)(2,1)S(1)}, u32[]{:S(2)}, u32[]{:S(2)}) collective-permute-start(bf16[512,128]{1,0:T(8,128)(2,1)S(1)} %get-tuple-element.31.own_ref.refs_7_), channel_id=1, source_target_pairs={{0,1},{1,2},{2,3},{3,4},{4,5},{5,6},{6,7},{7,8},{8,9},{9,10},{10,1... | collective-permute-start | bytes 393224 | tf_op jit(solution)/shard_map/ppermute | solution.py:24
  26.6 16.3 %collective-permute-start.2 = (bf16[256,256]{1,0:T(8,128)(2,1)S(1)}, bf16[256,256]{1,0:T(8,128)(2,1)S(1)}, u32[]{:S(2)}, u32[]{:S(2)}) collective-permute-start(bf16[256,256]{1,0:T(8,128)(2,1)S(1)} %get-tuple-element.27), channel_id=1, source_target_pairs={{2,0},{3,1},{4,2},{5,3},{6,4},{7,5},{8,6},{9,7},{10,8},{11,9},{12,... | collective-permute-start | bytes 393224 | tf_op jit(solution)/shard_map/ppermute | solution.py:24
  30.8 12.1 %collective-permute-start.3 = (bf16[256,256]{1,0:T(8,128)(2,1)S(1)}, bf16[256,256]{1,0:T(8,128)(2,1)S(1)}, u32[]{:S(2)}, u32[]{:S(2)}) collective-permute-start(bf16[256,256]{1,0:T(8,128)(2,1)S(1)} %get-tuple-element.28), channel_id=1, source_target_pairs={{1,0},{2,1},{3,2},{4,3},{5,4},{6,5},{7,6},{8,7},{9,8},{10,9},{11,1... | collective-permute-start | bytes 393224 | tf_op jit(solution)/shard_map/ppermute | solution.py:24
  35.8 11.9 %collective-permute-start.6 = (bf16[256,256]{1,0:T(8,128)(2,1)S(1)}, bf16[256,256]{1,0:T(8,128)(2,1)S(1)}, u32[]{:S(2)}, u32[]{:S(2)}) collective-permute-start(bf16[256,256]{1,0:T(8,128)(2,1)S(1)} %get-tuple-element.37), channel_id=1, source_target_pairs={{2,0},{3,1},{4,2},{5,3},{6,4},{7,5},{8,6},{9,7},{10,8},{11,9},{12,... | collective-permute-start | bytes 393224 | tf_op jit(solution)/shard_map/ppermute | solution.py:24
  40.2 10.0 %collective-permute-start.7 = (bf16[256,256]{1,0:T(8,128)(2,1)S(1)}, bf16[256,256]{1,0:T(8,128)(2,1)S(1)}, u32[]{:S(2)}, u32[]{:S(2)}) collective-permute-start(bf16[256,256]{1,0:T(8,128)(2,1)S(1)} %get-tuple-element.38), channel_id=1, source_target_pairs={{1,0},{2,1},{3,2},{4,3},{5,4},{6,5},{7,6},{8,7},{9,8},{10,9},{11,1... | collective-permute-start | bytes 393224 | tf_op jit(solution)/shard_map/ppermute | solution.py:24

commit v8 on v7

--- a/solution.py
+++ b/solution.py
@@ -75,17 +75,24 @@
         copy.wait()
 
 
-def turn_kernel(group, q_ref, g_ref, k_ref, v_ref, q_out, g_out, qt_ref, gt_ref, kv_out, sems, kv_sems):
+def turn_kernel(group, chunk, q_ref, g_ref, *refs):
+    halves = []
+    if chunk == 0:
+        k_ref, v_ref, q_out, g_out, qt_ref, gt_ref, kv_out, sems, kv_sems = refs
+        halves = payload_copies(1, q_ref.shape[0], k_ref, v_ref, kv_out, kv_sems)
+    else:
+        q_out, g_out, qt_ref, gt_ref, sems = refs
     width = group * HD
-    halves = payload_copies(1, q_ref.shape[0], k_ref, v_ref, kv_out, kv_sems)
+    count = HK // CHUNKS
     copies = []
-    for part in range(HK):
-        cols = pl.ds(part * width, width)
+    for part in range(count):
+        there = pl.ds((chunk * count + part) * width, width)
+        here = pl.ds(part * width, width)
         for side, (source, target) in enumerate(((q_ref, q_out), (g_ref, g_out))):
-            copies.append(pltpu.make_async_copy(source.at[:, cols], target.at[:, cols], sems.at[2 * part + side]))
+            copies.append(pltpu.make_async_copy(source.at[:, there], target.at[:, here], sems.at[2 * part + side]))
     for copy in halves + copies:
         copy.start()
-    for part in range(HK):
+    for part in range(count):
         for side, (source, target) in enumerate(((q_out, qt_ref), (g_out, gt_ref))):
             copies[2 * part + side].wait()
             for h in range(group):
@@ -95,7 +102,7 @@
         copy.wait()
 
 
-def score_kernel(group, tokens, scale, known, offset, q_ref, g_ref, qt_ref, gt_ref, own_ref, two_ref, one_ref, *refs):
+def score_kernel(group, tokens, scale, known, q_ref, g_ref, qt_ref, gt_ref, own_ref, one_ref, two_ref, *refs):
     p_ref, ds_ref, far_ref, near_ref = refs[1:] if known else refs[:-1]
     bias_ref = refs[0] if known else refs[-1]
     tri = sees_own(tokens, 1)
@@ -123,7 +130,7 @@
             jnp.concatenate([ref[first : first + tokens, :] for ref in (own_ref, one_ref, two_ref)], axis=0)
             for first in (part * tokens, (count + part) * tokens)
         ]
-        first = offset * group * HD + unit * wide
+        first = unit * wide
         return dot(keys, qt_ref[:, first : first + wide]), dot(vals, gt_ref[:, first : first + wide])
 
     ahead = products(0)
@@ -154,7 +161,7 @@
             p_ref[:, cols] = p_mix
             ds_ref[0:tokens, cols] = ds_mix
             ds_ref[tokens : 2 * tokens, cols] = ds_one
-            first = offset * group + unit * UNIT
+            first = unit * UNIT
             sum_k = sum_k + dot(jnp.concatenate([ds_one, ds_mix * far_mask], axis=0), stacked(q_ref, first, UNIT))
             sum_v = sum_v + dot(jnp.concatenate([p_one, p_mix * far_mask], axis=0), stacked(g_ref, first, UNIT))
         sum_k = sum_k * scale
@@ -178,8 +185,8 @@
     return copies
 
 
-def rest_kernel(group, tokens, scale, q_ref, g_ref, far_ref, near_ref, *refs):
-    per = 5
+def rest_kernel(group, tokens, scale, far_ref, near_ref, *refs):
+    per = 7
     chunk_refs = [refs[per * c : per * (c + 1)] for c in range(CHUNKS)]
     dq_out, k_out, v_out, own_out, dq_ref, kv_ref, sems, kv_sems = refs[per * CHUNKS :]
     tri = sees_own(tokens, 2)
@@ -188,7 +195,7 @@
     wide = group * HD
     count = HK // CHUNKS
     copies = []
-    for chunk, (p_ref, ds_ref, own_ref, two_ref, one_ref) in enumerate(chunk_refs):
+    for chunk, (q_ref, g_ref, p_ref, ds_ref, own_ref, two_ref, one_ref) in enumerate(chunk_refs):
         sums = []
         for part in range(count):
             block = slice(part * tokens, (part + 1) * tokens)
@@ -197,7 +204,7 @@
             sum_v = jnp.zeros((tokens, HD), jnp.float32)
             for pair in range(group // 2):
                 cols = slice(part * wide + pair * 2 * HD, part * wide + (pair + 1) * 2 * HD)
-                first = (chunk * count + part) * group + 2 * pair
+                first = part * group + 2 * pair
                 ds_mix = ds_ref[0:tokens, cols]
                 ds_own = ds_mix * own_mask
                 sum_k = sum_k + dot(ds_own, stacked(q_ref, first, 2))
@@ -205,9 +212,8 @@
                 rows = jnp.concatenate([ds_own, ds_ref[tokens : 2 * tokens, cols], ds_mix * far_mask], axis=0)
                 dq_t = (dot(keys_t, rows) * scale).astype(jnp.bfloat16)
                 for h in range(2):
-                    dq_ref[:, (first + h) * HD : (first + h + 1) * HD] = jnp.transpose(
-                        dq_t[:, h * HD : (h + 1) * HD]
-                    )
+                    at = (chunk * count * group + first + h) * HD
+                    dq_ref[:, at : at + HD] = jnp.transpose(dq_t[:, h * HD : (h + 1) * HD])
             sums.append(jnp.concatenate([sum_k * scale, sum_v], axis=0))
             index = chunk * count + part
             span = pl.ds(index * wide, wide)
@@ -265,26 +271,28 @@
     )(*in_hbm(key_states, value_states, segment_ids))
 
 
-def turn_call(q, g, key_states, value_states, group):
-    tokens, span = q.shape
-    count = HK // CHUNKS
-    return pl.pallas_call(
-        functools.partial(turn_kernel, group),
-        in_specs=[pl.BlockSpec(memory_space=pltpu.HBM)] * 4,
-        out_shape=[bf16(tokens, span)] * 2 + [bf16(HD, span)] * 2 + [bf16(2 * count * tokens, HD)],
-        scratch_shapes=[pltpu.SemaphoreType.DMA((2 * HK,)), pltpu.SemaphoreType.DMA((2 * count,))],
+def turn_call(chunk, group, q, g, *key_value):
+    tokens, count = q.shape[0], HK // CHUNKS
+    span = count * group * HD
+    return pl.pallas_call(
+        functools.partial(turn_kernel, group, chunk),
+        in_specs=[pl.BlockSpec(memory_space=pltpu.HBM)] * (2 + len(key_value)),
+        out_shape=[bf16(tokens, span)] * 2
+        + [bf16(HD, span)] * 2
+        + [bf16(2 * count * tokens, HD)] * (len(key_value) // 2),
+        scratch_shapes=[pltpu.SemaphoreType.DMA((2 * count,))] * (1 + len(key_value) // 2),
         cost_estimate=cost(0, 16 * tokens * span),
         compiler_params=PARAMS,
         name="turn",
-    )(*in_hbm(q, g, key_states, value_states))
-
-
-def score_call(q, g, qt, gt, own, two, one, bias, offset, group, tokens, scale):
+    )(*in_hbm(q, g, *key_value))
+
+
+def score_call(q, g, qt, gt, own, one, two, bias, group, tokens, scale):
     count = HK // CHUNKS
     span = count * group * HD
     known = bias is not None
     return pl.pallas_call(
-        functools.partial(score_kernel, group, tokens, scale, known, offset),
+        functools.partial(score_kernel, group, tokens, scale, known),
         out_shape=[
             bf16(tokens, span),
             bf16(2 * tokens, span),
@@ -295,30 +303,31 @@
         cost_estimate=cost(2 * tokens * 3 * span * tokens * 4, 12 * tokens * span, 2 * tokens * span),
         compiler_params=PARAMS,
         name="scores",
-    )(q, g, qt, gt, own, two, one, *([bias] if known else []))
+    )(q, g, qt, gt, own, one, two, *([bias] if known else []))
 
 
 ON_CHIP = pl.BlockSpec(memory_space=pltpu.VMEM)
 IN_HBM = pl.BlockSpec(memory_space=pltpu.HBM)
 
 
-def rest_call(q, g, far, near, parts, group, tokens, scale):
+def rest_call(far, near, parts, group, tokens, scale):
     grads = bf16(tokens, HK * HD)
+    span = HK * group * HD
     chunk = (2 * tokens, HK // CHUNKS * HD)
     return pl.pallas_call(
         functools.partial(rest_kernel, group, tokens, scale),
         out_specs=[IN_HBM] * 3 + [ON_CHIP],
-        out_shape=[bf16(*q.shape), grads, grads, f32(*chunk)],
+        out_shape=[bf16(tokens, span), grads, grads, f32(*chunk)],
         scratch_shapes=[
-            pltpu.VMEM(q.shape, jnp.bfloat16),
+            pltpu.VMEM((tokens, span), jnp.bfloat16),
             pltpu.VMEM(chunk, jnp.bfloat16),
             pltpu.SemaphoreType.DMA((HK,)),
             pltpu.SemaphoreType.DMA((2,)),
         ],
-        cost_estimate=cost(2 * tokens * 3 * q.shape[1] * tokens * 2, 12 * tokens * q.shape[1]),
+        cost_estimate=cost(2 * tokens * 3 * span * tokens * 2, 12 * tokens * span),
         compiler_params=PARAMS,
         name="rest",
-    )(q, g, far, near, *[x for part in parts for x in part])
+    )(far, near, *[x for part in parts for x in part])
 
 
 def final_call(own, far, near, key_grad, value_grad):
@@ -340,21 +349,24 @@
     group = queries.shape[1] // (HK * HD)
     scale = HD ** (-0.5)
     chunks = range(CHUNKS)
-    step = HK // CHUNKS
     own = [pack_call(key_states, value_states, segment_ids)]
-    q, g, qt, gt, later = turn_call(queries, out_grad, key_states, value_states, group)
+    *turned, later = turn_call(0, group, queries, out_grad, key_states, value_states)
     own.append(later)
     two = [shift(x, 2) for x in own]
     one = [shift(x, 1) for x in own]
-    first, near, far, bias = [], [], [], None
+    sides, first, near, far, bias = [], [], [], [], None
     for c in chunks:
-        results = score_call(q, g, qt, gt, own[c], two[c], one[c], bias, c * step, group, tokens, scale)
-        bias = results[4] if bias is None else bias
+        sides.append(turned)
+        results = score_call(*turned, own[c], one[c], two[c], bias, group, tokens, scale)
+        if c == 0:
+            bias, queries, out_grad = lax.optimization_barrier((results[4], queries, out_grad))
+            turned = turn_call(1, group, queries, out_grad)
         first.append(results)
         far.append(shift(results[2], -2))
         near.append(shift(results[3], -1))
     query_grad, key_grad, value_grad, own_terms = rest_call(
-        q, g, far[0], near[0], [(first[c][0], first[c][1], own[c], two[c], one[c]) for c in chunks],
+        far[0], near[0],
+        [(sides[c][0], sides[c][1], first[c][0], first[c][1], own[c], two[c], one[c]) for c in chunks],
         group, tokens, scale,
     )
     key_grad, value_grad = final_call(own_terms, far[1], near[1], key_grad, value_grad)

time: 51.5 us -> 53 us (1.029)
  Pallas kernels: 10.7 us -> 11.6 us
  waiting for transfers between devices: 6.3 us -> 6.83 us
    pallas_call x1 -> x2, Pallas kernels: 2.07 us -> 3.04 us  [turn_call(): pl.pallas_call(functools.partial(turn_kernel, group, chunk), in_specs=[pl...]
  transfers between devices with their start and end apart: 8 -> 8, of which waited for: 3 -> 3; matrix products, arithmetic and copies ran while one was open for 0% -> 0% of each run, Pallas kernels for 18% -> 19%
where the time goes in v8:
time: 53 us; the launch traced here: 52.4 us
  starting transfers between devices  33.2 us (63%)
  Pallas kernels  11.6 us (22%)
  waiting for transfers between devices  6.83 us (13%)
  between operations  0.78 us (1%)
    ppermute x8, starting transfers between devices, shift(): lax.ppermute(value, AXES, [(i, i + steps) for i in range(first, last)])  33.2 us
    ppermute x8, waiting for transfers between devices, shift(): lax.ppermute(value, AXES, [(i, i + steps) for i in range(first, last)])  6.83 us
    pallas_call x2, Pallas kernels, score_call(): pl.pallas_call(functools.partial(score_kernel, group, tokens, scale, know...  4.73 us
    pallas_call x2, Pallas kernels, turn_call(): pl.pallas_call(functools.partial(turn_kernel, group, chunk), in_specs=[pl...  3.04 us
    pallas_call x1, Pallas kernels, rest_call(): pl.pallas_call(functools.partial(rest_kernel, group, tokens, scale), out_...  2.25 us
  transfers between devices with their start and end apart: 8, of which 3 were waited for; matrix products, arithmetic and copies ran while one was open for 0% of the time, Pallas kernels for 19%

profile of v8, /device:TPU:4, one launch (start us, length us, event | category | flops | bytes accessed | tf_op | source)
XLA Modules:
  0.0 52.4 jit_solution(11301924231903400843)
XLA Ops:
  0.6 0.9 %pack.1.own_ref.refs_4_ = bf16[528,128]{1,0:T(8,128)(2,1)S(1)} custom-call(bf16[128,512]{1,0:T(8,128)(2,1)} %k_ref.1, bf16[128,512]{1,0:T(8,128)(2,1)} %v_ref.1, s32[128]{0:T(128)} %seg_ref.1), custom_call_target="tpu_custom_call" | custom-call | bytes 262144 | tf_op jit(solution)/shard_map/pack/pallas_call | solution.py:259
  1.5 5.2 %collective-permute-start.1 = (bf16[528,128]{1,0:T(8,128)(2,1)S(1)}, bf16[528,128]{1,0:T(8,128)(2,1)S(1)}, u32[]{:S(2)}, u32[]{:S(2)}) collective-permute-start(bf16[528,128]{1,0:T(8,128)(2,1)S(1)} %pack.1.own_ref.refs_4_), channel_id=1, source_target_pairs={{0,2},{1,3},{2,4},{3,5},{4,6},{5,7},{6,8},{7,9},{8,10},{9,11},{10,... | collective-permute-start | bytes 405512 | tf_op jit(solution)/shard_map/ppermute | solution.py:24
  6.7 3.8 %collective-permute-start = (bf16[528,128]{1,0:T(8,128)(2,1)S(1)}, bf16[528,128]{1,0:T(8,128)(2,1)S(1)}, u32[]{:S(2)}, u32[]{:S(2)}) collective-permute-start(bf16[528,128]{1,0:T(8,128)(2,1)S(1)} %pack.1.own_ref.refs_4_), channel_id=1, source_target_pairs={{0,1},{1,2},{2,3},{3,4},{4,5},{5,6},{6,7},{7,8},{8,9},{9,10},{10,1... | collective-permute-start | bytes 405512 | tf_op jit(solution)/shard_map/ppermute | solution.py:24
  10.5 1.6 %turn.2 = (bf16[128,2048]{1,0:T(8,128)(2,1)S(1)}, bf16[128,2048]{1,0:T(8,128)(2,1)S(1)}, bf16[128,2048]{1,0:T(8,128)(2,1)S(1)}, bf16[128,2048]{1,0:T(8,128)(2,1)S(1)}, bf16[512,128]{1,0:T(8,128)(2,1)S(1)}) custom-call(bf16[128,4096]{1,0:T(8,128)(2,1)} %q_ref.2, bf16[128,4096]{1,0:T(8,128)(2,1)} %g_ref.2, bf16[128,512]{1,0:T(8,128)(2,1)} %k_ref.1, ...), custom_call_target="tpu_custom_call" | custom-call | bytes 4194304 | tf_op jit(solution)/shard_map/turn/pallas_call | solution.py:277
  12.1 6.4 %collective-permute-start.5 = (bf16[512,128]{1,0:T(8,128)(2,1)S(1)}, bf16[512,128]{1,0:T(8,128)(2,1)S(1)}, u32[]{:S(2)}, u32[]{:S(2)}) collective-permute-start(bf16[512,128]{1,0:T(8,128)(2,1)S(1)} %get-tuple-element.45.own_ref.refs_11_), channel_id=1, source_target_pairs={{0,2},{1,3},{2,4},{3,5},{4,6},{5,7},{6,8},{7,9},{8,10},{9,11},{10,... | collective-permute-start | bytes 393224 | tf_op jit(solution)/shard_map/ppermute | solution.py:24
  18.5 3.8 %collective-permute-start.4 = (bf16[512,128]{1,0:T(8,128)(2,1)S(1)}, bf16[512,128]{1,0:T(8,128)(2,1)S(1)}, u32[]{:S(2)}, u32[]{:S(2)}) collective-permute-start(bf16[512,128]{1,0:T(8,128)(2,1)S(1)} %get-tuple-element.45.own_ref.refs_11_), channel_id=1, source_target_pairs={{0,1},{1,2},{2,3},{3,4},{4,5},{5,6},{6,7},{7,8},{8,9},{9,10},{10,1... | collective-permute-start | bytes 393224 | tf_op jit(solution)/shard_map/ppermute | solution.py:24
  22.3 0.0 collective-permute-done.1.two_ref.refs_5_
  22.3 1.9 %collective-permute-done.one_ref.refs_6_ = bf16[528,128]{1,0:T(8,128)(2,1)S(1)} collective-permute-done((bf16[528,128]{1,0:T(8,128)(2,1)S(1)}, bf16[528,128]{1,0:T(8,128)(2,1)S(1)}, u32[]{:S(2)}, u32[]{:S(2)}) %collective-permute-start) | collective-permute-done | bytes 135200 | tf_op jit(solution)/shard_map/ppermute | solution.py:24
  24.2 2.4 %scores.2 = (bf16[128,2048]{1,0:T(8,128)(2,1)S(1)}, bf16[256,2048]{1,0:T(8,128)(2,1)S(1)}, bf16[256,256]{1,0:T(8,128)(2,1)S(1)}, bf16[256,256]{1,0:T(8,128)(2,1)S(1)}, f32[256,128]{1,0:T(8,128)S(1)}) custom-call(bf16[128,2048]{1,0:T(8,128)(2,1)S(1)} %get-tuple-element.30.q_ref.refs_0_, bf16[128,2048]{1,0:T(8,128)(2,1)S(1)} %get-tuple-element.31.g_ref.refs_1_, ...), custom_call_target="tpu_custom_call" | custom-call | flops 805306368 | bytes 3145728 | tf_op jit(solution)/shard_map/scores/pallas_call | solution.py:294
  26.6 4.2 %collective-permute-start.2 = (bf16[256,256]{1,0:T(8,128)(2,1)S(1)}, bf16[256,256]{1,0:T(8,128)(2,1)S(1)}, u32[]{:S(2)}, u32[]{:S(2)}) collective-permute-start(bf16[256,256]{1,0:T(8,128)(2,1)S(1)} %get-tuple-element.34), channel_id=1, source_target_pairs={{2,0},{3,1},{4,2},{5,3},{6,4},{7,5},{8,6},{9,7},{10,8},{11,9},{12,... | collective-permute-start | bytes 393224 | tf_op jit(solution)/shard_map/ppermute | solution.py:24
  30.8 2.5 %collective-permute-start.3 = (bf16[256,256]{1,0:T(8,128)(2,1)S(1)}, bf16[256,256]{1,0:T(8,128)(2,1)S(1)}, u32[]{:S(2)}, u32[]{:S(2)}) collective-permute-start(bf16[256,256]{1,0:T(8,128)(2,1)S(1)} %get-tuple-element.35), channel_id=1, source_target_pairs={{1,0},{2,1},{3,2},{4,3},{5,4},{6,5},{7,6},{8,7},{9,8},{10,9},{11,1... | collective-permute-start | bytes 393224 | tf_op jit(solution)/shard_map/ppermute | solution.py:24
  33.3 1.5 %turn.3 = (bf16[128,2048]{1,0:T(8,128)(2,1)S(1)}, bf16[128,2048]{1,0:T(8,128)(2,1)S(1)}, bf16[128,2048]{1,0:T(8,128)(2,1)S(1)}, bf16[128,2048]{1,0:T(8,128)(2,1)S(1)}) custom-call(bf16[128,4096]{1,0:T(8,128)(2,1)} %q_ref.2, bf16[128,4096]{1,0:T(8,128)(2,1)} %g_ref.2), custom_call_target="tpu_custom_call" | custom-call | bytes 4194304 | tf_op jit(solution)/shard_map/turn/pallas_call | solution.py:277
  34.8 0.0 collective-permute-done.5.two_ref.refs_12_
  34.8 0.0 collective-permute-done.4.one_ref.refs_13_
  34.8 2.4 %scores.3 = (bf16[128,2048]{1,0:T(8,128)(2,1)S(1)}, bf16[256,2048]{1,0:T(8,128)(2,1)S(1)}, bf16[256,256]{1,0:T(8,128)(2,1)S(1)}, bf16[256,256]{1,0:T(8,128)(2,1)S(1)}) custom-call(bf16[128,2048]{1,0:T(8,128)(2,1)S(1)} %get-tuple-element.41.q_ref.refs_7_, bf16[128,2048]{1,0:T(8,128)(2,1)S(1)} %get-tuple-element.42.g_ref.refs_8_, ...), custom_call_target="tpu_custom_call" | custom-call | flops 805306368 | bytes 3145728 | tf_op jit(solution)/shard_map/scores/pallas_call | solution.py:294
  37.2 4.4 %collective-permute-start.6 = (bf16[256,256]{1,0:T(8,128)(2,1)S(1)}, bf16[256,256]{1,0:T(8,128)(2,1)S(1)}, u32[]{:S(2)}, u32[]{:S(2)}) collective-permute-start(bf16[256,256]{1,0:T(8,128)(2,1)S(1)} %get-tuple-element.51), channel_id=1, source_target_pairs={{2,0},{3,1},{4,2},{5,3},{6,4},{7,5},{8,6},{9,7},{10,8},{11,9},{12,... | collective-permute-start | bytes 393224 | tf_op jit(solution)/shard_map/ppermute | solution.py:24
  41.6 2.8 %collective-permute-start.7 = (bf16[256,256]{1,0:T(8,128)(2,1)S(1)}, bf16[256,256]{1,0:T(8,128)(2,1)S(1)}, u32[]{:S(2)}, u32[]{:S(2)}) collective-permute-start(bf16[256,256]{1,0:T(8,128)(2,1)S(1)} %get-tuple-element.52), channel_id=1, source_target_pairs={{1,0},{2,1},{3,2},{4,3},{5,4},{6,5},{7,6},{8,7},{9,8},{10,9},{11,1... | collective-permute-start | bytes 393224 | tf_op jit(solution)/shard_map/ppermute | solution.py:24
  44.4 0.0 collective-permute-done.2.far_ref
  44.4 0.0 collective-permute-done.3.near_ref
  44.4 2.3 %rest.1 = (bf16[128,4096]{1,0:T(8,128)(2,1)}, bf16[128,512]{1,0:T(8,128)(2,1)}, bf16[128,512]{1,0:T(8,128)(2,1)}, f32[256,256]{1,0:T(8,128)S(1)}) custom-call(bf16[256,256]{1,0:T(8,128)(2,1)S(1)} %collective-permute-done.2.far_ref, bf16[256,256]{1,0:T(8,128)(2,1)S(1)} %collective-permute-done.3.near_ref, ...), custom_call_target="tpu_custom_call" | custom-call | flops 805306368 | bytes 6291456 | tf_op jit(solution)/shard_map/rest/pallas_call | solution.py:317
  46.7 1.5 %collective-permute-done.6.far_ref = bf16[256,256]{1,0:T(8,128)(2,1)S(1)} collective-permute-done((bf16[256,256]{1,0:T(8,128)(2,1)S(1)}, bf16[256,256]{1,0:T(8,128)(2,1)S(1)}, u32[]{:S(2)}, u32[]{:S(2)}) %collective-permute-start.6) | collective-permute-done | bytes 131104 | tf_op jit(solution)/shard_map/ppermute | solution.py:24
  48.2 3.5 %collective-permute-done.7.near_ref = bf16[256,256]{1,0:T(8,128)(2,1)S(1)} collective-permute-done((bf16[256,256]{1,0:T(8,128)(2,1)S(1)}, bf16[256,256]{1,0:T(8,128)(2,1)S(1)}, u32[]{:S(2)}, u32[]{:S(2)}) %collective-permute-start.7) | collective-permute-done | bytes 131104 | tf_op jit(solution)/shard_map/ppermute | solution.py:24
  51.6 0.7 %final.1 = (bf16[128,512]{1,0:T(8,128)(2,1)}, bf16[128,512]{1,0:T(8,128)(2,1)}) custom-call(f32[256,256]{1,0:T(8,128)S(1)} %get-tuple-element.50.own_ref, bf16[256,256]{1,0:T(8,128)(2,1)S(1)} %collective-permute-done.6.far_ref, bf16[256,256]{1,0:T(8,128)(2,1)S(1)} %collective-permute-done.7.near_ref, ...), custom_call_target="tpu_custom_call", output_to_operand_aliasing={{0}: (3, {}), {1}: (4, {})} | custom-call | bytes 1048576 | tf_op jit(solution)/shard_map/final/pallas_call | solution.py:334
Async XLA Ops:
  1.5 20.8 %collective-permute-start.1 = (bf16[528,128]{1,0:T(8,128)(2,1)S(1)}, bf16[528,128]{1,0:T(8,128)(2,1)S(1)}, u32[]{:S(2)}, u32[]{:S(2)}) collective-permute-start(bf16[528,128]{1,0:T(8,128)(2,1)S(1)} %pack.1.own_ref.refs_4_), channel_id=1, source_target_pairs={{0,2},{1,3},{2,4},{3,5},{4,6},{5,7},{6,8},{7,9},{8,10},{9,11},{10,... | collective-permute-start | bytes 405512 | tf_op jit(solution)/shard_map/ppermute | solution.py:24
  6.7 17.5 %collective-permute-start = (bf16[528,128]{1,0:T(8,128)(2,1)S(1)}, bf16[528,128]{1,0:T(8,128)(2,1)S(1)}, u32[]{:S(2)}, u32[]{:S(2)}) collective-permute-start(bf16[528,128]{1,0:T(8,128)(2,1)S(1)} %pack.1.own_ref.refs_4_), channel_id=1, source_target_pairs={{0,1},{1,2},{2,3},{3,4},{4,5},{5,6},{6,7},{7,8},{8,9},{9,10},{10,1... | collective-permute-start | bytes 405512 | tf_op jit(solution)/shard_map/ppermute | solution.py:24
  12.1 22.7 %collective-permute-start.5 = (bf16[512,128]{1,0:T(8,128)(2,1)S(1)}, bf16[512,128]{1,0:T(8,128)(2,1)S(1)}, u32[]{:S(2)}, u32[]{:S(2)}) collective-permute-start(bf16[512,128]{1,0:T(8,128)(2,1)S(1)} %get-tuple-element.45.own_ref.refs_11_), channel_id=1, source_target_pairs={{0,2},{1,3},{2,4},{3,5},{4,6},{5,7},{6,8},{7,9},{8,10},{9,11},{10,... | collective-permute-start | bytes 393224 | tf_op jit(solution)/shard_map/ppermute | solution.py:24
  18.5 16.3 %collective-permute-start.4 = (bf16[512,128]{1,0:T(8,128)(2,1)S(1)}, bf16[512,128]{1,0:T(8,128)(2,1)S(1)}, u32[]{:S(2)}, u32[]{:S(2)}) collective-permute-start(bf16[512,128]{1,0:T(8,128)(2,1)S(1)} %get-tuple-element.45.own_ref.refs_11_), channel_id=1, source_target_pairs={{0,1},{1,2},{2,3},{3,4},{4,5},{5,6},{6,7},{7,8},{8,9},{9,10},{10,1... | collective-permute-start | bytes 393224 | tf_op jit(solution)/shard_map/ppermute | solution.py:24
  26.6 17.9 %collective-permute-start.2 = (bf16[256,256]{1,0:T(8,128)(2,1)S(1)}, bf16[256,256]{1,0:T(8,128)(2,1)S(1)}, u32[]{:S(2)}, u32[]{:S(2)}) collective-permute-start(bf16[256,256]{1,0:T(8,128)(2,1)S(1)} %get-tuple-element.34), channel_id=1, source_target_pairs={{2,0},{3,1},{4,2},{5,3},{6,4},{7,5},{8,6},{9,7},{10,8},{11,9},{12,... | collective-permute-start | bytes 393224 | tf_op jit(solution)/shard_map/ppermute | solution.py:24
  30.8 13.6 %collective-permute-start.3 = (bf16[256,256]{1,0:T(8,128)(2,1)S(1)}, bf16[256,256]{1,0:T(8,128)(2,1)S(1)}, u32[]{:S(2)}, u32[]{:S(2)}) collective-permute-start(bf16[256,256]{1,0:T(8,128)(2,1)S(1)} %get-tuple-element.35), channel_id=1, source_target_pairs={{1,0},{2,1},{3,2},{4,3},{5,4},{6,5},{7,6},{8,7},{9,8},{10,9},{11,1... | collective-permute-start | bytes 393224 | tf_op jit(solution)/shard_map/ppermute | solution.py:24
  37.2 11.0 %collective-permute-start.6 = (bf16[256,256]{1,0:T(8,128)(2,1)S(1)}, bf16[256,256]{1,0:T(8,128)(2,1)S(1)}, u32[]{:S(2)}, u32[]{:S(2)}) collective-permute-start(bf16[256,256]{1,0:T(8,128)(2,1)S(1)} %get-tuple-element.51), channel_id=1, source_target_pairs={{2,0},{3,1},{4,2},{5,3},{6,4},{7,5},{8,6},{9,7},{10,8},{11,9},{12,... | collective-permute-start | bytes 393224 | tf_op jit(solution)/shard_map/ppermute | solution.py:24
  41.6 10.1 %collective-permute-start.7 = (bf16[256,256]{1,0:T(8,128)(2,1)S(1)}, bf16[256,256]{1,0:T(8,128)(2,1)S(1)}, u32[]{:S(2)}, u32[]{:S(2)}) collective-permute-start(bf16[256,256]{1,0:T(8,128)(2,1)S(1)} %get-tuple-element.52), channel_id=1, source_target_pairs={{1,0},{2,1},{3,2},{4,3},{5,4},{6,5},{7,6},{8,7},{9,8},{10,9},{11,1... | collective-permute-start | bytes 393224 | tf_op jit(solution)/shard_map/ppermute | solution.py:24

commit v9 on v7

--- a/solution.py
+++ b/solution.py
@@ -95,7 +95,7 @@
         copy.wait()
 
 
-def score_kernel(group, tokens, scale, known, offset, q_ref, g_ref, qt_ref, gt_ref, own_ref, two_ref, one_ref, *refs):
+def score_kernel(group, tokens, scale, known, offset, q_ref, g_ref, qt_ref, gt_ref, own_ref, one_ref, two_ref, *refs):
     p_ref, ds_ref, far_ref, near_ref = refs[1:] if known else refs[:-1]
     bias_ref = refs[0] if known else refs[-1]
     tri = sees_own(tokens, 1)
@@ -164,24 +164,10 @@
             ref[tokens : 2 * tokens, cols] = sum_v[row : row + tokens].astype(ref.dtype)
 
 
-def leave(total, index, tokens, kv_ref, k_out, v_out, sems):
-    width = total.shape[1]
-    kv_ref[...] = total.astype(kv_ref.dtype)
-    copies = [
-        pltpu.make_async_copy(
-            kv_ref.at[pl.ds(half * tokens, tokens), :], out.at[:, pl.ds(index * width, width)], sems.at[half]
-        )
-        for half, out in enumerate((k_out, v_out))
-    ]
-    for copy in copies:
-        copy.start()
-    return copies
-
-
-def rest_kernel(group, tokens, scale, q_ref, g_ref, far_ref, near_ref, *refs):
+def rest_kernel(group, tokens, scale, q_ref, g_ref, *refs):
     per = 5
     chunk_refs = [refs[per * c : per * (c + 1)] for c in range(CHUNKS)]
-    dq_out, k_out, v_out, own_out, dq_ref, kv_ref, sems, kv_sems = refs[per * CHUNKS :]
+    dq_out, own_out, dq_ref, sems = refs[per * CHUNKS :]
     tri = sees_own(tokens, 2)
     own_mask = jnp.where(tri, 1.0, 0.0).astype(jnp.bfloat16)
     far_mask = jnp.where(tri, 0.0, 1.0).astype(jnp.bfloat16)
@@ -189,7 +175,6 @@
     count = HK // CHUNKS
     copies = []
     for chunk, (p_ref, ds_ref, own_ref, two_ref, one_ref) in enumerate(chunk_refs):
-        sums = []
         for part in range(count):
             block = slice(part * tokens, (part + 1) * tokens)
             keys_t = jnp.concatenate([jnp.transpose(ref[block, :]) for ref in (own_ref, one_ref, two_ref)], axis=1)
@@ -208,25 +193,28 @@
                     dq_ref[:, (first + h) * HD : (first + h + 1) * HD] = jnp.transpose(
                         dq_t[:, h * HD : (h + 1) * HD]
                     )
-            sums.append(jnp.concatenate([sum_k * scale, sum_v], axis=0))
+            total = jnp.concatenate([sum_k * scale, sum_v], axis=0)
             index = chunk * count + part
+            own_out[:, index * HD : (index + 1) * HD] = total
             span = pl.ds(index * wide, wide)
             copies.append(pltpu.make_async_copy(dq_ref.at[:, span], dq_out.at[:, span], sems.at[index]))
             copies[-1].start()
-        total = jnp.concatenate(sums, axis=1)
-        if chunk == 0:
-            total = total + near_ref[...].astype(jnp.float32) + far_ref[...].astype(jnp.float32)
-            copies += leave(total, 0, tokens, kv_ref, k_out, v_out, kv_sems)
-        else:
-            own_out[...] = total
     for copy in copies:
         copy.wait()
 
 
-def final_kernel(tokens, own_ref, far_ref, near_ref, k_before, v_before, k_out, v_out, kv_ref, sems):
-    total = own_ref[...] + near_ref[...].astype(jnp.float32) + far_ref[...].astype(jnp.float32)
-    for copy in leave(total, 1, tokens, kv_ref, k_out, v_out, sems):
-        copy.wait()
+def join_kernel(first_ref, handed_ref, second_ref, out_ref):
+    width = first_ref.shape[1]
+    out_ref[:, 0:width] = (first_ref[...] + handed_ref[...].astype(jnp.float32)).astype(out_ref.dtype)
+    out_ref[:, width:] = second_ref[...].astype(out_ref.dtype)
+
+
+def final_kernel(tokens, own_ref, far_ref, near_ref, k_out, v_out):
+    total = own_ref[...] + near_ref[...].astype(jnp.float32)
+    width = far_ref.shape[1]
+    total = jnp.concatenate([total[:, 0:width], total[:, width:] + far_ref[...].astype(jnp.float32)], axis=1)
+    k_out[...] = total[0:tokens].astype(k_out.dtype)
+    v_out[...] = total[tokens:].astype(v_out.dtype)
 
 
 def bf16(*shape):
@@ -279,7 +267,7 @@
     )(*in_hbm(q, g, key_states, value_states))
 
 
-def score_call(q, g, qt, gt, own, two, one, bias, offset, group, tokens, scale):
+def score_call(q, g, qt, gt, own, one, two, bias, offset, group, tokens, scale):
     count = HK // CHUNKS
     span = count * group * HD
     known = bias is not None
@@ -289,50 +277,47 @@
             bf16(tokens, span),
             bf16(2 * tokens, span),
             bf16(2 * tokens, count * HD),
-            bf16(2 * tokens, count * HD),
+            f32(2 * tokens, count * HD),
         ]
         + [f32(2 * tokens, tokens)] * (not known),
         cost_estimate=cost(2 * tokens * 3 * span * tokens * 4, 12 * tokens * span, 2 * tokens * span),
         compiler_params=PARAMS,
         name="scores",
-    )(q, g, qt, gt, own, two, one, *([bias] if known else []))
-
-
-ON_CHIP = pl.BlockSpec(memory_space=pltpu.VMEM)
-IN_HBM = pl.BlockSpec(memory_space=pltpu.HBM)
-
-
-def rest_call(q, g, far, near, parts, group, tokens, scale):
-    grads = bf16(tokens, HK * HD)
-    chunk = (2 * tokens, HK // CHUNKS * HD)
+    )(q, g, qt, gt, own, one, two, *([bias] if known else []))
+
+
+def rest_call(q, g, parts, group, tokens, scale):
     return pl.pallas_call(
         functools.partial(rest_kernel, group, tokens, scale),
-        out_specs=[IN_HBM] * 3 + [ON_CHIP],
-        out_shape=[bf16(*q.shape), grads, grads, f32(*chunk)],
-        scratch_shapes=[
-            pltpu.VMEM(q.shape, jnp.bfloat16),
-            pltpu.VMEM(chunk, jnp.bfloat16),
-            pltpu.SemaphoreType.DMA((HK,)),
-            pltpu.SemaphoreType.DMA((2,)),
-        ],
+        out_specs=[pl.BlockSpec(memory_space=pltpu.HBM), pl.BlockSpec(memory_space=pltpu.VMEM)],
+        out_shape=[bf16(*q.shape), f32(2 * tokens, HK * HD)],
+        scratch_shapes=[pltpu.VMEM(q.shape, jnp.bfloat16), pltpu.SemaphoreType.DMA((HK,))],
         cost_estimate=cost(2 * tokens * 3 * q.shape[1] * tokens * 2, 12 * tokens * q.shape[1]),
         compiler_params=PARAMS,
         name="rest",
-    )(q, g, far, near, *[x for part in parts for x in part])
-
-
-def final_call(own, far, near, key_grad, value_grad):
-    return pl.pallas_call(
-        functools.partial(final_kernel, key_grad.shape[0]),
-        in_specs=[ON_CHIP] * 3 + [IN_HBM] * 2,
-        out_specs=[IN_HBM] * 2,
-        out_shape=[bf16(*key_grad.shape)] * 2,
-        scratch_shapes=[pltpu.VMEM(own.shape, jnp.bfloat16), pltpu.SemaphoreType.DMA((2,))],
-        input_output_aliases={3: 0, 4: 1},
-        cost_estimate=cost(0, 16 * own.shape[0] * own.shape[1]),
+    )(q, g, *[x for part in parts for x in part])
+
+
+def join_call(first, handed, second):
+    rows, width = first.shape
+    return pl.pallas_call(
+        join_kernel,
+        out_shape=bf16(rows, 2 * width),
+        cost_estimate=cost(0, 12 * rows * width),
+        compiler_params=PARAMS,
+        name="join",
+    )(first, handed, second)
+
+
+def final_call(own, far, near):
+    tokens, width = own.shape[0] // 2, own.shape[1]
+    return pl.pallas_call(
+        functools.partial(final_kernel, tokens),
+        out_shape=[bf16(tokens, width)] * 2,
+        cost_estimate=cost(0, 16 * tokens * width),
         compiler_params=PARAMS,
         name="final",
-    )(own, far, near, key_grad, value_grad)
+    )(own, far, near)
 
 
 def shards(queries, key_states, value_states, out_grad, segment_ids):
@@ -346,18 +331,17 @@
     own.append(later)
     two = [shift(x, 2) for x in own]
     one = [shift(x, 1) for x in own]
-    first, near, far, bias = [], [], [], None
+    first, bias = [], None
     for c in chunks:
-        results = score_call(q, g, qt, gt, own[c], two[c], one[c], bias, c * step, group, tokens, scale)
-        bias = results[4] if bias is None else bias
-        first.append(results)
-        far.append(shift(results[2], -2))
-        near.append(shift(results[3], -1))
-    query_grad, key_grad, value_grad, own_terms = rest_call(
-        q, g, far[0], near[0], [(first[c][0], first[c][1], own[c], two[c], one[c]) for c in chunks],
-        group, tokens, scale,
+        first.append(score_call(q, g, qt, gt, own[c], one[c], two[c], bias, c * step, group, tokens, scale))
+        bias = first[0][4]
+    handed = shift(first[0][2], -1)
+    far = shift(first[1][2], -2)
+    near = shift(join_call(first[0][3], handed, first[1][3]), -1)
+    query_grad, own_terms = rest_call(
+        q, g, [(first[c][0], first[c][1], own[c], two[c], one[c]) for c in chunks], group, tokens, scale
     )
-    key_grad, value_grad = final_call(own_terms, far[1], near[1], key_grad, value_grad)
+    key_grad, value_grad = final_call(own_terms, far, near)
     return query_grad, key_grad, value_grad
 
 

time: 51.5 us -> 51.3 us (level)
  waiting for transfers between devices: 6.3 us -> 7.11 us
  starting transfers between devices: 33 us -> 32.4 us
    ppermute x8 -> x7, waiting for transfers between devices: 6.3 us -> 7.11 us  [shift(): lax.ppermute(value, AXES, [(i, i + steps) for i in range(first, last)])]
    ppermute x8 -> x7, starting transfers between devices: 33 us -> 32.4 us  [shift(): lax.ppermute(value, AXES, [(i, i + steps) for i in range(first, last)])]
  transfers between devices with their start and end apart: 8 -> 7, of which waited for: 3 -> 3; matrix products, arithmetic and copies ran while one was open for 0% -> 0% of each run, Pallas kernels for 18% -> 18%
where the time goes in v9:
time: 51.3 us; the launch traced here: 51 us
  starting transfers between devices  32.4 us (63%)
  Pallas kernels  10.8 us (21%)
  waiting for transfers between devices  7.11 us (14%)
  between operations  0.75 us (1%)
    ppermute x7, starting transfers between devices, shift(): lax.ppermute(value, AXES, [(i, i + steps) for i in range(first, last)])  32.4 us
    ppermute x7, waiting for transfers between devices, shift(): lax.ppermute(value, AXES, [(i, i + steps) for i in range(first, last)])  7.11 us
    pallas_call x2, Pallas kernels, score_call(): pl.pallas_call(functools.partial(score_kernel, group, tokens, scale, know...  4.83 us
    pallas_call x1, Pallas kernels, rest_call(): pl.pallas_call(functools.partial(rest_kernel, group, tokens, scale), out_...  2.22 us
    pallas_call x1, Pallas kernels, turn_call(): pl.pallas_call(functools.partial(turn_kernel, group), in_specs=[pl.BlockS...  2.07 us
  transfers between devices with their start and end apart: 7, of which 3 were waited for; matrix products, arithmetic and copies ran while one was open for 0% of the time, Pallas kernels for 18%

profile of v9, /device:TPU:4, one launch (start us, length us, event | category | flops | bytes accessed | tf_op | source)
XLA Modules:
  0.0 51.0 jit_solution(2231987485229665951)
XLA Ops:
  0.6 0.9 %pack.1.own_ref.refs_2_ = bf16[528,128]{1,0:T(8,128)(2,1)S(1)} custom-call(bf16[128,512]{1,0:T(8,128)(2,1)} %k_ref.3, bf16[128,512]{1,0:T(8,128)(2,1)} %v_ref.3, s32[128]{0:T(128)} %seg_ref.1), custom_call_target="tpu_custom_call" | custom-call | bytes 262144 | tf_op jit(solution)/shard_map/pack/pallas_call | solution.py:241
  1.5 5.2 %collective-permute-start.1 = (bf16[528,128]{1,0:T(8,128)(2,1)S(1)}, bf16[528,128]{1,0:T(8,128)(2,1)S(1)}, u32[]{:S(2)}, u32[]{:S(2)}) collective-permute-start(bf16[528,128]{1,0:T(8,128)(2,1)S(1)} %pack.1.own_ref.refs_2_), channel_id=1, source_target_pairs={{0,2},{1,3},{2,4},{3,5},{4,6},{5,7},{6,8},{7,9},{8,10},{9,11},{10,... | collective-permute-start | bytes 405512 | tf_op jit(solution)/shard_map/ppermute | solution.py:24
  6.7 3.8 %collective-permute-start = (bf16[528,128]{1,0:T(8,128)(2,1)S(1)}, bf16[528,128]{1,0:T(8,128)(2,1)S(1)}, u32[]{:S(2)}, u32[]{:S(2)}) collective-permute-start(bf16[528,128]{1,0:T(8,128)(2,1)S(1)} %pack.1.own_ref.refs_2_), channel_id=1, source_target_pairs={{0,1},{1,2},{2,3},{3,4},{4,5},{5,6},{6,7},{7,8},{8,9},{9,10},{10,1... | collective-permute-start | bytes 405512 | tf_op jit(solution)/shard_map/ppermute | solution.py:24
  10.5 2.1 %turn.1 = (bf16[128,4096]{1,0:T(8,128)(2,1)S(1)}, bf16[128,4096]{1,0:T(8,128)(2,1)S(1)}, bf16[128,4096]{1,0:T(8,128)(2,1)S(1)}, bf16[128,4096]{1,0:T(8,128)(2,1)S(1)}, bf16[512,128]{1,0:T(8,128)(2,1)S(1)}) custom-call(bf16[128,4096]{1,0:T(8,128)(2,1)} %q_ref.1, bf16[128,4096]{1,0:T(8,128)(2,1)} %g_ref.1, bf16[128,512]{1,0:T(8,128)(2,1)} %k_ref.3, ...), custom_call_target="tpu_custom_call" | custom-call | bytes 8388608 | tf_op jit(solution)/shard_map/turn/pallas_call | solution.py:259
  12.6 6.4 %collective-permute-start.3 = (bf16[512,128]{1,0:T(8,128)(2,1)S(1)}, bf16[512,128]{1,0:T(8,128)(2,1)S(1)}, u32[]{:S(2)}, u32[]{:S(2)}) collective-permute-start(bf16[512,128]{1,0:T(8,128)(2,1)S(1)} %get-tuple-element.27.own_ref.refs_7_), channel_id=1, source_target_pairs={{0,2},{1,3},{2,4},{3,5},{4,6},{5,7},{6,8},{7,9},{8,10},{9,11},{10,... | collective-permute-start | bytes 393224 | tf_op jit(solution)/shard_map/ppermute | solution.py:24
  19.0 3.8 %collective-permute-start.2 = (bf16[512,128]{1,0:T(8,128)(2,1)S(1)}, bf16[512,128]{1,0:T(8,128)(2,1)S(1)}, u32[]{:S(2)}, u32[]{:S(2)}) collective-permute-start(bf16[512,128]{1,0:T(8,128)(2,1)S(1)} %get-tuple-element.27.own_ref.refs_7_), channel_id=1, source_target_pairs={{0,1},{1,2},{2,3},{3,4},{4,5},{5,6},{6,7},{7,8},{8,9},{9,10},{10,1... | collective-permute-start | bytes 393224 | tf_op jit(solution)/shard_map/ppermute | solution.py:24
  22.8 0.0 collective-permute-done.1.two_ref.refs_3_
  22.8 1.3 %collective-permute-done.one_ref.refs_4_ = bf16[528,128]{1,0:T(8,128)(2,1)S(1)} collective-permute-done((bf16[528,128]{1,0:T(8,128)(2,1)S(1)}, bf16[528,128]{1,0:T(8,128)(2,1)S(1)}, u32[]{:S(2)}, u32[]{:S(2)}) %collective-permute-start) | collective-permute-done | bytes 135200 | tf_op jit(solution)/shard_map/ppermute | solution.py:24
  24.2 2.4 %scores.2 = (bf16[128,2048]{1,0:T(8,128)(2,1)S(1)}, bf16[256,2048]{1,0:T(8,128)(2,1)S(1)}, bf16[256,256]{1,0:T(8,128)(2,1)S(1)}, f32[256,256]{1,0:T(8,128)S(1)}, f32[256,128]{1,0:T(8,128)S(1)}) custom-call(bf16[128,4096]{1,0:T(8,128)(2,1)S(1)} %get-tuple-element.21.q_ref, bf16[128,4096]{1,0:T(8,128)(2,1)S(1)} %get-tuple-element.22.g_ref, ...), custom_call_target="tpu_custom_call" | custom-call | flops 805306368 | bytes 3145728 | tf_op jit(solution)/shard_map/scores/pallas_call | solution.py:274
  26.6 4.6 %collective-permute-start.5 = (bf16[256,256]{1,0:T(8,128)(2,1)S(1)}, bf16[256,256]{1,0:T(8,128)(2,1)S(1)}, u32[]{:S(2)}, u32[]{:S(2)}) collective-permute-start(bf16[256,256]{1,0:T(8,128)(2,1)S(1)} %get-tuple-element.35), channel_id=1, source_target_pairs={{1,0},{2,1},{3,2},{4,3},{5,4},{6,5},{7,6},{8,7},{9,8},{10,9},{11,1... | collective-permute-start | bytes 393224 | tf_op jit(solution)/shard_map/ppermute | solution.py:24
  31.3 0.0 collective-permute-done.3.two_ref.refs_8_
  31.3 1.5 %collective-permute-done.2.one_ref.refs_9_ = bf16[512,128]{1,0:T(8,128)(2,1)S(1)} collective-permute-done((bf16[512,128]{1,0:T(8,128)(2,1)S(1)}, bf16[512,128]{1,0:T(8,128)(2,1)S(1)}, u32[]{:S(2)}, u32[]{:S(2)}) %collective-permute-start.2) | collective-permute-done | bytes 131104 | tf_op jit(solution)/shard_map/ppermute | solution.py:24
  32.8 2.4 %scores.3 = (bf16[128,2048]{1,0:T(8,128)(2,1)S(1)}, bf16[256,2048]{1,0:T(8,128)(2,1)S(1)}, bf16[256,256]{1,0:T(8,128)(2,1)S(1)}, f32[256,256]{1,0:T(8,128)S(1)}) custom-call(bf16[128,4096]{1,0:T(8,128)(2,1)S(1)} %get-tuple-element.21.q_ref, bf16[128,4096]{1,0:T(8,128)(2,1)S(1)} %get-tuple-element.22.g_ref, bf16[128,4096]{1,0:T(8,128)(2,1)S(1)} %get-tuple-element.23.qt_ref, ...), custom_call_target="tpu_custom_call" | custom-call | flops 805306368 | bytes 3145728 | tf_op jit(solution)/shard_map/scores/pallas_call | solution.py:274
  35.2 0.0 collective-permute-done.5.handed_ref
  35.2 6.6 %collective-permute-start.6 = (bf16[256,512]{1,0:T(8,128)(2,1)S(1)}, bf16[256,512]{1,0:T(8,128)(2,1)S(1)}, u32[]{:S(2)}, u32[]{:S(2)}) collective-permute-start(bf16[256,512]{1,0:T(8,128)(2,1)S(1)} %join.1), channel_id=1, source_target_pairs={{1,0},{2,1},{3,2},{4,3},{5,4},{6,5},{7,6},{8,7},{9,8},{10,9},{11,1... | collective-permute-start | bytes 786440 | tf_op jit(solution)/shard_map/ppermute | solution.py:24
  41.8 1.9 %collective-permute-start.4 = (bf16[256,256]{1,0:T(8,128)(2,1)S(1)}, bf16[256,256]{1,0:T(8,128)(2,1)S(1)}, u32[]{:S(2)}, u32[]{:S(2)}) collective-permute-start(bf16[256,256]{1,0:T(8,128)(2,1)S(1)} %get-tuple-element.33), channel_id=1, source_target_pairs={{2,0},{3,1},{4,2},{5,3},{6,4},{7,5},{8,6},{9,7},{10,8},{11,9},{12,... | collective-permute-start | bytes 393224 | tf_op jit(solution)/shard_map/ppermute | solution.py:24
  43.7 2.2 %rest.1 = (bf16[128,4096]{1,0:T(8,128)(2,1)}, f32[256,512]{1,0:T(8,128)S(1)}) custom-call(bf16[128,4096]{1,0:T(8,128)(2,1)S(1)} %get-tuple-element.21.q_ref, bf16[128,4096]{1,0:T(8,128)(2,1)S(1)} %get-tuple-element.22.g_ref, bf16[128,2048]{1,0:T(8,128)(2,1)S(1)} %get-tuple-element.25.refs_0_, bf16[256,2048]{1,0:T(8,128)(2,1)S(1)} %get-tuple-element.26.refs_1_, ...), custom_call_target="tpu_custom_call" | custom-call | flops 805306368 | bytes 6291456 | tf_op jit(solution)/shard_map/rest/pallas_call | solution.py:290
  46.0 4.3 %collective-permute-done.4.far_ref = bf16[256,256]{1,0:T(8,128)(2,1)S(1)} collective-permute-done((bf16[256,256]{1,0:T(8,128)(2,1)S(1)}, bf16[256,256]{1,0:T(8,128)(2,1)S(1)}, u32[]{:S(2)}, u32[]{:S(2)}) %collective-permute-start.4) | collective-permute-done | bytes 131104 | tf_op jit(solution)/shard_map/ppermute | solution.py:24
  50.2 0.0 collective-permute-done.6.near_ref
  50.2 0.7 %final.1 = (bf16[128,512]{1,0:T(8,128)(2,1)}, bf16[128,512]{1,0:T(8,128)(2,1)}) custom-call(f32[256,512]{1,0:T(8,128)S(1)} %get-tuple-element.32.own_ref, bf16[256,256]{1,0:T(8,128)(2,1)S(1)} %collective-permute-done.4.far_ref, bf16[256,512]{1,0:T(8,128)(2,1)S(1)} %collective-permute-done.6.near_ref), custom_call_target="tpu_custom_call" | custom-call | bytes 1048576 | tf_op jit(solution)/shard_map/final/pallas_call | solution.py:314
  (1 shorter events, 0.0 us)
Async XLA Ops:
  1.5 21.3 %collective-permute-start.1 = (bf16[528,128]{1,0:T(8,128)(2,1)S(1)}, bf16[528,128]{1,0:T(8,128)(2,1)S(1)}, u32[]{:S(2)}, u32[]{:S(2)}) collective-permute-start(bf16[528,128]{1,0:T(8,128)(2,1)S(1)} %pack.1.own_ref.refs_2_), channel_id=1, source_target_pairs={{0,2},{1,3},{2,4},{3,5},{4,6},{5,7},{6,8},{7,9},{8,10},{9,11},{10,... | collective-permute-start | bytes 405512 | tf_op jit(solution)/shard_map/ppermute | solution.py:24
  6.7 17.5 %collective-permute-start = (bf16[528,128]{1,0:T(8,128)(2,1)S(1)}, bf16[528,128]{1,0:T(8,128)(2,1)S(1)}, u32[]{:S(2)}, u32[]{:S(2)}) collective-permute-start(bf16[528,128]{1,0:T(8,128)(2,1)S(1)} %pack.1.own_ref.refs_2_), channel_id=1, source_target_pairs={{0,1},{1,2},{2,3},{3,4},{4,5},{5,6},{6,7},{7,8},{8,9},{9,10},{10,1... | collective-permute-start | bytes 405512 | tf_op jit(solution)/shard_map/ppermute | solution.py:24
  12.6 18.7 %collective-permute-start.3 = (bf16[512,128]{1,0:T(8,128)(2,1)S(1)}, bf16[512,128]{1,0:T(8,128)(2,1)S(1)}, u32[]{:S(2)}, u32[]{:S(2)}) collective-permute-start(bf16[512,128]{1,0:T(8,128)(2,1)S(1)} %get-tuple-element.27.own_ref.refs_7_), channel_id=1, source_target_pairs={{0,2},{1,3},{2,4},{3,5},{4,6},{5,7},{6,8},{7,9},{8,10},{9,11},{10,... | collective-permute-start | bytes 393224 | tf_op jit(solution)/shard_map/ppermute | solution.py:24
  19.0 13.8 %collective-permute-start.2 = (bf16[512,128]{1,0:T(8,128)(2,1)S(1)}, bf16[512,128]{1,0:T(8,128)(2,1)S(1)}, u32[]{:S(2)}, u32[]{:S(2)}) collective-permute-start(bf16[512,128]{1,0:T(8,128)(2,1)S(1)} %get-tuple-element.27.own_ref.refs_7_), channel_id=1, source_target_pairs={{0,1},{1,2},{2,3},{3,4},{4,5},{5,6},{6,7},{7,8},{8,9},{9,10},{10,1... | collective-permute-start | bytes 393224 | tf_op jit(solution)/shard_map/ppermute | solution.py:24
  26.6 8.6 %collective-permute-start.5 = (bf16[256,256]{1,0:T(8,128)(2,1)S(1)}, bf16[256,256]{1,0:T(8,128)(2,1)S(1)}, u32[]{:S(2)}, u32[]{:S(2)}) collective-permute-start(bf16[256,256]{1,0:T(8,128)(2,1)S(1)} %get-tuple-element.35), channel_id=1, source_target_pairs={{1,0},{2,1},{3,2},{4,3},{5,4},{6,5},{7,6},{8,7},{9,8},{10,9},{11,1... | collective-permute-start | bytes 393224 | tf_op jit(solution)/shard_map/ppermute | solution.py:24
  35.2 15.0 %collective-permute-start.6 = (bf16[256,512]{1,0:T(8,128)(2,1)S(1)}, bf16[256,512]{1,0:T(8,128)(2,1)S(1)}, u32[]{:S(2)}, u32[]{:S(2)}) collective-permute-start(bf16[256,512]{1,0:T(8,128)(2,1)S(1)} %join.1), channel_id=1, source_target_pairs={{1,0},{2,1},{3,2},{4,3},{5,4},{6,5},{7,6},{8,7},{9,8},{10,9},{11,1... | collective-permute-start | bytes 786440 | tf_op jit(solution)/shard_map/ppermute | solution.py:24
  41.8 8.4 %collective-permute-start.4 = (bf16[256,256]{1,0:T(8,128)(2,1)S(1)}, bf16[256,256]{1,0:T(8,128)(2,1)S(1)}, u32[]{:S(2)}, u32[]{:S(2)}) collective-permute-start(bf16[256,256]{1,0:T(8,128)(2,1)S(1)} %get-tuple-element.33), channel_id=1, source_target_pairs={{2,0},{3,1},{4,2},{5,3},{6,4},{7,5},{8,6},{9,7},{10,8},{11,9},{12,... | collective-permute-start | bytes 393224 | tf_op jit(solution)/shard_map/ppermute | solution.py:24

commit v10 on v6

--- a/solution.py
+++ b/solution.py
@@ -14,7 +14,7 @@
 LOG2E = 1.4426950408889634
 AXES = ("inner", "outer")
 CHUNKS = 2
-UNIT = 4
+UNIT = 8
 VMEM_LIMIT = 24 * 1024 * 1024
 
 

time: 51.5 us -> 51.4 us (level)
  no operation moved by 1% of the time
where the time goes in v10:
time: 51.4 us; the launch traced here: 50.7 us
  starting transfers between devices  33 us (64%)
  Pallas kernels  10.5 us (20%)
  waiting for transfers between devices  6.35 us (12%)
  between operations  0.77 us (1%)
    ppermute x8, starting transfers between devices, shift(): lax.ppermute(value, AXES, [(i, i + steps) for i in range(first, last)])  33 us
    ppermute x8, waiting for transfers between devices, shift(): lax.ppermute(value, AXES, [(i, i + steps) for i in range(first, last)])  6.35 us
    pallas_call x2, Pallas kernels, score_call(): pl.pallas_call(functools.partial(score_kernel, group, tokens, scale, know...  4.62 us
    pallas_call x1, Pallas kernels, rest_call(): pl.pallas_call(functools.partial(rest_kernel, group, tokens, scale), out_...  2.25 us
    pallas_call x1, Pallas kernels, turn_call(): pl.pallas_call(functools.partial(turn_kernel, group), in_specs=[pl.BlockS...  2.07 us
  transfers between devices with their start and end apart: 8, of which 3 were waited for; matrix products, arithmetic and copies ran while one was open for 0% of the time, Pallas kernels for 18%

profile of v10, /device:TPU:4, one launch (start us, length us, event | category | flops | bytes accessed | tf_op | source)
XLA Modules:
  0.0 50.7 jit_solution(10896377582999434354)
XLA Ops:
  0.6 0.9 %pack.1.own_ref.refs_2_ = bf16[528,128]{1,0:T(8,128)(2,1)S(1)} custom-call(bf16[128,512]{1,0:T(8,128)(2,1)} %k_ref.3, bf16[128,512]{1,0:T(8,128)(2,1)} %v_ref.3, s32[128]{0:T(128)} %seg_ref.1), custom_call_target="tpu_custom_call" | custom-call | bytes 262144 | tf_op jit(solution)/shard_map/pack/pallas_call | solution.py:253
  1.5 5.2 %collective-permute-start = (bf16[528,128]{1,0:T(8,128)(2,1)S(1)}, bf16[528,128]{1,0:T(8,128)(2,1)S(1)}, u32[]{:S(2)}, u32[]{:S(2)}) collective-permute-start(bf16[528,128]{1,0:T(8,128)(2,1)S(1)} %pack.1.own_ref.refs_2_), channel_id=1, source_target_pairs={{0,2},{1,3},{2,4},{3,5},{4,6},{5,7},{6,8},{7,9},{8,10},{9,11},{10,... | collective-permute-start | bytes 405512 | tf_op jit(solution)/shard_map/ppermute | solution.py:24
  6.7 3.8 %collective-permute-start.1 = (bf16[528,128]{1,0:T(8,128)(2,1)S(1)}, bf16[528,128]{1,0:T(8,128)(2,1)S(1)}, u32[]{:S(2)}, u32[]{:S(2)}) collective-permute-start(bf16[528,128]{1,0:T(8,128)(2,1)S(1)} %pack.1.own_ref.refs_2_), channel_id=1, source_target_pairs={{0,1},{1,2},{2,3},{3,4},{4,5},{5,6},{6,7},{7,8},{8,9},{9,10},{10,1... | collective-permute-start | bytes 405512 | tf_op jit(solution)/shard_map/ppermute | solution.py:24
  10.5 2.1 %turn.1 = (bf16[128,4096]{1,0:T(8,128)(2,1)S(1)}, bf16[128,4096]{1,0:T(8,128)(2,1)S(1)}, bf16[128,4096]{1,0:T(8,128)(2,1)S(1)}, bf16[128,4096]{1,0:T(8,128)(2,1)S(1)}, bf16[512,128]{1,0:T(8,128)(2,1)S(1)}) custom-call(bf16[128,4096]{1,0:T(8,128)(2,1)} %q_ref.1, bf16[128,4096]{1,0:T(8,128)(2,1)} %g_ref.1, bf16[128,512]{1,0:T(8,128)(2,1)} %k_ref.3, ...), custom_call_target="tpu_custom_call" | custom-call | bytes 8388608 | tf_op jit(solution)/shard_map/turn/pallas_call | solution.py:271
  12.6 6.4 %collective-permute-start.4 = (bf16[512,128]{1,0:T(8,128)(2,1)S(1)}, bf16[512,128]{1,0:T(8,128)(2,1)S(1)}, u32[]{:S(2)}, u32[]{:S(2)}) collective-permute-start(bf16[512,128]{1,0:T(8,128)(2,1)S(1)} %get-tuple-element.31.own_ref.refs_7_), channel_id=1, source_target_pairs={{0,2},{1,3},{2,4},{3,5},{4,6},{5,7},{6,8},{7,9},{8,10},{9,11},{10,... | collective-permute-start | bytes 393224 | tf_op jit(solution)/shard_map/ppermute | solution.py:24
  19.0 3.8 %collective-permute-start.5 = (bf16[512,128]{1,0:T(8,128)(2,1)S(1)}, bf16[512,128]{1,0:T(8,128)(2,1)S(1)}, u32[]{:S(2)}, u32[]{:S(2)}) collective-permute-start(bf16[512,128]{1,0:T(8,128)(2,1)S(1)} %get-tuple-element.31.own_ref.refs_7_), channel_id=1, source_target_pairs={{0,1},{1,2},{2,3},{3,4},{4,5},{5,6},{6,7},{7,8},{8,9},{9,10},{10,1... | collective-permute-start | bytes 393224 | tf_op jit(solution)/shard_map/ppermute | solution.py:24
  22.8 0.0 collective-permute-done.two_ref.refs_3_
  22.8 1.3 %collective-permute-done.1.one_ref.refs_4_ = bf16[528,128]{1,0:T(8,128)(2,1)S(1)} collective-permute-done((bf16[528,128]{1,0:T(8,128)(2,1)S(1)}, bf16[528,128]{1,0:T(8,128)(2,1)S(1)}, u32[]{:S(2)}, u32[]{:S(2)}) %collective-permute-start.1) | collective-permute-done | bytes 135200 | tf_op jit(solution)/shard_map/ppermute | solution.py:24
  24.2 2.3 %scores.2 = (bf16[128,2048]{1,0:T(8,128)(2,1)S(1)}, bf16[256,2048]{1,0:T(8,128)(2,1)S(1)}, bf16[256,256]{1,0:T(8,128)(2,1)S(1)}, bf16[256,256]{1,0:T(8,128)(2,1)S(1)}, f32[256,128]{1,0:T(8,128)S(1)}) custom-call(bf16[128,4096]{1,0:T(8,128)(2,1)S(1)} %get-tuple-element.23.q_ref, bf16[128,4096]{1,0:T(8,128)(2,1)S(1)} %get-tuple-element.24.g_ref, ...), custom_call_target="tpu_custom_call" | custom-call | flops 805306368 | bytes 3145728 | tf_op jit(solution)/shard_map/scores/pallas_call | solution.py:286
  26.5 4.2 %collective-permute-start.2 = (bf16[256,256]{1,0:T(8,128)(2,1)S(1)}, bf16[256,256]{1,0:T(8,128)(2,1)S(1)}, u32[]{:S(2)}, u32[]{:S(2)}) collective-permute-start(bf16[256,256]{1,0:T(8,128)(2,1)S(1)} %get-tuple-element.27), channel_id=1, source_target_pairs={{2,0},{3,1},{4,2},{5,3},{6,4},{7,5},{8,6},{9,7},{10,8},{11,9},{12,... | collective-permute-start | bytes 393224 | tf_op jit(solution)/shard_map/ppermute | solution.py:24
  30.7 2.5 %collective-permute-start.3 = (bf16[256,256]{1,0:T(8,128)(2,1)S(1)}, bf16[256,256]{1,0:T(8,128)(2,1)S(1)}, u32[]{:S(2)}, u32[]{:S(2)}) collective-permute-start(bf16[256,256]{1,0:T(8,128)(2,1)S(1)} %get-tuple-element.28), channel_id=1, source_target_pairs={{1,0},{2,1},{3,2},{4,3},{5,4},{6,5},{7,6},{8,7},{9,8},{10,9},{11,1... | collective-permute-start | bytes 393224 | tf_op jit(solution)/shard_map/ppermute | solution.py:24
  33.2 0.0 collective-permute-done.4.two_ref.refs_8_
  33.2 0.0 collective-permute-done.5.one_ref.refs_9_
  33.2 2.3 %scores.3 = (bf16[128,2048]{1,0:T(8,128)(2,1)S(1)}, bf16[256,2048]{1,0:T(8,128)(2,1)S(1)}, bf16[256,256]{1,0:T(8,128)(2,1)S(1)}, bf16[256,256]{1,0:T(8,128)(2,1)S(1)}) custom-call(bf16[128,4096]{1,0:T(8,128)(2,1)S(1)} %get-tuple-element.23.q_ref, bf16[128,4096]{1,0:T(8,128)(2,1)S(1)} %get-tuple-element.24.g_ref, ...), custom_call_target="tpu_custom_call" | custom-call | flops 805306368 | bytes 3145728 | tf_op jit(solution)/shard_map/scores/pallas_call | solution.py:286
  35.5 4.4 %collective-permute-start.6 = (bf16[256,256]{1,0:T(8,128)(2,1)S(1)}, bf16[256,256]{1,0:T(8,128)(2,1)S(1)}, u32[]{:S(2)}, u32[]{:S(2)}) collective-permute-start(bf16[256,256]{1,0:T(8,128)(2,1)S(1)} %get-tuple-element.37), channel_id=1, source_target_pairs={{2,0},{3,1},{4,2},{5,3},{6,4},{7,5},{8,6},{9,7},{10,8},{11,9},{12,... | collective-permute-start | bytes 393224 | tf_op jit(solution)/shard_map/ppermute | solution.py:24
  40.0 2.7 %collective-permute-start.7 = (bf16[256,256]{1,0:T(8,128)(2,1)S(1)}, bf16[256,256]{1,0:T(8,128)(2,1)S(1)}, u32[]{:S(2)}, u32[]{:S(2)}) collective-permute-start(bf16[256,256]{1,0:T(8,128)(2,1)S(1)} %get-tuple-element.38), channel_id=1, source_target_pairs={{1,0},{2,1},{3,2},{4,3},{5,4},{6,5},{7,6},{8,7},{9,8},{10,9},{11,1... | collective-permute-start | bytes 393224 | tf_op jit(solution)/shard_map/ppermute | solution.py:24
  42.7 0.0 collective-permute-done.2.far_ref
  42.7 0.0 collective-permute-done.3.near_ref
  42.7 2.3 %rest.1 = (bf16[128,4096]{1,0:T(8,128)(2,1)}, bf16[128,512]{1,0:T(8,128)(2,1)}, bf16[128,512]{1,0:T(8,128)(2,1)}, f32[256,256]{1,0:T(8,128)S(1)}) custom-call(bf16[128,4096]{1,0:T(8,128)(2,1)S(1)} %get-tuple-element.23.q_ref, bf16[128,4096]{1,0:T(8,128)(2,1)S(1)} %get-tuple-element.24.g_ref, bf16[256,256]{1,0:T(8,128)(2,1)S(1)} %collective-permute-done.2.far_ref, ...), custom_call_target="tpu_custom_call" | custom-call | flops 805306368 | bytes 6291456 | tf_op jit(solution)/shard_map/rest/pallas_call | solution.py:308
  45.0 2.4 %collective-permute-done.6.far_ref = bf16[256,256]{1,0:T(8,128)(2,1)S(1)} collective-permute-done((bf16[256,256]{1,0:T(8,128)(2,1)S(1)}, bf16[256,256]{1,0:T(8,128)(2,1)S(1)}, u32[]{:S(2)}, u32[]{:S(2)}) %collective-permute-start.6) | collective-permute-done | bytes 131104 | tf_op jit(solution)/shard_map/ppermute | solution.py:24
  47.4 2.6 %collective-permute-done.7.near_ref = bf16[256,256]{1,0:T(8,128)(2,1)S(1)} collective-permute-done((bf16[256,256]{1,0:T(8,128)(2,1)S(1)}, bf16[256,256]{1,0:T(8,128)(2,1)S(1)}, u32[]{:S(2)}, u32[]{:S(2)}) %collective-permute-start.7) | collective-permute-done | bytes 131104 | tf_op jit(solution)/shard_map/ppermute | solution.py:24
  50.0 0.7 %final.1 = (bf16[128,512]{1,0:T(8,128)(2,1)}, bf16[128,512]{1,0:T(8,128)(2,1)}) custom-call(f32[256,256]{1,0:T(8,128)S(1)} %get-tuple-element.36.own_ref, bf16[256,256]{1,0:T(8,128)(2,1)S(1)} %collective-permute-done.6.far_ref, bf16[256,256]{1,0:T(8,128)(2,1)S(1)} %collective-permute-done.7.near_ref, ...), custom_call_target="tpu_custom_call", output_to_operand_aliasing={{0}: (3, {}), {1}: (4, {})} | custom-call | bytes 1048576 | tf_op jit(solution)/shard_map/final/pallas_call | solution.py:325
Async XLA Ops:
  1.5 21.3 %collective-permute-start = (bf16[528,128]{1,0:T(8,128)(2,1)S(1)}, bf16[528,128]{1,0:T(8,128)(2,1)S(1)}, u32[]{:S(2)}, u32[]{:S(2)}) collective-permute-start(bf16[528,128]{1,0:T(8,128)(2,1)S(1)} %pack.1.own_ref.refs_2_), channel_id=1, source_target_pairs={{0,2},{1,3},{2,4},{3,5},{4,6},{5,7},{6,8},{7,9},{8,10},{9,11},{10,... | collective-permute-start | bytes 405512 | tf_op jit(solution)/shard_map/ppermute | solution.py:24
  6.7 17.5 %collective-permute-start.1 = (bf16[528,128]{1,0:T(8,128)(2,1)S(1)}, bf16[528,128]{1,0:T(8,128)(2,1)S(1)}, u32[]{:S(2)}, u32[]{:S(2)}) collective-permute-start(bf16[528,128]{1,0:T(8,128)(2,1)S(1)} %pack.1.own_ref.refs_2_), channel_id=1, source_target_pairs={{0,1},{1,2},{2,3},{3,4},{4,5},{5,6},{6,7},{7,8},{8,9},{9,10},{10,1... | collective-permute-start | bytes 405512 | tf_op jit(solution)/shard_map/ppermute | solution.py:24
  12.6 20.6 %collective-permute-start.4 = (bf16[512,128]{1,0:T(8,128)(2,1)S(1)}, bf16[512,128]{1,0:T(8,128)(2,1)S(1)}, u32[]{:S(2)}, u32[]{:S(2)}) collective-permute-start(bf16[512,128]{1,0:T(8,128)(2,1)S(1)} %get-tuple-element.31.own_ref.refs_7_), channel_id=1, source_target_pairs={{0,2},{1,3},{2,4},{3,5},{4,6},{5,7},{6,8},{7,9},{8,10},{9,11},{10,... | collective-permute-start | bytes 393224 | tf_op jit(solution)/shard_map/ppermute | solution.py:24
  19.0 14.2 %collective-permute-start.5 = (bf16[512,128]{1,0:T(8,128)(2,1)S(1)}, bf16[512,128]{1,0:T(8,128)(2,1)S(1)}, u32[]{:S(2)}, u32[]{:S(2)}) collective-permute-start(bf16[512,128]{1,0:T(8,128)(2,1)S(1)} %get-tuple-element.31.own_ref.refs_7_), channel_id=1, source_target_pairs={{0,1},{1,2},{2,3},{3,4},{4,5},{5,6},{6,7},{7,8},{8,9},{9,10},{10,1... | collective-permute-start | bytes 393224 | tf_op jit(solution)/shard_map/ppermute | solution.py:24
  26.5 16.2 %collective-permute-start.2 = (bf16[256,256]{1,0:T(8,128)(2,1)S(1)}, bf16[256,256]{1,0:T(8,128)(2,1)S(1)}, u32[]{:S(2)}, u32[]{:S(2)}) collective-permute-start(bf16[256,256]{1,0:T(8,128)(2,1)S(1)} %get-tuple-element.27), channel_id=1, source_target_pairs={{2,0},{3,1},{4,2},{5,3},{6,4},{7,5},{8,6},{9,7},{10,8},{11,9},{12,... | collective-permute-start | bytes 393224 | tf_op jit(solution)/shard_map/ppermute | solution.py:24
  30.7 12.0 %collective-permute-start.3 = (bf16[256,256]{1,0:T(8,128)(2,1)S(1)}, bf16[256,256]{1,0:T(8,128)(2,1)S(1)}, u32[]{:S(2)}, u32[]{:S(2)}) collective-permute-start(bf16[256,256]{1,0:T(8,128)(2,1)S(1)} %get-tuple-element.28), channel_id=1, source_target_pairs={{1,0},{2,1},{3,2},{4,3},{5,4},{6,5},{7,6},{8,7},{9,8},{10,9},{11,1... | collective-permute-start | bytes 393224 | tf_op jit(solution)/shard_map/ppermute | solution.py:24
  35.5 11.8 %collective-permute-start.6 = (bf16[256,256]{1,0:T(8,128)(2,1)S(1)}, bf16[256,256]{1,0:T(8,128)(2,1)S(1)}, u32[]{:S(2)}, u32[]{:S(2)}) collective-permute-start(bf16[256,256]{1,0:T(8,128)(2,1)S(1)} %get-tuple-element.37), channel_id=1, source_target_pairs={{2,0},{3,1},{4,2},{5,3},{6,4},{7,5},{8,6},{9,7},{10,8},{11,9},{12,... | collective-permute-start | bytes 393224 | tf_op jit(solution)/shard_map/ppermute | solution.py:24
  40.0 10.0 %collective-permute-start.7 = (bf16[256,256]{1,0:T(8,128)(2,1)S(1)}, bf16[256,256]{1,0:T(8,128)(2,1)S(1)}, u32[]{:S(2)}, u32[]{:S(2)}) collective-permute-start(bf16[256,256]{1,0:T(8,128)(2,1)S(1)} %get-tuple-element.38), channel_id=1, source_target_pairs={{1,0},{2,1},{3,2},{4,3},{5,4},{6,5},{7,6},{8,7},{9,8},{10,9},{11,1... | collective-permute-start | bytes 393224 | tf_op jit(solution)/shard_map/ppermute | solution.py:24
